TPU v7x, 128 devices: a whole 4x4x4 slice. The times are simulated.
128 devices in a mesh: section: 8 (over z, core), expert: 16 (over y, x).
Axes of the slice: x: 4, y: 4, z: 4, core: 2. Of those that a mesh axis runs over, the one named last changes fastest.
Arguments:
- d_output: bfloat16 [16384, 4096], P(('section', 'expert')), may hold values from -3 to 3
- gate_values: bfloat16 [16384, 8], P(('section', 'expert')), may hold values from 0.049804688 to 0.5
- routes: int32 [16384, 8], P(('section', 'expert')), may hold values from 0 to 31, all different within a row; in each aligned block of 128 rows (0 to 127, 128 to 255, ...) at most 40 rows name the same one
- hidden_saved: bfloat16 [8, 32, 16, 40, 768], P('section', 'expert'), may hold values from -3 to 3
- w_down: bfloat16 [32, 768, 4096], P('expert'), may hold values from -0.21875 to 0.21875
Outputs:
- d_hidden: bfloat16 [8, 32, 16, 40, 768], P('section', 'expert')
- d_weight: bfloat16 [32, 768, 4096], P('expert', 'section')
- d_gate: float32 [16384, 8], P(('section', 'expert'))
Inputs may be any that keep to these rules, and one draw needn't show every extreme that they name: `routes`: each row names 8 different experts. Within the rows of one device (128 tokens) no expert is named by more than 40 rows, a bound that some block reaches.
All inputs are finite; a program needn't handle non-finite values.
Results may differ from a plain program's by a relative error of at most 0.017.
Values may be sent and summed in bfloat16 or wider, within the bound.
No kernel may reach another device: no remote copies, remote signals or barrier semaphores. Data moves between devices by JAX's collectives and lax.ppermute only.
A program may use at most 192 MiB of HBM per device.

v0:
```python
import jax
import jax.numpy as jnp
from jax import lax
from jax.sharding import PartitionSpec as P


def slot_ranks(route_block, expert_count):
    one_hot = (route_block[..., None] == jnp.arange(expert_count, dtype=jnp.int32)).astype(
        jnp.int32
    )
    earlier = jnp.cumsum(one_hot, axis=1) - one_hot
    return jnp.sum(earlier * one_hot, axis=2)


def shards(d_output, gate_values, routes, hidden_saved, w_down):
    experts_held = w_down.shape[0]
    hidden_width = w_down.shape[1]
    model_width = d_output.shape[1]
    tok_rows = d_output.shape[0]
    top_count = gate_values.shape[1]
    capacity = hidden_saved.shape[3]
    expert_groups = lax.axis_size("expert")
    expert_count = experts_held * expert_groups
    slot_total = expert_count * capacity
    route_list = routes.reshape(-1)
    slot_rank = slot_ranks(route_list[None, :], expert_count)[0]
    slot_index = (
        route_list % experts_held * (expert_groups * capacity)
        + route_list // experts_held * capacity
        + slot_rank
    )
    pair_total = tok_rows * top_count
    source_pair = (
        jnp.full((slot_total + 1,), pair_total, jnp.int32)
        .at[slot_index]
        .set(jnp.arange(pair_total, dtype=jnp.int32))[:slot_total]
    )
    dy_padded = jnp.concatenate([d_output, jnp.zeros((1, model_width), jnp.bfloat16)], axis=0)
    gate_padded = jnp.concatenate([gate_values.reshape(-1), jnp.zeros((1,), jnp.bfloat16)], axis=0)
    dy_slots = dy_padded[source_pair // top_count].reshape(
        experts_held, expert_groups, capacity, model_width
    )
    gate_slots = gate_padded[source_pair].reshape(experts_held, expert_groups, capacity)
    got_dy, got_gate = (
        lax.all_to_all(dy_slots, "expert", split_axis=1, concat_axis=1, tiled=True),
        lax.all_to_all(gate_slots, "expert", split_axis=1, concat_axis=1, tiled=True),
    )
    gated_rows = (got_gate.astype(jnp.float32)[..., None] * got_dy.astype(jnp.float32)).astype(
        jnp.bfloat16
    )
    gated_rows = gated_rows.reshape(experts_held, expert_groups * capacity, model_width)
    hidden = hidden_saved.reshape(experts_held, expert_groups * capacity, hidden_width)
    d_hidden = jnp.einsum(
        "lrd,lfd->lrf", gated_rows, w_down, preferred_element_type=jnp.float32
    ).astype(jnp.bfloat16)
    partial_value = jnp.einsum(
        "lrf,lrd->lfd", hidden, gated_rows, preferred_element_type=jnp.float32
    )
    d_weight = lax.psum_scatter(
        partial_value.astype(jnp.bfloat16), "section", scatter_dimension=1, tiled=True
    )
    expert_rows = jnp.einsum(
        "lrf,lfd->lrd", hidden, w_down, preferred_element_type=jnp.float32
    ).astype(jnp.bfloat16)
    returned = lax.all_to_all(
        expert_rows.reshape(experts_held, expert_groups, capacity, model_width),
        "expert",
        split_axis=1,
        concat_axis=1,
        tiled=True,
    )
    picked = returned.reshape(-1, model_width)[slot_index].reshape(tok_rows, top_count, model_width)
    d_gate = jnp.sum(d_output.astype(jnp.float32)[:, None, :] * picked.astype(jnp.float32), axis=2)
    return (d_hidden.reshape(hidden_saved.shape), d_weight, d_gate)


def solution(mesh):
    placed = (
        P(("section", "expert"), None),
        P(("section", "expert"), None),
        P(("section", "expert"), None),
        P("section", "expert", None, None, None),
        P("expert", None, None),
    )
    return jax.shard_map(
        shards,
        mesh=mesh,
        in_specs=placed,
        out_specs=(
            P("section", "expert", None, None, None),
            P("expert", "section", None),
            P(("section", "expert"), None),
        ),
        check_vma=False,
    )
```

profile of v0, /device:TPU:0, one launch (start us, length us, event | category | flops | bytes accessed | tf_op | source)
XLA Modules:
  0.0 441.8 jit_solution(14113252587065343236)
XLA Ops:
  7.2 0.0 copy-start
  7.2 0.9 copy.48
  8.1 0.1 eq.29
  8.3 9.0 %reduce-window.6 = s32[1,32,8,128]{3,2,1,0:T(8,128)S(1)} reduce-window(s32[1,32,8,128]{3,2,1,0:T(8,128)S(1)} %bitcast.41, s32[]{:T(128)} %constant.52.clone.1), window={size=1x1x1x128 pad=0_0x0_0x0_0x127_0}, to_apply=%region_0.0 | reduce-window | flops 4161536 | bytes 262148 | tf_op jit(solution)/shard_map/reduce-window
  17.3 0.1 slice.18
  17.4 0.1 reshape.312
  17.5 0.1 copy.50
  17.7 0.1 copy.51
  17.7 0.1 broadcast.225
  18.0 4.3 scatter_custom_fusion
  22.4 0.8 copy.47
  23.2 0.1 reshape.311
  23.3 8.0 %gather_fusion = bf16[1280]{0:T(1024)(128)(2,1)S(1)} fusion(bf16[1025]{0:T(1024)(128)(2,1)S(1)} %pad_maximum_fusion, s32[2048]{0:T(1024)S(1)} %get-tuple-element.23), kind=kCustom, calls=%fused_computation | custom fusion | bytes 10240 | tf_op jit(solution)/shard_map/gather | solution.py:43
  31.3 0.1 reshape.318
  31.4 0.6 copy.52
  32.0 7.1 %all-to-all-start = ((bf16[2,16,40]{2,0,1:T(2,128)(2,1)}), bf16[2,16,40]{2,0,1:T(2,128)(2,1)S(1)}, u32[]{:S(2)}, u32[]{:S(2)}) async-start(bf16[2,16,40]{2,0,1:T(2,128)(2,1)} %copy.52), calls=%async_computation | async-start | bytes 16384 | tf_op jit(solution)/shard_map/all_to_all | solution.py:46
  39.1 1.3 concatenate.7
  40.4 8.4 %gather_fusion.1 = bf16[1280,4096]{1,0:T(8,128)(2,1)} fusion(bf16[129,4096]{1,0:T(8,128)(2,1)S(1)} %concatenate.7, s32[2048]{0:T(1024)S(1)} %get-tuple-element.22), kind=kCustom, calls=%fused_computation.1 | custom fusion | bytes 20976640 | tf_op jit(solution)/shard_map/gather | solution.py:40
  48.8 9.5 %copy.54 = bf16[2,16,40,4096]{3,2,0,1:T(8,128)(2,1)} copy(bf16[2,16,40,4096]{3,2,1,0:T(8,128)(2,1)} %bitcast.37) | data formatting | bytes 20971520 | tf_op jit(solution)/shard_map/reshape | solution.py:40
  58.3 0.0 all-to-all-done
  58.3 7.3 %all-to-all-start.1 = ((bf16[2,16,40,4096]{3,2,0,1:T(8,128)(2,1)}), bf16[2,16,40,4096]{3,2,0,1:T(8,128)(2,1)}, u32[]{:S(2)}, u32[]{:S(2)}) async-start(bf16[2,16,40,4096]{3,2,0,1:T(8,128)(2,1)} %copy.54), calls=%async_computation.1 | async-start | bytes 20971520 | tf_op jit(solution)/shard_map/all_to_all | solution.py:45
  65.5 0.0 copy-done
  65.5 15.2 %convolution_convert_fusion = bf16[2,640,4096]{2,1,0:T(8,128)(2,1)} fusion(bf16[2,640,768]{2,1,0:T(8,128)(2,1)S(1)} %bitcast.35, bf16[2,768,4096]{2,1,0:T(8,128)(2,1)} %param.9), kind=kOutput, calls=%fused_computation.8 | convolution fusion | flops 8058306560 | bytes 25034752 | tf_op jit(solution)/shard_map/lrf,lfd->lrd/dot_general | solution.py:62
  80.7 9.5 %copy.58 = bf16[2,16,40,4096]{3,2,0,1:T(8,128)(2,1)} copy(bf16[2,16,40,4096]{3,2,1,0:T(8,128)(2,1)} %bitcast.38) | data formatting | bytes 20971520 | tf_op jit(solution)/shard_map/reshape | solution.py:66
  90.2 128.6 %all-to-all-done.1 = bf16[2,16,40,4096]{3,2,0,1:T(8,128)(2,1)} async-done(((bf16[2,16,40,4096]{3,2,0,1:T(8,128)(2,1)}), bf16[2,16,40,4096]{3,2,0,1:T(8,128)(2,1)}, u32[]{:S(2)}, u32[]{:S(2)}) %all-to-all-start.1) | async-done | bytes 10485792 | tf_op jit(solution)/shard_map/all_to_all | solution.py:45
  218.8 6.1 %all-to-all-start.2 = ((bf16[2,16,40,4096]{3,2,0,1:T(8,128)(2,1)}), bf16[2,16,40,4096]{3,2,0,1:T(8,128)(2,1)}, u32[]{:S(2)}, u32[]{:S(2)}) async-start(bf16[2,16,40,4096]{3,2,0,1:T(8,128)(2,1)} %copy.58), calls=%async_computation.2 | async-start | bytes 20971520 | tf_op jit(solution)/shard_map/all_to_all | solution.py:65
  224.8 0.2 all-reduce.4.cloned.1.call-start
  225.1 11.0 %multiply_convert_fusion = bf16[2,16,40,4096]{3,2,1,0:T(8,128)(2,1)} fusion(bf16[2,16,40,4096]{3,2,0,1:T(8,128)(2,1)} %all-to-all-done.1, f32[2,16,40]{2,1,0:T(8,128)S(1)} %copy_convert_fusion), kind=kLoop, calls=%fused_computation.4 | loop fusion | flops 15728640 | bytes 20976640 | tf_op jit(solution)/shard_map/convert_element_type | solution.py:48
  236.0 15.5 %convert_bitcast_fusion = bf16[2,768,4096]{1,2,0:T(8,128)(2,1)} fusion(bf16[2,640,4096]{2,1,0:T(8,128)(2,1)} %bitcast.39, bf16[2,640,768]{2,1,0:T(8,128)(2,1)S(1)} %bitcast.34), kind=kOutput, calls=%fused_computation.7 | convolution fusion | flops 8059355136 | bytes 25034752 | tf_op jit(solution)/shard_map/lrf,lrd->lfd/dot_general | solution.py:56
  251.5 31.6 %copy.57 = bf16[2,768,4096]{2,0,1:T(2,128)(2,1)} copy(bf16[2,768,4096]{1,2,0:T(8,128)(2,1)} %convert_bitcast_fusion) | data formatting | bytes 25165824 | tf_op jit(solution)/shard_map/convert_element_type | solution.py:60
  283.1 0.0 copy-start.2
  283.1 0.0 copy-start.3
  283.1 0.0 all-reduce.4.cloned.1.call-update
  283.1 1.2 copy-done.2
  284.3 1.5 convert_element_type.52
  285.8 0.0 copy-done.3
  285.8 0.6 dynamic-slice
  287.1 89.1 %all-to-all-done.2 = bf16[2,16,40,4096]{3,2,0,1:T(8,128)(2,1)} async-done(((bf16[2,16,40,4096]{3,2,0,1:T(8,128)(2,1)}), bf16[2,16,40,4096]{3,2,0,1:T(8,128)(2,1)}, u32[]{:S(2)}, u32[]{:S(2)}) %all-to-all-start.2) | async-done | bytes 10485792 | tf_op jit(solution)/shard_map/all_to_all | solution.py:65
  376.1 9.6 %copy.59 = bf16[2,16,40,4096]{3,2,1,0:T(8,128)(2,1)} copy(bf16[2,16,40,4096]{3,2,0,1:T(8,128)(2,1)} %all-to-all-done.2) | data formatting | bytes 20971520 | tf_op jit(solution)/shard_map/all_to_all | solution.py:65
  385.8 20.6 %gather_fusion.2 = bf16[1024,4096]{1,0:T(8,128)(2,1)} fusion(bf16[1280,4096]{1,0:T(8,128)(2,1)} %bitcast.36, s32[1024]{0:T(1024)S(1)} %broadcast_clamp_fusion), kind=kCustom, calls=%fused_computation.2 | custom fusion | bytes 16781312 | tf_op jit(solution)/shard_map/gather | solution.py:72
  406.4 5.9 %fusion = f32[128,8]{1,0:T(8,128)S(1)} fusion(bf16[1024,4096]{1,0:T(8,128)(2,1)} %gather_fusion.2, f32[128,4096]{1,0:T(8,128)} %convert_element_type.52), kind=kLoop, calls=%fused_computation.6 | loop fusion | flops 12581888 | bytes 10489856 | tf_op jit(solution)/shard_map/reduce_sum | solution.py:73
  412.3 0.7 copy.61
  413.0 0.0 copy-start.1
  413.0 16.1 %convolution_convert_fusion.1 = bf16[2,640,768]{2,1,0:T(8,128)(2,1)} fusion(bf16[2,640,4096]{2,1,0:T(8,128)(2,1)} %bitcast.40, bf16[2,768,4096]{2,1,0:T(8,128)(2,1)} %param.9), kind=kOutput, calls=%fused_computation.9 | convolution fusion | flops 8054046720 | bytes 25034752 | tf_op jit(solution)/shard_map/lrd,lfd->lrf/dot_general | solution.py:53
  429.1 0.9 all-reduce.4.cloned.1.call-done
  430.0 2.9 constant_dynamic-slice_fusion
  432.9 2.0 copy.60
  434.9 0.0 copy-done.1
  (15 shorter events, 0.3 us)
Async XLA Ops:
  7.2 58.4 %copy-start = (bf16[1,2,16,40,768]{4,3,2,1,0:T(8,128)(2,1)S(1)}, bf16[1,2,16,40,768]{4,3,2,1,0:T(8,128)(2,1)}, u32[]{:S(2)}) copy-start(bf16[1,2,16,40,768]{4,3,2,1,0:T(8,128)(2,1)} %param.8) | copy-start | bytes 5898244
  32.0 26.3 %all-to-all-start = ((bf16[2,16,40]{2,0,1:T(2,128)(2,1)}), bf16[2,16,40]{2,0,1:T(2,128)(2,1)S(1)}, u32[]{:S(2)}, u32[]{:S(2)}) async-start(bf16[2,16,40]{2,0,1:T(2,128)(2,1)} %copy.52), calls=%async_computation | async-start | bytes 16384 | tf_op jit(solution)/shard_map/all_to_all | solution.py:46
  58.3 160.5 %all-to-all-start.1 = ((bf16[2,16,40,4096]{3,2,0,1:T(8,128)(2,1)}), bf16[2,16,40,4096]{3,2,0,1:T(8,128)(2,1)}, u32[]{:S(2)}, u32[]{:S(2)}) async-start(bf16[2,16,40,4096]{3,2,0,1:T(8,128)(2,1)} %copy.54), calls=%async_computation.1 | async-start | bytes 20971520 | tf_op jit(solution)/shard_map/all_to_all | solution.py:45
  218.8 157.4 %all-to-all-start.2 = ((bf16[2,16,40,4096]{3,2,0,1:T(8,128)(2,1)}), bf16[2,16,40,4096]{3,2,0,1:T(8,128)(2,1)}, u32[]{:S(2)}, u32[]{:S(2)}) async-start(bf16[2,16,40,4096]{3,2,0,1:T(8,128)(2,1)} %copy.58), calls=%async_computation.2 | async-start | bytes 20971520 | tf_op jit(solution)/shard_map/all_to_all | solution.py:65
  224.8 205.2 %all-reduce.4.cloned.1.call-start = ((), (), s32[]{:S(2)}) async-start(), calls=%async_computation.3 | async-start | bytes 25165824
  283.1 1.2 copy-start.2
  283.1 2.7 copy-start.3
  413.0 21.9 %copy-start.1 = (bf16[1,2,16,40,768]{4,3,2,1,0:T(8,128)(2,1)S(1)}, bf16[1,2,16,40,768]{4,3,2,1,0:T(8,128)(2,1)}, u32[]{:S(2)}) copy-start(bf16[1,2,16,40,768]{4,3,2,1,0:T(8,128)(2,1)} %param.8) | copy-start | bytes 5898244
Sparse Core Ops, SparseCore 0:
  283.2 146.7 all-reduce.3
where the time goes:
time: 444 us; the launch traced here: 442 us
  waiting for transfers between devices  219 us (49%)
  local copies, waits for them, and re-layouts  113 us (25%)
  matrix products  46.7 us (11%)
  other arithmetic  27.6 us (6%)
  starting transfers between devices  20.7 us (5%)
  between operations  14.9 us (3%)
    all_to_all x1, waiting for transfers between devices, shards(): lax.all_to_all(dy_slots, 'expert', split_axis=1, concat_axis=1, tiled=True)  129 us
    all_to_all x1, waiting for transfers between devices, shards(): lax.all_to_all(expert_rows.reshape(experts_held, expert_groups, capacity,...  89.1 us
    convert_element_type x1, local copies, waits for them, and re-layouts, shards(): partial_value.astype(jnp.bfloat16)  31.6 us
    gather x1, local copies, waits for them, and re-layouts, shards(): returned.reshape(-1, model_width)[slot_index]  20.6 us
    dot_general x1, matrix products, shards(): jnp.einsum('lrd,lfd->lrf', gated_rows, w_down, preferred_element_type=jnp...  16.1 us
    dot_general x1, matrix products, shards(): jnp.einsum('lrf,lrd->lfd', hidden, gated_rows, preferred_element_type=jnp...  15.5 us
    dot_general x1, matrix products, shards(): jnp.einsum('lrf,lfd->lrd', hidden, w_down, preferred_element_type=jnp.flo...  15.2 us
    convert_element_type x1, other arithmetic, shards(): (got_gate.astype(jnp.float32)[..., None] * got_dy.astype(jnp.float32)).as...  11 us
  transfers between devices with their start and end apart: 4, of which 3 were waited for; matrix products, arithmetic and copies ran while one was open for 35% of the time, Pallas kernels for 0%

commit v1 on v0

v1 whole, which is shorter than its diff:
```python
import jax
import jax.numpy as jnp
from jax import lax
from jax.experimental import pallas as pl
from jax.experimental.pallas import tpu as pltpu
from jax.sharding import PartitionSpec as P

AXES = ("section", "expert")
CHUNKS = (1024, 1024, 1024, 1024)
TILE = 512
DEEP = 1024
VMEM_LIMIT = 20 * 1024 * 1024
COSTS = {"o": 20, "a": 20, "r": 20, "I": 20, "P": 20, "T": 20, "p": 20, "w": 20, "m": 20, "s": 20, "t": 20, "e": 20, "h": 20, "H": 20}
PLAN = (
    "a0", "a1", "I", "o2", "o3", "r0", "r1", "a2", "a3", "P", "T", "r2", "r3", "p0", "p1", "p2",
    "p3", "w0", "m0", "w1", "m1", "s0", "s1", "h", "w2", "w3", "t0", "t1", "m2", "m3", "s2",
    "s3", "H", "t2", "t3", "e",
)
F32, BF16 = jnp.float32, jnp.bfloat16


def moves(move):
    pairs = []
    for z in range(4):
        for core in range(2):
            for y in range(4):
                for x in range(4):
                    tz, tcore, ty, tx = move(z, core, y, x)
                    pairs.append(
                        (
                            ((z * 2 + core) * 4 + y) * 4 + x,
                            ((tz % 4 * 2 + tcore) * 4 + ty % 4) * 4 + tx % 4,
                        )
                    )
    return pairs


MEET = ((1, 3), (3, 1))


def along(axis, step, parity=0):
    def move(z, core, y, x):
        mask = MEET[core][(step + parity) % 2]
        if axis == "z":
            return (z ^ mask, core, y, x)
        if (axis == "first") == (core == 0):
            return (z, core, y, x ^ mask)
        return (z, core, y ^ mask, x)

    return moves(move)


SWAP = moves(lambda z, core, y, x: (z, 1 - core, y, x))


def send(value, pairs):
    return lax.ppermute(value, AXES, pairs)


class Order:
    def __init__(self):
        self.token = None
        self.cost = 0


ORDER = Order()


def call(kernel, grid, inputs, outputs, scratch=()):
    held = [] if ORDER.token is None else [ORDER.token]
    unused = len(held)

    def run(*refs):
        body = list(refs[unused:])
        body.pop(len(inputs) + len(outputs))[...] = jnp.zeros((8, 128), F32)
        kernel(*body)

    *results, ORDER.token = pl.pallas_call(
        run,
        grid=grid,
        in_specs=[pl.BlockSpec(memory_space=pltpu.HBM)] * unused + [spec for _, spec in inputs],
        out_specs=[spec for _, spec in outputs] + [whole((8, 128))],
        out_shape=[shape for shape, _ in outputs] + [out(8, 128, dtype=F32)],
        scratch_shapes=list(scratch),
        compiler_params=pltpu.CompilerParams(vmem_limit_bytes=VMEM_LIMIT),
        cost_estimate=pl.CostEstimate(
            flops=int(ORDER.cost * 10**9), bytes_accessed=0, transcendentals=0
        ),
    )(*held, *[value for value, _ in inputs])
    return results


def whole(shape):
    return pl.BlockSpec(shape, lambda *_: (0,) * len(shape))


def columns(shape, offset=0):
    lead = (0,) * (len(shape) - 1)
    return pl.BlockSpec(tuple(shape[:-1]) + (TILE,), lambda i: lead + (i + offset // TILE,))


def out(*shape, dtype=BF16):
    return jax.ShapeDtypeStruct(shape, dtype)


SMEM = pl.BlockSpec(memory_space=pltpu.SMEM)


def mm(a, b):
    return jnp.dot(a, b, preferred_element_type=F32)


def mm_turned(a, b):
    return lax.dot_general(a, b, (((1,), (1,)), ((), ())), preferred_element_type=F32)


PIECES = ((0, 0), (0, 1), (0, 2), (2, 0), (2, 1), (1, 0), (1, 2))
RANKED = [(0, r) for r in range(16)] + [
    (g, r) for g in (1, 2) for line in (0, 3 - g) for r in range(line * 4, line * 4 + 4)
]


def prepare(at, info, cap, held):
    sources, _, tokens = info.shape
    row_of = {(g, r, e): n * held + e for n, (g, r) in enumerate(RANKED) for e in range(held)}
    rows = len(row_of)
    packed, line = held * 4 * cap, 4 * tokens

    def kernel(at_ref, info_ref, pick_ref, key_ref, gate_ref, named_ref):
        for n, (g, r) in enumerate(RANKED):
            block = info_ref[at_ref[r]].astype(F32)
            for e in range(held):
                expert = at_ref[16 + g * held + e].astype(F32)
                hit = block[:8] == expert
                named_ref[n * held + e : n * held + e + 1, :] = jnp.max(
                    jnp.where(hit, 1.0, 0.0), axis=0, keepdims=True
                )
                if g == 0:
                    gate_ref[n * held + e : n * held + e + 1, :] = jnp.sum(
                        jnp.where(hit, block[8:], 0.0), axis=0, keepdims=True
                    )
        named = named_ref[...]
        first = lax.broadcasted_iota(jnp.int32, (tokens, tokens), 0)
        second = lax.broadcasted_iota(jnp.int32, (tokens, tokens), 1)
        before = jnp.where(first < second, 1.0, 0.0).astype(BF16)
        key = jnp.where(named > 0.5, mm(named.astype(BF16), before), -1.0)
        key_ref[...] = key[: sources * held]
        named_ref[...] = key
        slot = lax.broadcasted_iota(jnp.int32, (cap, tokens), 0).astype(F32)
        none = jnp.zeros((cap, tokens), F32)
        for n, (g, l) in enumerate(PIECES):
            for s in range(4):
                parts = []
                for e in range(held):
                    row = row_of[g, l * 4 + s, e]
                    mine = jnp.where(slot == named_ref[row : row + 1, :], 1.0, 0.0)
                    parts += [mine if t == s else none for t in range(4)]
                pick_ref[n, :, s * tokens : (s + 1) * tokens] = jnp.concatenate(parts, axis=0).astype(BF16)

    return call(
        kernel,
        (1,),
        [(at, SMEM), (info, whole(info.shape))],
        [
            (out(len(PIECES), packed, line), whole((len(PIECES), packed, line))),
            (out(sources * held, tokens, dtype=F32), whole((sources * held, tokens))),
            (out(sources * held, tokens, dtype=F32), whole((sources * held, tokens))),
        ],
        scratch=[pltpu.VMEM((rows, tokens), F32)],
    )


def slot_hits(key_ref, row, cap):
    key = key_ref[row : row + 1, :]
    slot = lax.broadcasted_iota(jnp.int32, (cap, key.shape[1]), 0).astype(F32)
    return slot == key


def turn_hidden(at, key, gate, hidden):
    held, sources, cap, ff = hidden.shape
    block = ff // 8

    def kernel(at_ref, key_ref, gate_ref, hidden_ref, out_ref):
        for e in range(held):
            parts = []
            for r in range(sources):
                row = r * held + e
                weight = jnp.sum(
                    jnp.where(slot_hits(key_ref, row, cap), gate_ref[row : row + 1, :], 0.0),
                    axis=1,
                    keepdims=True,
                )
                parts.append(hidden_ref[e, at_ref[r]].astype(F32) * weight)
            turned = jnp.concatenate(parts, axis=0).T.astype(BF16)
            for b in range(8):
                out_ref[at_ref[24 + b], e] = turned[b * block : (b + 1) * block]

    shape = (8, held, block, sources * cap)
    return call(
        kernel,
        (1,),
        [(at, SMEM), (key, whole(key.shape)), (gate, whole(gate.shape)), (hidden, whole(hidden.shape))],
        [(out(*shape), whole(shape))],
    )[0]


def share(info, sources):
    def kernel(info_ref, out_ref):
        out_ref[...] = jnp.broadcast_to(info_ref[...].astype(BF16)[None], out_ref.shape)

    shape = (sources,) + info.shape
    return call(kernel, (1,), [(info, whole(info.shape))], [(out(*shape), whole(shape))])[0]


def own_rows(d_output, offset, size):
    tokens = d_output.shape[0]

    def kernel(in_ref, out_ref):
        out_ref[...] = in_ref[...]

    return call(
        kernel,
        (size // TILE,),
        [(d_output, columns(d_output.shape, offset))],
        [(out(tokens, size), columns((tokens, size)))],
    )[0]


def join(d_output, offset, pieces):
    tokens, size = d_output.shape[0], pieces[0][0].shape[1]

    def spec(at):
        return pl.BlockSpec((tokens, TILE), lambda i: (at, i))

    def kernel(*refs):
        for n, ref in enumerate(refs[:-1]):
            refs[-1][n * tokens : (n + 1) * tokens, :] = ref[...]

    shape = (tokens * (1 + len(pieces)), size)
    return call(
        kernel,
        (size // TILE,),
        [(d_output, columns(d_output.shape, offset))] + [(b, spec(at)) for b, at in pieces],
        [(out(*shape), columns(shape))],
    )[0]


def pack(rows, far, pick, held, parity):
    line, size = rows.shape
    count = pick.shape[1]
    per = count // held
    shape = (held, 2 * per, size)
    near, there = 1 + parity, 2 - parity

    places = [(group, start) for group in (there, 0) for start in (0, near)]

    def kernel(rows_ref, far_ref, *refs):
        picks, (here_ref, there_ref) = refs[:4], refs[4:]
        for k, pick_ref in enumerate(picks):
            chosen = mm(pick_ref[0], (rows_ref, far_ref)[k % 2][...]).astype(BF16)
            target, n = (there_ref, here_ref)[k // 2], k % 2
            for e in range(held):
                target[e, n * per : (n + 1) * per, :] = chosen[e * per : (e + 1) * per]

    def piece(place):
        at = PIECES.index(place)
        return pl.BlockSpec((1, count, line), lambda i: (at, 0, 0))

    return call(
        kernel,
        (size // TILE,),
        [(rows, columns(rows.shape)), (far, columns(far.shape))]
        + [(pick, piece(place)) for place in places],
        [(out(*shape), columns(shape)), (out(*shape), columns(shape))],
    )


def collect(here, came, turned, parity):
    held, half, size = here.shape
    block, total = turned.shape[2:]
    per = half // 2
    places = ((0, 1), (2, 3)) if parity == 0 else ((0, 2), (1, 3))

    def kernel(here_ref, came_ref, turned_ref, slots_ref, other_ref):
        for e in range(held):
            for ref, lines in zip((here_ref, came_ref), places):
                for n, at in enumerate(lines):
                    slots_ref[e, at * per : (at + 1) * per, :] = ref[e, n * per : (n + 1) * per]
            left = turned_ref[:, e].reshape(4 * block, total)
            product = mm(left, slots_ref[e])
            for n in range(4):
                other_ref[n, e] = product[n * block : (n + 1) * block].astype(BF16)

    return call(
        kernel,
        (size // TILE,),
        [
            (here, columns(here.shape)),
            (came, columns(came.shape)),
            (turned, pl.BlockSpec((4, held, block, total), lambda i: (1, 0, 0, 0))),
        ],
        [
            (out(held, total, size), columns((held, total, size))),
            (out(4, held, block, size), columns((4, held, block, size))),
        ],
    )


def own_product(slots, turned):
    held, total, size = slots.shape
    block = turned.shape[2]

    def kernel(slots_ref, turned_ref, mine_ref):
        for e in range(held):
            product = mm(turned_ref[:, e].reshape(4 * block, total), slots_ref[e])
            for n in range(4):
                mine_ref[n, e] = product[n * block : (n + 1) * block].astype(BF16)

    return call(
        kernel,
        (size // TILE,),
        [
            (slots, columns(slots.shape)),
            (turned, pl.BlockSpec((4, held, block, total), lambda i: (0, 0, 0, 0))),
        ],
        [(out(4, held, block, size), columns((4, held, block, size)))],
    )[0]


def add_parts(terms):
    shape = (len(terms),) + terms[0][0][0].shape[1:]
    flat = [term for group in terms for term in group]
    width = len(terms[0])

    def spec(at):
        return pl.BlockSpec((1,) + shape[1:-1] + (TILE,), lambda i: (at, 0, 0, i))

    def kernel(*refs):
        for n in range(len(terms)):
            value = 0.0
            for ref in refs[n * width : (n + 1) * width]:
                value = value + ref[0].astype(F32)
            refs[-1][n] = value.astype(BF16)

    return call(
        kernel,
        (shape[-1] // TILE,),
        [(array, spec(at)) for array, at in flat],
        [(out(*shape), columns(shape))],
    )[0]


def finish(parts, width):
    _, held, block, _ = parts[0][0].shape
    counts = [group[0].shape[3] // TILE for group in parts]
    starts = [sum(counts[:n]) for n in range(len(counts))]
    terms = len(parts[0])

    def kernel(*refs):
        step = pl.program_id(0)
        for n, (start, count) in enumerate(zip(starts, counts)):

            @pl.when((step >= start) & (step < start + count))
            def _(n=n):
                value = 0.0
                for ref in refs[n * terms : (n + 1) * terms]:
                    value = value + ref[0].astype(F32)
                refs[-1][...] = value.astype(BF16)

    def spec(start, count):
        return pl.BlockSpec(
            (1, held, block, TILE),
            lambda i: (0, 0, 0, jnp.minimum(jnp.maximum(i - start, 0), count - 1)),
        )

    shape = (held, block, width)
    return call(
        kernel,
        (width // TILE,),
        [(part, spec(a, c)) for group, a, c in zip(parts, starts, counts) for part in group],
        [(out(*shape), columns(shape))],
    )[0]


def chunk_specs(halves, ff):
    rows = halves[0].shape[1]
    counts = [h.shape[2] // DEEP for h in halves]
    starts = [sum(counts[:n]) for n in range(len(halves))]

    def spec(start, count):
        return pl.BlockSpec(
            (1, rows, DEEP), lambda e, i: (e, 0, jnp.minimum(jnp.maximum(i - start, 0), count - 1))
        )

    specs = [spec(a, b) for a, b in zip(starts, counts)]
    return counts, starts, specs, pl.BlockSpec((1, ff, DEEP), lambda e, i: (e, 0, i))


def add_chunks(refs, starts, counts, lines, w_ref, sum_ref):
    step = pl.program_id(1)
    for n, (ref, start, count) in enumerate(zip(refs, starts, counts)):

        @pl.when((step >= start) & (step < start + count))
        def _(n=n, ref=ref):
            product = mm_turned(ref[0], w_ref[0])
            per = product.shape[0] // 2
            for k, line in enumerate(lines[n % 2]):
                sum_ref[line * per : (line + 1) * per, :] += product[k * per : (k + 1) * per]


HERE = ((0, 1), (0, 2))
CAME = ((2, 3), (1, 3))


def hidden_sums(halves, w_down):
    held, rows, _ = halves[0].shape
    ff, total = w_down.shape[1], 2 * rows
    counts, starts, specs, w_spec = chunk_specs(halves, ff)

    def kernel(*refs):
        w_ref, sum_ref, acc_ref = refs[len(halves) :]

        @pl.when(pl.program_id(1) == 0)
        def _():
            acc_ref[...] = jnp.zeros_like(acc_ref)

        add_chunks(refs, starts, counts, HERE, w_ref, acc_ref)

        @pl.when(pl.program_id(1) == sum(counts) - 1)
        def _():
            sum_ref[0] = acc_ref[...]

    return call(
        kernel,
        (held, sum(counts)),
        list(zip(halves, specs)) + [(w_down, w_spec)],
        [(out(held, total, ff, dtype=F32), pl.BlockSpec((1, total, ff), lambda e, i: (e, 0, 0)))],
        scratch=[pltpu.VMEM((total, ff), F32)],
    )[0]


def hidden_end(at, key, gate, hidden, sums, halves, w_down):
    held, sources, cap, ff = hidden.shape
    total = sums.shape[1]
    tokens = key.shape[1]
    counts, starts, specs, w_spec = chunk_specs(halves, ff)

    def kernel(at_ref, key_ref, gate_ref, hidden_ref, sums_ref, *refs):
        w_ref, d_hidden_ref, grad_ref, acc_ref = refs[len(halves) :]

        @pl.when(pl.program_id(1) == 0)
        def _():
            acc_ref[...] = sums_ref[0]

        add_chunks(refs, starts, counts, CAME, w_ref, acc_ref)

        def end(e):
            for r in range(sources):
                row = r * held + e
                hits = slot_hits(key_ref, row, cap)
                weight = jnp.sum(
                    jnp.where(hits, gate_ref[row : row + 1, :], 0.0), axis=1, keepdims=True
                )
                value = acc_ref[r * cap : (r + 1) * cap, :]
                place = at_ref[r]
                d_hidden_ref[0, place] = (value * weight).astype(BF16)
                dots = jnp.sum(value * hidden_ref[0, place].astype(F32), axis=1, keepdims=True)
                grad_ref[place, e : e + 1, :] = jnp.sum(
                    jnp.where(hits, dots, 0.0), axis=0, keepdims=True
                )

        for e in range(held):

            @pl.when((pl.program_id(1) == sum(counts) - 1) & (pl.program_id(0) == e))
            def _(e=e):
                end(e)

    by_expert = pl.BlockSpec((1, sources, cap, ff), lambda e, i: (e, 0, 0, 0))
    return call(
        kernel,
        (held, sum(counts)),
        [
            (at, SMEM),
            (key, whole(key.shape)),
            (gate, whole(gate.shape)),
            (hidden, by_expert),
            (sums, pl.BlockSpec((1, total, ff), lambda e, i: (e, 0, 0))),
        ]
        + list(zip(halves, specs))
        + [(w_down, w_spec)],
        [
            (out(*hidden.shape), by_expert),
            (out(sources, held, tokens, dtype=F32), whole((sources, held, tokens))),
        ],
        scratch=[pltpu.VMEM((total, ff), F32)],
    )


def shards(d_output, gate_values, routes, hidden_saved, w_down):
    ORDER.token = None
    tokens, width = d_output.shape
    hidden = hidden_saved[0]
    held, sources, cap, ff = hidden.shape

    section, group = lax.axis_index("section"), lax.axis_index("expert")
    z, core, y, x = section // 2, section % 2, group // 4, group % 4
    masks = jnp.stack([0 * core, 1 + 2 * core, 3 - 2 * core, 0 * core + 2])
    first_at = jnp.where(core == 0, x, y) ^ masks
    second_at = jnp.where(core == 0, y, x) ^ masks
    up_first, up_second = jnp.where(core == 0, 1, 4), jnp.where(core == 0, 4, 1)
    source_at = (second_at[:, None] * up_second + first_at[None, :] * up_first).reshape(-1)
    group_at = second_at[:4] * up_second + first_at[0] * up_first
    experts = (group_at[:, None] * held + jnp.arange(held)[None, :]).reshape(-1)
    section_at = jnp.arange(8)
    met = (section_at // 2) ^ z
    place = jnp.where(met == 2, 3, jnp.where(met == 0, 0, jnp.where((met == 1) == (section_at % 2 == 0), 2, 1)))
    is_mine = section_at % 2 == core
    at = jnp.concatenate([source_at, experts, jnp.where(is_mine, place, 4 + place)]).astype(jnp.int32)

    offsets = [sum(CHUNKS[:n]) for n in range(len(CHUNKS))]
    info = jnp.concatenate([routes.astype(F32), gate_values.astype(F32)], axis=1).T
    count = len(CHUNKS)
    one, two, rows, far, here, came, slots = ([None] * count for _ in range(7))
    got, mine, passed, more = ([None] * count for _ in range(4))
    for n in range(2):
        own = d_output[:, offsets[n] : offsets[n] + CHUNKS[n]]
        one[n] = send(own, along("first", 0, n % 2))

    for step in PLAN:
        kind, n = step[0], int(step[1:] or 0)
        parity = n % 2
        ORDER.cost = COSTS[kind]
        if kind == "o":
            one[n] = send(own_rows(d_output, offsets[n], CHUNKS[n]), along("first", 0, parity))
        elif kind == "I":
            all_info = lax.all_to_all(share(info, sources), "expert", 0, 0, tiled=True)
        elif kind == "P":
            pick, key, gate = prepare(at, all_info, cap, held)
        elif kind == "T":
            turned = turn_hidden(at, key, gate, hidden)
        elif kind == "a":
            two[n] = send(join(d_output, offsets[n], [(one[n], 0)]), along("first", 1, parity))
        elif kind == "r":
            came_rows = [(one[n], 0), (two[n], 0), (two[n], 1)]
            if parity == 1:
                came_rows = [(two[n], 0), (one[n], 0), (two[n], 1)]
            rows[n] = join(d_output, offsets[n], came_rows)
            far[n] = send(rows[n], along("second", 0, parity))
        elif kind == "p":
            here[n], there = pack(rows[n], far[n], pick, held, parity)
            came[n] = send(there, along("second", 1, parity))
        elif kind == "w":
            slots[n], other = collect(here[n], came[n], turned, parity)
            got[n] = send(other, SWAP)
        elif kind == "m":
            mine[n] = own_product(slots[n], turned)
        elif kind == "s":
            sums = add_parts([[(mine[n], k), (got[n], k)] for k in (2 - parity, 3)])
            passed[n] = send(sums, along("z", 0, parity))
        elif kind == "t":
            sums = add_parts([[(mine[n], 1 + parity), (got[n], 1 + parity), (passed[n], 1)]])
            more[n] = send(sums, along("z", 1, parity))
        elif kind == "e":
            parts = [(mine[k], got[k], passed[k], more[k]) for k in range(count)]
            d_weight = finish(parts, width)
        elif kind == "h":
            hidden_part = hidden_sums(here, w_down)
        elif kind == "H":
            d_hidden, token_grad = hidden_end(at, key, gate, hidden, hidden_part, came, w_down)
    returned = lax.all_to_all(token_grad, "expert", 0, 0, tiled=True).reshape(-1, tokens)
    chosen = routes.T[None] == jnp.arange(sources * held)[:, None, None]
    d_gate = jnp.sum(jnp.where(chosen, returned[:, None, :], 0.0), axis=0).T
    return (d_hidden[None], d_weight, d_gate)


def solution(mesh):
    placed = (
        P(("section", "expert"), None),
        P(("section", "expert"), None),
        P(("section", "expert"), None),
        P("section", "expert", None, None, None),
        P("expert", None, None),
    )
    return jax.shard_map(
        shards,
        mesh=mesh,
        in_specs=placed,
        out_specs=(
            P("section", "expert", None, None, None),
            P("expert", "section", None),
            P(("section", "expert"), None),
        ),
        check_vma=False,
    )
```

time: 444 us -> 168 us (0.38)
  waiting for transfers between devices: 219 us -> 41.1 us
  local copies, waits for them, and re-layouts: 113 us -> 6.88 us
  Pallas kernels: 0 us -> 60.8 us
  matrix products: 46.7 us -> 0 us
  other arithmetic: 27.6 us -> 2.32 us
  starting transfers between devices: 20.7 us -> 41 us
  blocking collectives: 0 us -> 14 us
  between operations: 14.9 us -> 1.36 us
    all_to_all x3 -> x1, waiting for transfers between devices: 218 us -> 0.01 us  [shards(): all_info = lax.all_to_all(share(info, sources), 'expert', 0, 0, tiled=True)]
    pallas_call x0 -> x36, Pallas kernels: none -> 60.8 us  [call(): pl.pallas_call(run, grid=grid, in_specs=[pl.BlockSpec(memory_space=pltpu....]
    dot_general x3 -> x0, matrix products: 46.7 us -> none  [the longest x1 16.1 us: shards(): jnp.einsum('lrd,lfd->lrf', gated_rows, w_down, preferred_element_type=jnp...]
    ppermute x0 -> x28, waiting for transfers between devices: none -> 41.1 us  [send(): return lax.ppermute(value, AXES, pairs)]
    gather x3 -> x0, local copies, waits for them, and re-layouts: 37 us -> none  [the longest x1 20.6 us: shards(): returned.reshape(-1, model_width)[slot_index]]
    ppermute x0 -> x28, starting transfers between devices: none -> 36.2 us  [send(): return lax.ppermute(value, AXES, pairs)]
    convert_element_type x1 -> x0, local copies, waits for them, and re-layouts: 31.6 us -> none  [shards(): partial_value.astype(jnp.bfloat16)]
    reshape x6 -> x0, local copies, waits for them, and re-layouts: 19.8 us -> none  [the longest x1 9.47 us: shards(): expert_rows.reshape(experts_held, expert_groups, capacity, model_width)]
  transfers between devices with their start and end apart: 4 -> 29, of which waited for: 3 -> 8; matrix products, arithmetic and copies ran while one was open for 35% -> 1% of each run, Pallas kernels for 0% -> 33%
where the time goes in v1:
time: 168 us; the launch traced here: 167 us
  Pallas kernels  60.8 us (36%)
  waiting for transfers between devices  41.1 us (24%)
  starting transfers between devices  41 us (24%)
  blocking collectives  14 us (8%)
  local copies, waits for them, and re-layouts  6.88 us (4%)
  other arithmetic  2.32 us (1%)
    pallas_call x36, Pallas kernels, call(): pl.pallas_call(run, grid=grid, in_specs=[pl.BlockSpec(memory_space=pltpu....  60.8 us
    ppermute x28, waiting for transfers between devices, send(): return lax.ppermute(value, AXES, pairs)  41.1 us
    ppermute x28, starting transfers between devices, send(): return lax.ppermute(value, AXES, pairs)  36.2 us
    all_to_all x1, blocking collectives, shards(): lax.all_to_all(token_grad, 'expert', 0, 0, tiled=True).reshape(-1, tokens)  14 us
    unnamed x70, local copies, waits for them, and re-layouts  5.64 us
    all_to_all x1, starting transfers between devices, shards(): all_info = lax.all_to_all(share(info, sources), 'expert', 0, 0, tiled=True)  4.81 us
  transfers between devices with their start and end apart: 29, of which 8 were waited for; matrix products, arithmetic and copies ran while one was open for 1% of the time, Pallas kernels for 33%

profile of v1, /device:TPU:0, one launch (start us, length us, event | category | flops | bytes accessed | tf_op | source)
XLA Modules:
  0.0 167.5 jit_solution(14576607043798555697)
XLA Ops:
  0.6 1.1 fusion.1
  1.7 2.9 %collective-permute-start.1 = (bf16[128,1024]{1,0:T(8,128)(2,1)S(1)}, bf16[128,1024]{1,0:T(8,128)(2,1)S(1)}, u32[]{:S(2)}, u32[]{:S(2)}) collective-permute-start(bf16[128,1024]{1,0:T(8,128)(2,1)S(1)} %get-tuple-element.172), channel_id=1, source_target_pairs={{0,3},{1,2},{2,1},{3,0},{4,7},{5,6},{6,5},{7,4},{8,11},{9,10},{10,... | collective-permute-start | bytes 786440 | tf_op jit(solution)/shard_map/ppermute | solution.py:57
  6.8 4.2 %collective-permute-done.refs_1_.refs_2_ = bf16[128,1024]{1,0:T(8,128)(2,1)S(1)} collective-permute-done((bf16[128,1024]{1,0:T(8,128)(2,1)S(1)}, bf16[128,1024]{1,0:T(8,128)(2,1)S(1)}, u32[]{:S(2)}, u32[]{:S(2)}) %collective-permute-start) | collective-permute-done | bytes 262176 | tf_op jit(solution)/shard_map/ppermute | solution.py:57
  11.0 1.2 copy-done
  13.3 4.8 %all-to-all-start = ((bf16[16,16,128]{2,1,0:T(8,128)(2,1)}), bf16[16,16,128]{2,1,0:T(8,128)(2,1)S(1)}, u32[]{:S(2)}, u32[]{:S(2)}) async-start(bf16[16,16,128]{2,1,0:T(8,128)(2,1)} %get-tuple-element.98), calls=%async_computation | async-start | bytes 131072 | tf_op jit(solution)/shard_map/all_to_all | solution.py:536
  18.2 3.2 %collective-permute-start.2 = (bf16[256,1024]{1,0:T(8,128)(2,1)S(1)}, bf16[256,1024]{1,0:T(8,128)(2,1)S(1)}, u32[]{:S(2)}, u32[]{:S(2)}) collective-permute-start(bf16[256,1024]{1,0:T(8,128)(2,1)S(1)} %get-tuple-element.90), channel_id=1, source_target_pairs={{0,3},{1,2},{2,1},{3,0},{4,7},{5,6},{6,5},{7,4},{8,11},{9,10},{10,... | collective-permute-start | bytes 1572872 | tf_op jit(solution)/shard_map/ppermute | solution.py:57
  22.5 1.3 collective-permute-start.3
  23.8 5.2 %collective-permute-done.2.refs_3_.refs_4_ = bf16[256,1024]{1,0:T(8,128)(2,1)S(1)} collective-permute-done((bf16[256,1024]{1,0:T(8,128)(2,1)S(1)}, bf16[256,1024]{1,0:T(8,128)(2,1)S(1)}, u32[]{:S(2)}, u32[]{:S(2)}) %collective-permute-start.2) | collective-permute-done | bytes 524320 | tf_op jit(solution)/shard_map/ppermute | solution.py:57
  29.2 4.5 %collective-permute-done.3.refs_2_.refs_4_ = bf16[256,1024]{1,0:T(8,128)(2,1)S(1)} collective-permute-done((bf16[256,1024]{1,0:T(8,128)(2,1)S(1)}, bf16[256,1024]{1,0:T(8,128)(2,1)S(1)}, u32[]{:S(2)}, u32[]{:S(2)}) %collective-permute-start.3) | collective-permute-done | bytes 524320 | tf_op jit(solution)/shard_map/ppermute | solution.py:57
  34.0 0.9 shard_map.83
  35.0 0.9 shard_map.84
  36.6 2.4 %collective-permute-start.6 = (bf16[256,1024]{1,0:T(8,128)(2,1)}, bf16[256,1024]{1,0:T(8,128)(2,1)}, u32[]{:S(2)}, u32[]{:S(2)}) collective-permute-start(bf16[256,1024]{1,0:T(8,128)(2,1)} %get-tuple-element.103), channel_id=1, source_target_pairs={{0,3},{1,2},{2,1},{3,0},{4,7},{5,6},{6,5},{7,4},{8,11},{9,10},{10,... | collective-permute-start | bytes 1572872 | tf_op jit(solution)/shard_map/ppermute | solution.py:57
  39.1 2.7 %collective-permute-start.9 = (bf16[512,1024]{1,0:T(8,128)(2,1)S(1)}, bf16[512,1024]{1,0:T(8,128)(2,1)}, u32[]{:S(2)}, u32[]{:S(2)}) collective-permute-start(bf16[512,1024]{1,0:T(8,128)(2,1)S(1)} %get-tuple-element.110.refs_1_), channel_id=1, source_target_pairs={{0,12},{1,13},{2,14},{3,15},{4,8},{5,9},{6,10},{7,11},{8,4},{9,5},... | collective-permute-start | bytes 3145736 | tf_op jit(solution)/shard_map/ppermute | solution.py:57
  42.0 1.0 shard_map.85
  43.5 1.5 shard_map.86
  45.1 7.8 %collective-permute-done.6.refs_3_.refs_4_ = bf16[256,1024]{1,0:T(8,128)(2,1)} collective-permute-done((bf16[256,1024]{1,0:T(8,128)(2,1)}, bf16[256,1024]{1,0:T(8,128)(2,1)}, u32[]{:S(2)}, u32[]{:S(2)}) %collective-permute-start.6) | collective-permute-done | bytes 524320 | tf_op jit(solution)/shard_map/ppermute | solution.py:57
  52.9 1.3 shard_map.87
  54.2 1.2 shard_map.88
  55.4 2.9 %collective-permute-start.11 = (bf16[512,1024]{1,0:T(8,128)(2,1)S(1)}, bf16[512,1024]{1,0:T(8,128)(2,1)S(1)}, u32[]{:S(2)}, u32[]{:S(2)}) collective-permute-start(bf16[512,1024]{1,0:T(8,128)(2,1)S(1)} %get-tuple-element.114.refs_1_), channel_id=1, source_target_pairs={{0,12},{1,13},{2,14},{3,15},{4,8},{5,9},{6,10},{7,11},{8,4},{9,5},... | collective-permute-start | bytes 3145736 | tf_op jit(solution)/shard_map/ppermute | solution.py:57
  58.6 3.0 %shard_map.89 = (bf16[2,320,1024]{2,1,0:T(8,128)(2,1)S(1)}, bf16[2,320,1024]{2,1,0:T(8,128)(2,1)S(1)}, f32[8,128]{1,0:T(8,128)S(1)}) custom-call(f32[8,128]{1,0:T(8,128)S(1)} %get-tuple-element.106.refs_0_, bf16[512,1024]{1,0:T(8,128)(2,1)S(1)} %get-tuple-element.107.refs_1_, bf16[512,1024]{1,0:T(8,128)(2,1)} %collective-permute-done.8.refs_2_, ...), custom_call_target="tpu_custom_call" | custom-call | flops 20000000000 | tf_op jit(solution)/shard_map/pallas_call | solution.py:78
  61.6 3.0 %shard_map.90 = (bf16[2,320,1024]{2,1,0:T(8,128)(2,1)S(1)}, bf16[2,320,1024]{2,1,0:T(8,128)(2,1)S(1)}, f32[8,128]{1,0:T(8,128)S(1)}) custom-call(f32[8,128]{1,0:T(8,128)S(1)} %get-tuple-element.109.refs_0_, bf16[512,1024]{1,0:T(8,128)(2,1)S(1)} %get-tuple-element.110.refs_1_, bf16[512,1024]{1,0:T(8,128)(2,1)} %collective-permute-done.9.refs_2_, ...), custom_call_target="tpu_custom_call" | custom-call | flops 20000000000 | tf_op jit(solution)/shard_map/pallas_call | solution.py:78
  64.6 1.9 %collective-permute-start.13 = (bf16[2,320,1024]{2,1,0:T(8,128)(2,1)S(1)}, bf16[2,320,1024]{2,1,0:T(8,128)(2,1)S(1)}, u32[]{:S(2)}, u32[]{:S(2)}) collective-permute-start(bf16[2,320,1024]{2,1,0:T(8,128)(2,1)S(1)} %get-tuple-element.123), channel_id=1, source_target_pairs={{0,4},{1,5},{2,6},{3,7},{4,0},{5,1},{6,2},{7,3},{8,12},{9,13},{10,... | collective-permute-start | bytes 3932168 | tf_op jit(solution)/shard_map/ppermute | solution.py:57
  66.8 6.3 %collective-permute-done.10.refs_2_ = bf16[512,1024]{1,0:T(8,128)(2,1)S(1)} collective-permute-done((bf16[512,1024]{1,0:T(8,128)(2,1)S(1)}, bf16[512,1024]{1,0:T(8,128)(2,1)S(1)}, u32[]{:S(2)}, u32[]{:S(2)}) %collective-permute-start.10) | collective-permute-done | bytes 1048608 | tf_op jit(solution)/shard_map/ppermute | solution.py:57
  73.1 2.1 %shard_map.91 = (bf16[2,320,1024]{2,1,0:T(8,128)(2,1)S(1)}, bf16[2,320,1024]{2,1,0:T(8,128)(2,1)S(1)}, f32[8,128]{1,0:T(8,128)S(1)}) custom-call(f32[8,128]{1,0:T(8,128)S(1)} %get-tuple-element.111.refs_0_, bf16[512,1024]{1,0:T(8,128)(2,1)S(1)} %get-tuple-element.112.refs_1_, bf16[512,1024]{1,0:T(8,128)(2,1)S(1)} %collective-permute-done.10.refs_2_, ...), custom_call_target="tpu_custom_call" | custom-call | flops 20000000000 | tf_op jit(solution)/shard_map/pallas_call | solution.py:78
  75.2 2.8 %shard_map.92 = (bf16[2,320,1024]{2,1,0:T(8,128)(2,1)S(1)}, bf16[2,320,1024]{2,1,0:T(8,128)(2,1)}, f32[8,128]{1,0:T(8,128)S(1)}) custom-call(f32[8,128]{1,0:T(8,128)S(1)} %get-tuple-element.113.refs_0_, bf16[512,1024]{1,0:T(8,128)(2,1)S(1)} %get-tuple-element.114.refs_1_, bf16[512,1024]{1,0:T(8,128)(2,1)S(1)} %collective-permute-done.11.refs_2_, ...), custom_call_target="tpu_custom_call" | custom-call | flops 20000000000 | tf_op jit(solution)/shard_map/pallas_call | solution.py:78
  78.2 1.1 collective-permute-start.16
  79.3 6.2 %collective-permute-done.12.refs_2_.refs_6_ = bf16[2,320,1024]{2,1,0:T(8,128)(2,1)S(1)} collective-permute-done((bf16[2,320,1024]{2,1,0:T(8,128)(2,1)S(1)}, bf16[2,320,1024]{2,1,0:T(8,128)(2,1)S(1)}, u32[]{:S(2)}, u32[]{:S(2)}) %collective-permute-start.12) | collective-permute-done | bytes 1310752 | tf_op jit(solution)/shard_map/ppermute | solution.py:57
  85.5 2.1 %shard_map.93 = (bf16[2,640,1024]{2,1,0:T(8,128)(2,1)S(1)}, bf16[4,2,96,1024]{3,2,1,0:T(8,128)(2,1)S(1)}, f32[8,128]{1,0:T(8,128)S(1)}) custom-call(f32[8,128]{1,0:T(8,128)S(1)} %get-tuple-element.115.refs_0_, bf16[2,320,1024]{2,1,0:T(8,128)(2,1)S(1)} %get-tuple-element.116.refs_1_, bf16[2,320,1024]{2,1,0:T(8,128)(2,1)S(1)} %collective-permute-done.12.refs_2_.refs_6_, ...), custom_call_target="tpu_custom_call" | custom-call | flops 20000000000 | tf_op jit(solution)/shard_map/pallas_call | solution.py:78
  87.9 1.9 %shard_map.94 = (bf16[4,2,96,1024]{3,2,1,0:T(8,128)(2,1)S(1)}, f32[8,128]{1,0:T(8,128)S(1)}) custom-call(f32[8,128]{1,0:T(8,128)S(1)} %get-tuple-element.119.refs_0_, bf16[2,640,1024]{2,1,0:T(8,128)(2,1)S(1)} %get-tuple-element.120.refs_1_, bf16[8,2,96,640]{3,2,1,0:T(8,128)(2,1)S(1)} %get-tuple-element.118.refs_3_.refs_2_), custom_call_target="tpu_custom_call" | custom-call | flops 20000000000 | tf_op jit(solution)/shard_map/pallas_call | solution.py:78
  89.8 2.1 %shard_map.95 = (bf16[2,640,1024]{2,1,0:T(8,128)(2,1)S(1)}, bf16[4,2,96,1024]{3,2,1,0:T(8,128)(2,1)S(1)}, f32[8,128]{1,0:T(8,128)S(1)}) custom-call(f32[8,128]{1,0:T(8,128)S(1)} %get-tuple-element.121.refs_0_, bf16[2,320,1024]{2,1,0:T(8,128)(2,1)S(1)} %get-tuple-element.122.refs_1_.refs_2_, ...), custom_call_target="tpu_custom_call" | custom-call | flops 20000000000 | tf_op jit(solution)/shard_map/pallas_call | solution.py:78
  92.5 1.9 %shard_map.96 = (bf16[4,2,96,1024]{3,2,1,0:T(8,128)(2,1)S(1)}, f32[8,128]{1,0:T(8,128)S(1)}) custom-call(f32[8,128]{1,0:T(8,128)S(1)} %get-tuple-element.124.refs_0_, bf16[2,640,1024]{2,1,0:T(8,128)(2,1)S(1)} %get-tuple-element.125.refs_1_, bf16[8,2,96,640]{3,2,1,0:T(8,128)(2,1)S(1)} %get-tuple-element.118.refs_3_.refs_2_), custom_call_target="tpu_custom_call" | custom-call | flops 20000000000 | tf_op jit(solution)/shard_map/pallas_call | solution.py:78
  94.9 2.0 %collective-permute-start.18 = (bf16[2,2,96,1024]{3,2,1,0:T(8,128)(2,1)S(1)}, bf16[2,2,96,1024]{3,2,1,0:T(8,128)(2,1)S(1)}, u32[]{:S(2)}, u32[]{:S(2)}) collective-permute-start(bf16[2,2,96,1024]{3,2,1,0:T(8,128)(2,1)S(1)} %get-tuple-element.140), channel_id=1, source_target_pairs={{0,32},{1,33},{2,34},{3,35},{4,36},{5,37},{6,38},{7,39},{8,40},{9,... | collective-permute-start | bytes 2359304 | tf_op jit(solution)/shard_map/ppermute | solution.py:57
  97.3 2.8 %collective-permute-start.19 = (bf16[2,2,96,1024]{3,2,1,0:T(8,128)(2,1)S(1)}, bf16[2,2,96,1024]{3,2,1,0:T(8,128)(2,1)S(1)}, u32[]{:S(2)}, u32[]{:S(2)}) collective-permute-start(bf16[2,2,96,1024]{3,2,1,0:T(8,128)(2,1)S(1)} %get-tuple-element.142), channel_id=1, source_target_pairs={{0,96},{1,97},{2,98},{3,99},{4,100},{5,101},{6,102},{7,103},{8,104... | collective-permute-start | bytes 2359304 | tf_op jit(solution)/shard_map/ppermute | solution.py:57
  100.1 7.4 %shard_map.99 = (f32[2,640,768]{2,1,0:T(8,128)S(1)}, f32[8,128]{1,0:T(8,128)S(1)}) custom-call(f32[8,128]{1,0:T(8,128)S(1)} %get-tuple-element.132.refs_0_, bf16[2,320,1024]{2,1,0:T(8,128)(2,1)S(1)} %get-tuple-element.116.refs_1_, bf16[2,320,1024]{2,1,0:T(8,128)(2,1)S(1)} %get-tuple-element.122.refs_1_.refs_2_, ...), custom_call_target="tpu_custom_call" | custom-call | flops 20000000000 | tf_op jit(solution)/shard_map/pallas_call | solution.py:78
  107.6 2.1 %shard_map.100 = (bf16[2,640,1024]{2,1,0:T(8,128)(2,1)S(1)}, bf16[4,2,96,1024]{3,2,1,0:T(8,128)(2,1)S(1)}, f32[8,128]{1,0:T(8,128)S(1)}) custom-call(f32[8,128]{1,0:T(8,128)S(1)} %get-tuple-element.135.refs_0_, bf16[2,320,1024]{2,1,0:T(8,128)(2,1)S(1)} %get-tuple-element.133.refs_3_.refs_1_, ...), custom_call_target="tpu_custom_call" | custom-call | flops 20000000000 | tf_op jit(solution)/shard_map/pallas_call | solution.py:78
  110.5 3.0 %shard_map.101 = (bf16[2,640,1024]{2,1,0:T(8,128)(2,1)S(1)}, bf16[4,2,96,1024]{3,2,1,0:T(8,128)(2,1)S(1)}, f32[8,128]{1,0:T(8,128)S(1)}) custom-call(f32[8,128]{1,0:T(8,128)S(1)} %get-tuple-element.137.refs_0_, bf16[2,320,1024]{2,1,0:T(8,128)(2,1)S(1)} %copy-done.21, bf16[2,320,1024]{2,1,0:T(8,128)(2,1)} %collective-permute-done.17.refs_2_.refs_9_, ...), custom_call_target="tpu_custom_call" | custom-call | flops 20000000000 | tf_op jit(solution)/shard_map/pallas_call | solution.py:78
  114.6 2.1 %collective-permute-done.19.refs_3_.refs_7_ = bf16[2,2,96,1024]{3,2,1,0:T(8,128)(2,1)S(1)} collective-permute-done((bf16[2,2,96,1024]{3,2,1,0:T(8,128)(2,1)S(1)}, bf16[2,2,96,1024]{3,2,1,0:T(8,128)(2,1)S(1)}, u32[]{:S(2)}, u32[]{:S(2)}) %collective-permute-start.19) | collective-permute-done | bytes 786464 | tf_op jit(solution)/shard_map/ppermute | solution.py:57
  117.1 3.5 %collective-permute-start.24 = (bf16[1,2,96,1024]{3,2,1,0:T(8,128)(2,1)S(1)}, bf16[1,2,96,1024]{3,2,1,0:T(8,128)(2,1)S(1)}, u32[]{:S(2)}, u32[]{:S(2)}) collective-permute-start(bf16[1,2,96,1024]{3,2,1,0:T(8,128)(2,1)S(1)} %get-tuple-element.161), channel_id=1, source_target_pairs={{0,96},{1,97},{2,98},{3,99},{4,100},{5,101},{6,102},{7,103},{8,104... | collective-permute-start | bytes 1179656 | tf_op jit(solution)/shard_map/ppermute | solution.py:57
  120.6 1.9 %shard_map.104 = (bf16[4,2,96,1024]{3,2,1,0:T(8,128)(2,1)S(1)}, f32[8,128]{1,0:T(8,128)S(1)}) custom-call(f32[8,128]{1,0:T(8,128)S(1)} %get-tuple-element.143.refs_0_, bf16[2,640,1024]{2,1,0:T(8,128)(2,1)S(1)} %get-tuple-element.144.refs_1_, bf16[8,2,96,640]{3,2,1,0:T(8,128)(2,1)S(1)} %copy-done.23), custom_call_target="tpu_custom_call" | custom-call | flops 20000000000 | tf_op jit(solution)/shard_map/pallas_call | solution.py:78
  122.5 1.9 %shard_map.105 = (bf16[4,2,96,1024]{3,2,1,0:T(8,128)(2,1)S(1)}, f32[8,128]{1,0:T(8,128)S(1)}) custom-call(f32[8,128]{1,0:T(8,128)S(1)} %get-tuple-element.145.refs_0_, bf16[2,640,1024]{2,1,0:T(8,128)(2,1)S(1)} %get-tuple-element.146.refs_1_, bf16[8,2,96,640]{3,2,1,0:T(8,128)(2,1)S(1)} %copy-done.23), custom_call_target="tpu_custom_call" | custom-call | flops 20000000000 | tf_op jit(solution)/shard_map/pallas_call | solution.py:78
  124.8 1.1 collective-permute-start.22
  126.4 0.9 collective-permute-start.23
  127.9 1.4 slice-done.5
  130.5 10.2 %shard_map.108 = (bf16[2,16,40,768]{3,2,1,0:T(8,128)(2,1)}, f32[16,2,128]{2,1,0:T(2,128)S(1)}, f32[8,128]{1,0:T(8,128)S(1)}) custom-call(f32[8,128]{1,0:T(8,128)S(1)} %get-tuple-element.153.refs_0_, s32[32]{0:T(128)S(1)} %pad_add_fusion.1.refs_1_, f32[32,128]{1,0:T(8,128)S(1)} %copy-done.25, f32[32,128]{1,0:T(8,128)S(1)} %copy-done.27, ...), custom_call_target="tpu_custom_call" | custom-call | flops 20000000000 | tf_op jit(solution)/shard_map/pallas_call | solution.py:78
  140.7 4.7 %collective-permute-done.22.refs_3_.refs_11_ = bf16[2,2,96,1024]{3,2,1,0:T(8,128)(2,1)S(1)} collective-permute-done((bf16[2,2,96,1024]{3,2,1,0:T(8,128)(2,1)S(1)}, bf16[2,2,96,1024]{3,2,1,0:T(8,128)(2,1)S(1)}, u32[]{:S(2)}, u32[]{:S(2)}) %collective-permute-start.22) | collective-permute-done | bytes 786464 | tf_op jit(solution)/shard_map/ppermute | solution.py:57
  145.7 2.5 %collective-permute-start.26 = (bf16[1,2,96,1024]{3,2,1,0:T(8,128)(2,1)S(1)}, bf16[1,2,96,1024]{3,2,1,0:T(8,128)(2,1)S(1)}, u32[]{:S(2)}, u32[]{:S(2)}) collective-permute-start(bf16[1,2,96,1024]{3,2,1,0:T(8,128)(2,1)S(1)} %get-tuple-element.163), channel_id=1, source_target_pairs={{0,96},{1,97},{2,98},{3,99},{4,100},{5,101},{6,102},{7,103},{8,104... | collective-permute-start | bytes 1179656 | tf_op jit(solution)/shard_map/ppermute | solution.py:57
  148.7 14.0 %all_to_all.10 = f32[16,2,128]{2,1,0:T(2,128)S(1)} all-to-all(f32[16,2,128]{2,1,0:T(2,128)S(1)} %get-tuple-element.166), channel_id=1, replica_groups=mesh['section'=8,'expert'=16] {'expert'}, dimensions={0} | all-to-all | bytes 32768 | tf_op jit(solution)/shard_map/all_to_all | solution.py:570
  163.4 4.1 %shard_map.111 = (bf16[2,96,4096]{2,1,0:T(8,128)(2,1)}, f32[8,128]{1,0:T(8,128)}) custom-call(f32[8,128]{1,0:T(8,128)S(1)} %get-tuple-element.160.refs_0_, bf16[4,2,96,1024]{3,2,1,0:T(8,128)(2,1)S(1)} %copy-done.17, bf16[4,2,96,1024]{3,2,1,0:T(8,128)(2,1)S(1)} %copy-done.5, bf16[2,2,96,1024]{3,2,1,0:T(8,128)(2,1)S(1)} %copy-done.11, ...), custom_call_target="tpu_custom_call" | custom-call | flops 20000000000 | tf_op jit(solution)/shard_map/pallas_call | solution.py:78
  (132 shorter events, 15.2 us)
Async XLA Ops:
  1.7 10.7 %collective-permute-start.1 = (bf16[128,1024]{1,0:T(8,128)(2,1)S(1)}, bf16[128,1024]{1,0:T(8,128)(2,1)S(1)}, u32[]{:S(2)}, u32[]{:S(2)}) collective-permute-start(bf16[128,1024]{1,0:T(8,128)(2,1)S(1)} %get-tuple-element.172), channel_id=1, source_target_pairs={{0,3},{1,2},{2,1},{3,0},{4,7},{5,6},{6,5},{7,4},{8,11},{9,10},{10,... | collective-permute-start | bytes 786440 | tf_op jit(solution)/shard_map/ppermute | solution.py:57
  4.6 6.4 %collective-permute-start = (bf16[128,1024]{1,0:T(8,128)(2,1)S(1)}, bf16[128,1024]{1,0:T(8,128)(2,1)S(1)}, u32[]{:S(2)}, u32[]{:S(2)}) collective-permute-start(bf16[128,1024]{1,0:T(8,128)(2,1)S(1)} %get-tuple-element.173), channel_id=1, source_target_pairs={{0,1},{1,0},{2,3},{3,2},{4,5},{5,4},{6,7},{7,6},{8,9},{9,8},{10,11... | collective-permute-start | bytes 786440 | tf_op jit(solution)/shard_map/ppermute | solution.py:57
  12.6 5.5 %copy-start.1 = (bf16[128,4096]{1,0:T(8,128)(2,1)S(1)}, bf16[128,4096]{1,0:T(8,128)(2,1)}, u32[]{:S(2)}) copy-start(bf16[128,4096]{1,0:T(8,128)(2,1)} %refs_1_.17) | copy-start | bytes 3145732
  13.3 28.7 %all-to-all-start = ((bf16[16,16,128]{2,1,0:T(8,128)(2,1)}), bf16[16,16,128]{2,1,0:T(8,128)(2,1)S(1)}, u32[]{:S(2)}, u32[]{:S(2)}) async-start(bf16[16,16,128]{2,1,0:T(8,128)(2,1)} %get-tuple-element.98), calls=%async_computation | async-start | bytes 131072 | tf_op jit(solution)/shard_map/all_to_all | solution.py:536
  18.2 10.7 %collective-permute-start.2 = (bf16[256,1024]{1,0:T(8,128)(2,1)S(1)}, bf16[256,1024]{1,0:T(8,128)(2,1)S(1)}, u32[]{:S(2)}, u32[]{:S(2)}) collective-permute-start(bf16[256,1024]{1,0:T(8,128)(2,1)S(1)} %get-tuple-element.90), channel_id=1, source_target_pairs={{0,3},{1,2},{2,1},{3,0},{4,7},{5,6},{6,5},{7,4},{8,11},{9,10},{10,... | collective-permute-start | bytes 1572872 | tf_op jit(solution)/shard_map/ppermute | solution.py:57
  21.6 13.4 %collective-permute-start.5 = (bf16[128,1024]{1,0:T(8,128)(2,1)S(1)}, bf16[128,1024]{1,0:T(8,128)(2,1)S(1)}, u32[]{:S(2)}, u32[]{:S(2)}) collective-permute-start(bf16[128,1024]{1,0:T(8,128)(2,1)S(1)} %get-tuple-element.96), channel_id=1, source_target_pairs={{0,3},{1,2},{2,1},{3,0},{4,7},{5,6},{6,5},{7,4},{8,11},{9,10},{10,... | collective-permute-start | bytes 786440 | tf_op jit(solution)/shard_map/ppermute | solution.py:57
  21.7 12.3 %collective-permute-start.4 = (bf16[128,1024]{1,0:T(8,128)(2,1)S(1)}, bf16[128,1024]{1,0:T(8,128)(2,1)S(1)}, u32[]{:S(2)}, u32[]{:S(2)}) collective-permute-start(bf16[128,1024]{1,0:T(8,128)(2,1)S(1)} %get-tuple-element.94), channel_id=1, source_target_pairs={{0,1},{1,0},{2,3},{3,2},{4,5},{5,4},{6,7},{7,6},{8,9},{9,8},{10,11... | collective-permute-start | bytes 786440 | tf_op jit(solution)/shard_map/ppermute | solution.py:57
  22.5 11.3 %collective-permute-start.3 = (bf16[256,1024]{1,0:T(8,128)(2,1)S(1)}, bf16[256,1024]{1,0:T(8,128)(2,1)S(1)}, u32[]{:S(2)}, u32[]{:S(2)}) collective-permute-start(bf16[256,1024]{1,0:T(8,128)(2,1)S(1)} %get-tuple-element.92), channel_id=1, source_target_pairs={{0,1},{1,0},{2,3},{3,2},{4,5},{5,4},{6,7},{7,6},{8,9},{9,8},{10,11... | collective-permute-start | bytes 1572872 | tf_op jit(solution)/shard_map/ppermute | solution.py:57
  35.9 18.2 %collective-permute-start.7 = (bf16[256,1024]{1,0:T(8,128)(2,1)}, bf16[256,1024]{1,0:T(8,128)(2,1)}, u32[]{:S(2)}, u32[]{:S(2)}) collective-permute-start(bf16[256,1024]{1,0:T(8,128)(2,1)} %get-tuple-element.105), channel_id=1, source_target_pairs={{0,1},{1,0},{2,3},{3,2},{4,5},{5,4},{6,7},{7,6},{8,9},{9,8},{10,11... | collective-permute-start | bytes 1572872 | tf_op jit(solution)/shard_map/ppermute | solution.py:57
  36.6 16.2 %collective-permute-start.6 = (bf16[256,1024]{1,0:T(8,128)(2,1)}, bf16[256,1024]{1,0:T(8,128)(2,1)}, u32[]{:S(2)}, u32[]{:S(2)}) collective-permute-start(bf16[256,1024]{1,0:T(8,128)(2,1)} %get-tuple-element.103), channel_id=1, source_target_pairs={{0,3},{1,2},{2,1},{3,0},{4,7},{5,6},{6,5},{7,4},{8,11},{9,10},{10,... | collective-permute-start | bytes 1572872 | tf_op jit(solution)/shard_map/ppermute | solution.py:57
  39.1 22.5 %collective-permute-start.9 = (bf16[512,1024]{1,0:T(8,128)(2,1)S(1)}, bf16[512,1024]{1,0:T(8,128)(2,1)}, u32[]{:S(2)}, u32[]{:S(2)}) collective-permute-start(bf16[512,1024]{1,0:T(8,128)(2,1)S(1)} %get-tuple-element.110.refs_1_), channel_id=1, source_target_pairs={{0,12},{1,13},{2,14},{3,15},{4,8},{5,9},{6,10},{7,11},{8,4},{9,5},... | collective-permute-start | bytes 3145736 | tf_op jit(solution)/shard_map/ppermute | solution.py:57
  41.7 16.8 %collective-permute-start.8 = (bf16[512,1024]{1,0:T(8,128)(2,1)S(1)}, bf16[512,1024]{1,0:T(8,128)(2,1)}, u32[]{:S(2)}, u32[]{:S(2)}) collective-permute-start(bf16[512,1024]{1,0:T(8,128)(2,1)S(1)} %get-tuple-element.107.refs_1_), channel_id=1, source_target_pairs={{0,4},{1,5},{2,6},{3,7},{4,0},{5,1},{6,2},{7,3},{8,12},{9,13},{10,... | collective-permute-start | bytes 3145736 | tf_op jit(solution)/shard_map/ppermute | solution.py:57
  43.5 9.3 %copy-start.15 = (bf16[128,1024]{1,0:T(8,128)(2,1)S(1)}, bf16[128,1024]{1,0:T(8,128)(2,1)}, u32[]{:S(2)}) copy-start(bf16[128,1024]{1,0:T(8,128)(2,1)} %copy-done.14) | copy-start | bytes 786436
  45.0 47.5 %copy-start.22 = (bf16[8,2,96,640]{3,2,1,0:T(8,128)(2,1)}, bf16[8,2,96,640]{3,2,1,0:T(8,128)(2,1)S(1)}, u32[]{:S(2)}) copy-start(bf16[8,2,96,640]{3,2,1,0:T(8,128)(2,1)S(1)} %get-tuple-element.118.refs_3_.refs_2_) | copy-start | bytes 5898244
  55.4 19.8 %collective-permute-start.11 = (bf16[512,1024]{1,0:T(8,128)(2,1)S(1)}, bf16[512,1024]{1,0:T(8,128)(2,1)S(1)}, u32[]{:S(2)}, u32[]{:S(2)}) collective-permute-start(bf16[512,1024]{1,0:T(8,128)(2,1)S(1)} %get-tuple-element.114.refs_1_), channel_id=1, source_target_pairs={{0,12},{1,13},{2,14},{3,15},{4,8},{5,9},{6,10},{7,11},{8,4},{9,5},... | collective-permute-start | bytes 3145736 | tf_op jit(solution)/shard_map/ppermute | solution.py:57
  58.3 14.8 %collective-permute-start.10 = (bf16[512,1024]{1,0:T(8,128)(2,1)S(1)}, bf16[512,1024]{1,0:T(8,128)(2,1)S(1)}, u32[]{:S(2)}, u32[]{:S(2)}) collective-permute-start(bf16[512,1024]{1,0:T(8,128)(2,1)S(1)} %get-tuple-element.112.refs_1_), channel_id=1, source_target_pairs={{0,4},{1,5},{2,6},{3,7},{4,0},{5,1},{6,2},{7,3},{8,12},{9,13},{10,... | collective-permute-start | bytes 3145736 | tf_op jit(solution)/shard_map/ppermute | solution.py:57
  64.6 25.3 %collective-permute-start.13 = (bf16[2,320,1024]{2,1,0:T(8,128)(2,1)S(1)}, bf16[2,320,1024]{2,1,0:T(8,128)(2,1)S(1)}, u32[]{:S(2)}, u32[]{:S(2)}) collective-permute-start(bf16[2,320,1024]{2,1,0:T(8,128)(2,1)S(1)} %get-tuple-element.123), channel_id=1, source_target_pairs={{0,4},{1,5},{2,6},{3,7},{4,0},{5,1},{6,2},{7,3},{8,12},{9,13},{10,... | collective-permute-start | bytes 3932168 | tf_op jit(solution)/shard_map/ppermute | solution.py:57
  66.4 19.1 %collective-permute-start.12 = (bf16[2,320,1024]{2,1,0:T(8,128)(2,1)S(1)}, bf16[2,320,1024]{2,1,0:T(8,128)(2,1)S(1)}, u32[]{:S(2)}, u32[]{:S(2)}) collective-permute-start(bf16[2,320,1024]{2,1,0:T(8,128)(2,1)S(1)} %get-tuple-element.117), channel_id=1, source_target_pairs={{0,12},{1,13},{2,14},{3,15},{4,8},{5,9},{6,10},{7,11},{8,4},{9,5},... | collective-permute-start | bytes 3932168 | tf_op jit(solution)/shard_map/ppermute | solution.py:57
  78.0 22.1 %copy-start.20 = (bf16[2,320,1024]{2,1,0:T(8,128)(2,1)}, bf16[2,320,1024]{2,1,0:T(8,128)(2,1)S(1)}, u32[]{:S(2)}) copy-start(bf16[2,320,1024]{2,1,0:T(8,128)(2,1)S(1)} %get-tuple-element.134.refs_4_.refs_1_) | copy-start | bytes 3932164
  78.0 32.6 %collective-permute-start.17 = (bf16[2,320,1024]{2,1,0:T(8,128)(2,1)}, bf16[2,320,1024]{2,1,0:T(8,128)(2,1)}, u32[]{:S(2)}, u32[]{:S(2)}) collective-permute-start(bf16[2,320,1024]{2,1,0:T(8,128)(2,1)} %get-tuple-element.138), channel_id=1, source_target_pairs={{0,4},{1,5},{2,6},{3,7},{4,0},{5,1},{6,2},{7,3},{8,12},{9,13},{10,... | collective-permute-start | bytes 3932168 | tf_op jit(solution)/shard_map/ppermute | solution.py:57
  78.2 29.3 %collective-permute-start.16 = (bf16[2,320,1024]{2,1,0:T(8,128)(2,1)S(1)}, bf16[2,320,1024]{2,1,0:T(8,128)(2,1)S(1)}, u32[]{:S(2)}, u32[]{:S(2)}) collective-permute-start(bf16[2,320,1024]{2,1,0:T(8,128)(2,1)S(1)} %get-tuple-element.136), channel_id=1, source_target_pairs={{0,12},{1,13},{2,14},{3,15},{4,8},{5,9},{6,10},{7,11},{8,4},{9,5},... | collective-permute-start | bytes 3932168 | tf_op jit(solution)/shard_map/ppermute | solution.py:57
  87.7 6.7 %collective-permute-start.14 = (bf16[4,2,96,1024]{3,2,1,0:T(8,128)(2,1)S(1)}, bf16[4,2,96,1024]{3,2,1,0:T(8,128)(2,1)S(1)}, u32[]{:S(2)}, u32[]{:S(2)}) collective-permute-start(bf16[4,2,96,1024]{3,2,1,0:T(8,128)(2,1)S(1)} %get-tuple-element.128), channel_id=1, source_target_pairs={{0,16},{1,17},{2,18},{3,19},{4,20},{5,21},{6,22},{7,23},{8,24},{9,... | collective-permute-start | bytes 4718600 | tf_op jit(solution)/shard_map/ppermute | solution.py:57
  89.8 23.9 %copy-start.16 = (bf16[4,2,96,1024]{3,2,1,0:T(8,128)(2,1)}, bf16[4,2,96,1024]{3,2,1,0:T(8,128)(2,1)S(1)}, u32[]{:S(2)}) copy-start(bf16[4,2,96,1024]{3,2,1,0:T(8,128)(2,1)S(1)} %get-tuple-element.127.refs_1_.refs_3_) | copy-start | bytes 4718596
  92.0 4.9 %collective-permute-start.15 = (bf16[4,2,96,1024]{3,2,1,0:T(8,128)(2,1)S(1)}, bf16[4,2,96,1024]{3,2,1,0:T(8,128)(2,1)S(1)}, u32[]{:S(2)}, u32[]{:S(2)}) collective-permute-start(bf16[4,2,96,1024]{3,2,1,0:T(8,128)(2,1)S(1)} %get-tuple-element.131), channel_id=1, source_target_pairs={{0,16},{1,17},{2,18},{3,19},{4,20},{5,21},{6,22},{7,23},{8,24},{9,... | collective-permute-start | bytes 4718600 | tf_op jit(solution)/shard_map/ppermute | solution.py:57
  94.4 19.3 %copy-start.4 = (bf16[4,2,96,1024]{3,2,1,0:T(8,128)(2,1)}, bf16[4,2,96,1024]{3,2,1,0:T(8,128)(2,1)S(1)}, u32[]{:S(2)}) copy-start(bf16[4,2,96,1024]{3,2,1,0:T(8,128)(2,1)S(1)} %collective-permute-done.14.refs_2_.refs_4_) | copy-start | bytes 4718596
  94.4 5.7 %slice-start = ((s8[12582912]{0:T(1024)(128)(4,1)}), s8[4194304]{0:T(1024)(128)(4,1)S(1)}, s32[]{:S(2)}) async-start(s8[12582912]{0:T(1024)(128)(4,1)} %bitcast.11), calls=%async_computation.2 | async-start | bytes 8388608
  94.4 5.7 %slice-start.1 = ((s8[12582912]{0:T(1024)(128)(4,1)}), s8[4194304]{0:T(1024)(128)(4,1)S(1)}, s32[]{:S(2)}) async-start(s8[12582912]{0:T(1024)(128)(4,1)} %bitcast.11), calls=%async_computation.3 | async-start | bytes 8388608
  94.9 18.8 %collective-permute-start.18 = (bf16[2,2,96,1024]{3,2,1,0:T(8,128)(2,1)S(1)}, bf16[2,2,96,1024]{3,2,1,0:T(8,128)(2,1)S(1)}, u32[]{:S(2)}, u32[]{:S(2)}) collective-permute-start(bf16[2,2,96,1024]{3,2,1,0:T(8,128)(2,1)S(1)} %get-tuple-element.140), channel_id=1, source_target_pairs={{0,32},{1,33},{2,34},{3,35},{4,36},{5,37},{6,38},{7,39},{8,40},{9,... | collective-permute-start | bytes 2359304 | tf_op jit(solution)/shard_map/ppermute | solution.py:57
  97.3 19.5 %collective-permute-start.19 = (bf16[2,2,96,1024]{3,2,1,0:T(8,128)(2,1)S(1)}, bf16[2,2,96,1024]{3,2,1,0:T(8,128)(2,1)S(1)}, u32[]{:S(2)}, u32[]{:S(2)}) collective-permute-start(bf16[2,2,96,1024]{3,2,1,0:T(8,128)(2,1)S(1)} %get-tuple-element.142), channel_id=1, source_target_pairs={{0,96},{1,97},{2,98},{3,99},{4,100},{5,101},{6,102},{7,103},{8,104... | collective-permute-start | bytes 2359304 | tf_op jit(solution)/shard_map/ppermute | solution.py:57
  100.1 7.5 %copy-start.23 = (bf16[8,2,96,640]{3,2,1,0:T(8,128)(2,1)S(1)}, bf16[8,2,96,640]{3,2,1,0:T(8,128)(2,1)}, u32[]{:S(2)}) copy-start(bf16[8,2,96,640]{3,2,1,0:T(8,128)(2,1)} %copy-done.22) | copy-start | bytes 5898244
  109.7 14.7 %collective-permute-start.20 = (bf16[4,2,96,1024]{3,2,1,0:T(8,128)(2,1)S(1)}, bf16[4,2,96,1024]{3,2,1,0:T(8,128)(2,1)S(1)}, u32[]{:S(2)}, u32[]{:S(2)}) collective-permute-start(bf16[4,2,96,1024]{3,2,1,0:T(8,128)(2,1)S(1)} %get-tuple-element.149), channel_id=1, source_target_pairs={{0,16},{1,17},{2,18},{3,19},{4,20},{5,21},{6,22},{7,23},{8,24},{9,... | collective-permute-start | bytes 4718600 | tf_op jit(solution)/shard_map/ppermute | solution.py:57
  113.6 12.4 %collective-permute-start.21 = (bf16[4,2,96,1024]{3,2,1,0:T(8,128)(2,1)S(1)}, bf16[4,2,96,1024]{3,2,1,0:T(8,128)(2,1)S(1)}, u32[]{:S(2)}, u32[]{:S(2)}) collective-permute-start(bf16[4,2,96,1024]{3,2,1,0:T(8,128)(2,1)S(1)} %get-tuple-element.152), channel_id=1, source_target_pairs={{0,16},{1,17},{2,18},{3,19},{4,20},{5,21},{6,22},{7,23},{8,24},{9,... | collective-permute-start | bytes 4718600 | tf_op jit(solution)/shard_map/ppermute | solution.py:57
  117.0 46.3 %collective-permute-start.25 = (bf16[1,2,96,1024]{3,2,1,0:T(8,128)(2,1)S(1)}, bf16[1,2,96,1024]{3,2,1,0:T(8,128)(2,1)S(1)}, u32[]{:S(2)}, u32[]{:S(2)}) collective-permute-start(bf16[1,2,96,1024]{3,2,1,0:T(8,128)(2,1)S(1)} %get-tuple-element.162), channel_id=1, source_target_pairs={{0,32},{1,33},{2,34},{3,35},{4,36},{5,37},{6,38},{7,39},{8,40},{9,... | collective-permute-start | bytes 1179656 | tf_op jit(solution)/shard_map/ppermute | solution.py:57
  117.1 46.2 %collective-permute-start.24 = (bf16[1,2,96,1024]{3,2,1,0:T(8,128)(2,1)S(1)}, bf16[1,2,96,1024]{3,2,1,0:T(8,128)(2,1)S(1)}, u32[]{:S(2)}, u32[]{:S(2)}) collective-permute-start(bf16[1,2,96,1024]{3,2,1,0:T(8,128)(2,1)S(1)} %get-tuple-element.161), channel_id=1, source_target_pairs={{0,96},{1,97},{2,98},{3,99},{4,100},{5,101},{6,102},{7,103},{8,104... | collective-permute-start | bytes 1179656 | tf_op jit(solution)/shard_map/ppermute | solution.py:57
  122.5 22.9 %copy-start.18 = (bf16[4,2,96,1024]{3,2,1,0:T(8,128)(2,1)}, bf16[4,2,96,1024]{3,2,1,0:T(8,128)(2,1)S(1)}, u32[]{:S(2)}) copy-start(bf16[4,2,96,1024]{3,2,1,0:T(8,128)(2,1)S(1)} %get-tuple-element.148.refs_1_.refs_3_.refs_9_) | copy-start | bytes 4718596
  124.8 20.6 %collective-permute-start.22 = (bf16[2,2,96,1024]{3,2,1,0:T(8,128)(2,1)S(1)}, bf16[2,2,96,1024]{3,2,1,0:T(8,128)(2,1)S(1)}, u32[]{:S(2)}, u32[]{:S(2)}) collective-permute-start(bf16[2,2,96,1024]{3,2,1,0:T(8,128)(2,1)S(1)} %get-tuple-element.157), channel_id=1, source_target_pairs={{0,32},{1,33},{2,34},{3,35},{4,36},{5,37},{6,38},{7,39},{8,40},{9,... | collective-permute-start | bytes 2359304 | tf_op jit(solution)/shard_map/ppermute | solution.py:57
  125.9 4.2 %copy-start.7 = (bf16[2,320,1024]{2,1,0:T(8,128)(2,1)S(1)}, bf16[2,320,1024]{2,1,0:T(8,128)(2,1)}, u32[]{:S(2)}) copy-start(bf16[2,320,1024]{2,1,0:T(8,128)(2,1)} %copy-done.6) | copy-start | bytes 3932164
  125.9 4.6 %copy-start.9 = (bf16[2,320,1024]{2,1,0:T(8,128)(2,1)S(1)}, bf16[2,320,1024]{2,1,0:T(8,128)(2,1)}, u32[]{:S(2)}) copy-start(bf16[2,320,1024]{2,1,0:T(8,128)(2,1)} %copy-done.8) | copy-start | bytes 3932164
  125.9 4.6 %copy-start.25 = (f32[32,128]{1,0:T(8,128)S(1)}, f32[32,128]{1,0:T(8,128)}, u32[]{:S(2)}) copy-start(f32[32,128]{1,0:T(8,128)} %copy-done.24) | copy-start | bytes 49156
  126.0 4.6 %copy-start.27 = (f32[32,128]{1,0:T(8,128)S(1)}, f32[32,128]{1,0:T(8,128)}, u32[]{:S(2)}) copy-start(f32[32,128]{1,0:T(8,128)} %copy-done.26) | copy-start | bytes 49156
  126.4 21.9 %collective-permute-start.23 = (bf16[2,2,96,1024]{3,2,1,0:T(8,128)(2,1)S(1)}, bf16[2,2,96,1024]{3,2,1,0:T(8,128)(2,1)S(1)}, u32[]{:S(2)}, u32[]{:S(2)}) collective-permute-start(bf16[2,2,96,1024]{3,2,1,0:T(8,128)(2,1)S(1)} %get-tuple-element.159), channel_id=1, source_target_pairs={{0,96},{1,97},{2,98},{3,99},{4,100},{5,101},{6,102},{7,103},{8,104... | collective-permute-start | bytes 2359304 | tf_op jit(solution)/shard_map/ppermute | solution.py:57
  145.7 17.6 %collective-permute-start.26 = (bf16[1,2,96,1024]{3,2,1,0:T(8,128)(2,1)S(1)}, bf16[1,2,96,1024]{3,2,1,0:T(8,128)(2,1)S(1)}, u32[]{:S(2)}, u32[]{:S(2)}) collective-permute-start(bf16[1,2,96,1024]{3,2,1,0:T(8,128)(2,1)S(1)} %get-tuple-element.163), channel_id=1, source_target_pairs={{0,96},{1,97},{2,98},{3,99},{4,100},{5,101},{6,102},{7,103},{8,104... | collective-permute-start | bytes 1179656 | tf_op jit(solution)/shard_map/ppermute | solution.py:57
  148.2 14.4 %copy-start.28 = (s32[128,8]{0,1:T(8,128)S(1)}, s32[128,8]{0,1:T(8,128)}, u32[]{:S(2)}) copy-start(s32[128,8]{0,1:T(8,128)} %param.7) | copy-start | bytes 12292
  148.2 15.1 %copy-start.5 = (bf16[4,2,96,1024]{3,2,1,0:T(8,128)(2,1)S(1)}, bf16[4,2,96,1024]{3,2,1,0:T(8,128)(2,1)}, u32[]{:S(2)}) copy-start(bf16[4,2,96,1024]{3,2,1,0:T(8,128)(2,1)} %copy-done.4) | copy-start | bytes 4718596
  148.3 15.1 %copy-start.11 = (bf16[2,2,96,1024]{3,2,1,0:T(8,128)(2,1)S(1)}, bf16[2,2,96,1024]{3,2,1,0:T(8,128)(2,1)}, u32[]{:S(2)}) copy-start(bf16[2,2,96,1024]{3,2,1,0:T(8,128)(2,1)} %copy-done.10) | copy-start | bytes 2359300
  148.3 15.1 %copy-start.17 = (bf16[4,2,96,1024]{3,2,1,0:T(8,128)(2,1)S(1)}, bf16[4,2,96,1024]{3,2,1,0:T(8,128)(2,1)}, u32[]{:S(2)}) copy-start(bf16[4,2,96,1024]{3,2,1,0:T(8,128)(2,1)} %copy-done.16) | copy-start | bytes 4718596
  148.3 15.1 %copy-start.19 = (bf16[4,2,96,1024]{3,2,1,0:T(8,128)(2,1)S(1)}, bf16[4,2,96,1024]{3,2,1,0:T(8,128)(2,1)}, u32[]{:S(2)}) copy-start(bf16[4,2,96,1024]{3,2,1,0:T(8,128)(2,1)} %copy-done.18) | copy-start | bytes 4718596
  148.6 14.7 %collective-permute-start.27 = (bf16[1,2,96,1024]{3,2,1,0:T(8,128)(2,1)S(1)}, bf16[1,2,96,1024]{3,2,1,0:T(8,128)(2,1)S(1)}, u32[]{:S(2)}, u32[]{:S(2)}) collective-permute-start(bf16[1,2,96,1024]{3,2,1,0:T(8,128)(2,1)S(1)} %get-tuple-element.164), channel_id=1, source_target_pairs={{0,32},{1,33},{2,34},{3,35},{4,36},{5,37},{6,38},{7,39},{8,40},{9,... | collective-permute-start | bytes 1179656 | tf_op jit(solution)/shard_map/ppermute | solution.py:57
  (16 other events, 34.9 us)

commit v2 on v1

--- a/solution.py
+++ b/solution.py
@@ -10,11 +10,10 @@
 TILE = 512
 DEEP = 1024
 VMEM_LIMIT = 20 * 1024 * 1024
-COSTS = {"o": 20, "a": 20, "r": 20, "I": 20, "P": 20, "T": 20, "p": 20, "w": 20, "m": 20, "s": 20, "t": 20, "e": 20, "h": 20, "H": 20}
 PLAN = (
-    "a0", "a1", "I", "o2", "o3", "r0", "r1", "a2", "a3", "P", "T", "r2", "r3", "p0", "p1", "p2",
-    "p3", "w0", "m0", "w1", "m1", "s0", "s1", "h", "w2", "w3", "t0", "t1", "m2", "m3", "s2",
-    "s3", "H", "t2", "t3", "e",
+    "a0", "a1", "o2", "o3-", "r0-", "r1", "a2", "a3", "I-", "P-", "T-", "r2", "r3", "p0", "p1",
+    "h0", "p2", "p3", "h1", "w0", "m0", "w1", "m1", "s0", "s1", "w2", "w3", "m2", "m3", "s2",
+    "s3", "H", "t0-", "t1-", "t2-", "t3-", "e",
 )
 F32, BF16 = jnp.float32, jnp.bfloat16
 
@@ -352,7 +351,7 @@
 
 def finish(parts, width):
     _, held, block, _ = parts[0][0].shape
-    counts = [group[0].shape[3] // TILE for group in parts]
+    counts = [group[0].shape[3] // DEEP for group in parts]
     starts = [sum(counts[:n]) for n in range(len(counts))]
     terms = len(parts[0])
 
@@ -369,20 +368,20 @@
 
     def spec(start, count):
         return pl.BlockSpec(
-            (1, held, block, TILE),
+            (1, held, block, DEEP),
             lambda i: (0, 0, 0, jnp.minimum(jnp.maximum(i - start, 0), count - 1)),
         )
 
     shape = (held, block, width)
     return call(
         kernel,
-        (width // TILE,),
+        (width // DEEP,),
         [(part, spec(a, c)) for group, a, c in zip(parts, starts, counts) for part in group],
-        [(out(*shape), columns(shape))],
-    )[0]
-
-
-def chunk_specs(halves, ff):
+        [(out(*shape), pl.BlockSpec((held, block, DEEP), lambda i: (0, 0, i)))],
+    )[0]
+
+
+def chunk_specs(halves, offset, ff):
     rows = halves[0].shape[1]
     counts = [h.shape[2] // DEEP for h in halves]
     starts = [sum(counts[:n]) for n in range(len(halves))]
@@ -393,7 +392,7 @@
         )
 
     specs = [spec(a, b) for a, b in zip(starts, counts)]
-    return counts, starts, specs, pl.BlockSpec((1, ff, DEEP), lambda e, i: (e, 0, i))
+    return counts, starts, specs, pl.BlockSpec((1, ff, DEEP), lambda e, i: (e, 0, i + offset // DEEP))
 
 
 def add_chunks(refs, starts, counts, lines, w_ref, sum_ref):
@@ -412,10 +411,10 @@
 CAME = ((2, 3), (1, 3))
 
 
-def hidden_sums(halves, w_down):
+def hidden_sums(halves, offset, w_down):
     held, rows, _ = halves[0].shape
     ff, total = w_down.shape[1], 2 * rows
-    counts, starts, specs, w_spec = chunk_specs(halves, ff)
+    counts, starts, specs, w_spec = chunk_specs(halves, offset, ff)
 
     def kernel(*refs):
         w_ref, sum_ref, acc_ref = refs[len(halves) :]
@@ -441,16 +440,17 @@
 
 def hidden_end(at, key, gate, hidden, sums, halves, w_down):
     held, sources, cap, ff = hidden.shape
-    total = sums.shape[1]
+    total = sums[0].shape[1]
     tokens = key.shape[1]
-    counts, starts, specs, w_spec = chunk_specs(halves, ff)
-
-    def kernel(at_ref, key_ref, gate_ref, hidden_ref, sums_ref, *refs):
+    counts, starts, specs, w_spec = chunk_specs(halves, 0, ff)
+
+    def kernel(at_ref, key_ref, gate_ref, hidden_ref, *refs):
+        sums_refs, refs = refs[: len(sums)], refs[len(sums) :]
         w_ref, d_hidden_ref, grad_ref, acc_ref = refs[len(halves) :]
 
         @pl.when(pl.program_id(1) == 0)
         def _():
-            acc_ref[...] = sums_ref[0]
+            acc_ref[...] = sum(ref[0] for ref in sums_refs)
 
         add_chunks(refs, starts, counts, CAME, w_ref, acc_ref)
 
@@ -484,8 +484,8 @@
             (key, whole(key.shape)),
             (gate, whole(gate.shape)),
             (hidden, by_expert),
-            (sums, pl.BlockSpec((1, total, ff), lambda e, i: (e, 0, 0))),
         ]
+        + [(part, pl.BlockSpec((1, total, ff), lambda e, i: (e, 0, 0))) for part in sums]
         + list(zip(halves, specs))
         + [(w_down, w_spec)],
         [
@@ -521,15 +521,16 @@
     info = jnp.concatenate([routes.astype(F32), gate_values.astype(F32)], axis=1).T
     count = len(CHUNKS)
     one, two, rows, far, here, came, slots = ([None] * count for _ in range(7))
+    hidden_parts = [None] * (count // 2)
     got, mine, passed, more = ([None] * count for _ in range(4))
     for n in range(2):
         own = d_output[:, offsets[n] : offsets[n] + CHUNKS[n]]
         one[n] = send(own, along("first", 0, n % 2))
 
     for step in PLAN:
-        kind, n = step[0], int(step[1:] or 0)
+        kind, n = step[0], int(step[1:2].strip("-") or 0)
         parity = n % 2
-        ORDER.cost = COSTS[kind]
+        ORDER.cost = 0 if step.endswith("-") else 20
         if kind == "o":
             one[n] = send(own_rows(d_output, offsets[n], CHUNKS[n]), along("first", 0, parity))
         elif kind == "I":
@@ -564,9 +565,9 @@
             parts = [(mine[k], got[k], passed[k], more[k]) for k in range(count)]
             d_weight = finish(parts, width)
         elif kind == "h":
-            hidden_part = hidden_sums(here, w_down)
+            hidden_parts[n] = hidden_sums(here[2 * n : 2 * n + 2], offsets[2 * n], w_down)
         elif kind == "H":
-            d_hidden, token_grad = hidden_end(at, key, gate, hidden, hidden_part, came, w_down)
+            d_hidden, token_grad = hidden_end(at, key, gate, hidden, hidden_parts, came, w_down)
     returned = lax.all_to_all(token_grad, "expert", 0, 0, tiled=True).reshape(-1, tokens)
     chosen = routes.T[None] == jnp.arange(sources * held)[:, None, None]
     d_gate = jnp.sum(jnp.where(chosen, returned[:, None, :], 0.0), axis=0).T

time: 168 us -> 155 us (0.923)
  waiting for transfers between devices: 41.1 us -> 22.8 us
  local copies, waits for them, and re-layouts: 6.88 us -> 11.4 us
  Pallas kernels: 60.8 us -> 62.5 us
    ppermute x28, waiting for transfers between devices: 41.1 us -> 19.7 us  [send(): return lax.ppermute(value, AXES, pairs)]
    unnamed x70 -> x62, local copies, waits for them, and re-layouts: 5.64 us -> 10.2 us
    all_to_all x1, waiting for transfers between devices: 0.01 us -> 3.11 us  [shards(): all_info = lax.all_to_all(share(info, sources), 'expert', 0, 0, tiled=True)]
    ppermute x28, starting transfers between devices: 36.2 us -> 34.4 us  [send(): return lax.ppermute(value, AXES, pairs)]
    pallas_call x36 -> x37, Pallas kernels: 60.8 us -> 62.5 us  [call(): pl.pallas_call(run, grid=grid, in_specs=[pl.BlockSpec(memory_space=pltpu....]
  transfers between devices with their start and end apart: 29 -> 29, of which waited for: 8 -> 7; matrix products, arithmetic and copies ran while one was open for 1% -> 2% of each run, Pallas kernels for 33% -> 38%
where the time goes in v2:
time: 155 us
  Pallas kernels  62.5 us (40%)
  starting transfers between devices  40.5 us (26%)
  waiting for transfers between devices  22.8 us (15%)
  blocking collectives  13.9 us (9%)
  local copies, waits for them, and re-layouts  11.4 us (7%)
  other arithmetic  2.32 us (1%)
    pallas_call x37, Pallas kernels, call(): pl.pallas_call(run, grid=grid, in_specs=[pl.BlockSpec(memory_space=pltpu....  62.5 us
    ppermute x28, starting transfers between devices, send(): return lax.ppermute(value, AXES, pairs)  34.4 us
    ppermute x28, waiting for transfers between devices, send(): return lax.ppermute(value, AXES, pairs)  19.7 us
    all_to_all x1, blocking collectives, shards(): lax.all_to_all(token_grad, 'expert', 0, 0, tiled=True).reshape(-1, tokens)  13.9 us
    unnamed x62, local copies, waits for them, and re-layouts  10.2 us
    all_to_all x1, starting transfers between devices, shards(): all_info = lax.all_to_all(share(info, sources), 'expert', 0, 0, tiled=True)  6.11 us
    all_to_all x1, waiting for transfers between devices, shards(): all_info = lax.all_to_all(share(info, sources), 'expert', 0, 0, tiled=True)  3.11 us
  transfers between devices with their start and end apart: 29, of which 7 were waited for; matrix products, arithmetic and copies ran while one was open for 2% of the time, Pallas kernels for 38%

profile of v2, /device:TPU:0, one launch (start us, length us, event | category | flops | bytes accessed | tf_op | source)
XLA Modules:
  0.0 154.7 jit_solution(10068778343062254925)
XLA Ops:
  1.7 2.9 %collective-permute-start.1 = (bf16[128,1024]{1,0:T(8,128)(2,1)S(1)}, bf16[128,1024]{1,0:T(8,128)(2,1)S(1)}, u32[]{:S(2)}, u32[]{:S(2)}) collective-permute-start(bf16[128,1024]{1,0:T(8,128)(2,1)S(1)} %get-tuple-element.176), channel_id=1, source_target_pairs={{0,3},{1,2},{2,1},{3,0},{4,7},{5,6},{6,5},{7,4},{8,11},{9,10},{10,... | collective-permute-start | bytes 786440 | tf_op jit(solution)/shard_map/ppermute | solution.py:56
  6.7 4.3 %collective-permute-done.refs_1_.refs_2_ = bf16[128,1024]{1,0:T(8,128)(2,1)S(1)} collective-permute-done((bf16[128,1024]{1,0:T(8,128)(2,1)S(1)}, bf16[128,1024]{1,0:T(8,128)(2,1)S(1)}, u32[]{:S(2)}, u32[]{:S(2)}) %collective-permute-start) | collective-permute-done | bytes 262176 | tf_op jit(solution)/shard_map/ppermute | solution.py:56
  11.0 1.2 copy-done
  12.9 1.1 collective-permute-start.2
  14.3 2.2 %collective-permute-start.5 = (bf16[128,1024]{1,0:T(8,128)(2,1)S(1)}, bf16[128,1024]{1,0:T(8,128)(2,1)S(1)}, u32[]{:S(2)}, u32[]{:S(2)}) collective-permute-start(bf16[128,1024]{1,0:T(8,128)(2,1)S(1)} %get-tuple-element.97), channel_id=1, source_target_pairs={{0,3},{1,2},{2,1},{3,0},{4,7},{5,6},{6,5},{7,4},{8,11},{9,10},{10,... | collective-permute-start | bytes 786440 | tf_op jit(solution)/shard_map/ppermute | solution.py:56
  17.1 6.2 %collective-permute-done.2.refs_3_.refs_4_ = bf16[256,1024]{1,0:T(8,128)(2,1)S(1)} collective-permute-done((bf16[256,1024]{1,0:T(8,128)(2,1)S(1)}, bf16[256,1024]{1,0:T(8,128)(2,1)S(1)}, u32[]{:S(2)}, u32[]{:S(2)}) %collective-permute-start.2) | collective-permute-done | bytes 524320 | tf_op jit(solution)/shard_map/ppermute | solution.py:56
  26.7 1.1 collective-permute-start.6
  29.5 6.1 %all-to-all-start = ((bf16[16,16,128]{2,1,0:T(8,128)(2,1)}), bf16[16,16,128]{2,1,0:T(8,128)(2,1)S(1)}, u32[]{:S(2)}, u32[]{:S(2)}) async-start(bf16[16,16,128]{2,1,0:T(8,128)(2,1)} %get-tuple-element.100), calls=%async_computation | async-start | bytes 131072 | tf_op jit(solution)/shard_map/all_to_all | solution.py:537
  35.7 1.9 %collective-permute-start.7 = (bf16[256,1024]{1,0:T(8,128)(2,1)}, bf16[256,1024]{1,0:T(8,128)(2,1)}, u32[]{:S(2)}, u32[]{:S(2)}) collective-permute-start(bf16[256,1024]{1,0:T(8,128)(2,1)} %copy-done.24), channel_id=1, source_target_pairs={{0,1},{1,0},{2,3},{3,2},{4,5},{5,4},{6,7},{7,6},{8,9},{9,8},{10,11... | collective-permute-start | bytes 1572872 | tf_op jit(solution)/shard_map/ppermute | solution.py:56
  37.6 2.7 %collective-permute-start.9 = (bf16[512,1024]{1,0:T(8,128)(2,1)}, bf16[512,1024]{1,0:T(8,128)(2,1)}, u32[]{:S(2)}, u32[]{:S(2)}) collective-permute-start(bf16[512,1024]{1,0:T(8,128)(2,1)} %copy-done.22), channel_id=1, source_target_pairs={{0,12},{1,13},{2,14},{3,15},{4,8},{5,9},{6,10},{7,11},{8,4},{9,5},... | collective-permute-start | bytes 3145736 | tf_op jit(solution)/shard_map/ppermute | solution.py:56
  40.6 3.1 %all-to-all-done.refs_2_ = bf16[16,16,128]{2,1,0:T(8,128)(2,1)S(1)} async-done(((bf16[16,16,128]{2,1,0:T(8,128)(2,1)}), bf16[16,16,128]{2,1,0:T(8,128)(2,1)S(1)}, u32[]{:S(2)}, u32[]{:S(2)}) %all-to-all-start) | async-done | bytes 65568 | tf_op jit(solution)/shard_map/all_to_all | solution.py:537
  44.7 1.5 shard_map.86
  46.3 1.9 %shard_map.87 = (bf16[512,1024]{1,0:T(8,128)(2,1)S(1)}, f32[8,128]{1,0:T(8,128)S(1)}) custom-call(f32[8,128]{1,0:T(8,128)S(1)} %get-tuple-element.104.refs_0_, bf16[128,4096]{1,0:T(8,128)(2,1)S(1)} %copy-done.1, bf16[128,1024]{1,0:T(8,128)(2,1)S(1)} %copy-done.26, bf16[256,1024]{1,0:T(8,128)(2,1)} %collective-permute-done.6.refs_3_.refs_4_, ...), custom_call_target="tpu_custom_call" | custom-call | flops 20000000000 | tf_op jit(solution)/shard_map/pallas_call | solution.py:77
  48.1 3.2 %collective-permute-done.7.refs_2_.refs_4_ = bf16[256,1024]{1,0:T(8,128)(2,1)} collective-permute-done((bf16[256,1024]{1,0:T(8,128)(2,1)}, bf16[256,1024]{1,0:T(8,128)(2,1)}, u32[]{:S(2)}, u32[]{:S(2)}) %collective-permute-start.7) | collective-permute-done | bytes 524320 | tf_op jit(solution)/shard_map/ppermute | solution.py:56
  51.3 1.3 shard_map.88
  52.6 2.8 %collective-permute-start.11 = (bf16[512,1024]{1,0:T(8,128)(2,1)S(1)}, bf16[512,1024]{1,0:T(8,128)(2,1)S(1)}, u32[]{:S(2)}, u32[]{:S(2)}) collective-permute-start(bf16[512,1024]{1,0:T(8,128)(2,1)S(1)} %get-tuple-element.119.refs_1_), channel_id=1, source_target_pairs={{0,12},{1,13},{2,14},{3,15},{4,8},{5,9},{6,10},{7,11},{8,4},{9,5},... | collective-permute-start | bytes 3145736 | tf_op jit(solution)/shard_map/ppermute | solution.py:56
  55.7 3.1 %shard_map.89 = (bf16[2,320,1024]{2,1,0:T(8,128)(2,1)S(1)}, bf16[2,320,1024]{2,1,0:T(8,128)(2,1)S(1)}, f32[8,128]{1,0:T(8,128)S(1)}) custom-call(f32[8,128]{1,0:T(8,128)S(1)} %get-tuple-element.108.refs_0_, bf16[512,1024]{1,0:T(8,128)(2,1)S(1)} %copy-done.21, bf16[512,1024]{1,0:T(8,128)(2,1)} %collective-permute-done.8.refs_2_, ...), custom_call_target="tpu_custom_call" | custom-call | flops 20000000000 | tf_op jit(solution)/shard_map/pallas_call | solution.py:77
  58.9 3.1 %shard_map.90 = (bf16[2,320,1024]{2,1,0:T(8,128)(2,1)S(1)}, bf16[2,320,1024]{2,1,0:T(8,128)(2,1)S(1)}, f32[8,128]{1,0:T(8,128)S(1)}) custom-call(f32[8,128]{1,0:T(8,128)S(1)} %get-tuple-element.111.refs_0_, bf16[512,1024]{1,0:T(8,128)(2,1)S(1)} %copy-done.23, bf16[512,1024]{1,0:T(8,128)(2,1)} %collective-permute-done.9.refs_2_, ...), custom_call_target="tpu_custom_call" | custom-call | flops 20000000000 | tf_op jit(solution)/shard_map/pallas_call | solution.py:77
  62.0 1.9 %collective-permute-start.13 = (bf16[2,320,1024]{2,1,0:T(8,128)(2,1)S(1)}, bf16[2,320,1024]{2,1,0:T(8,128)(2,1)S(1)}, u32[]{:S(2)}, u32[]{:S(2)}) collective-permute-start(bf16[2,320,1024]{2,1,0:T(8,128)(2,1)S(1)} %get-tuple-element.129), channel_id=1, source_target_pairs={{0,4},{1,5},{2,6},{3,7},{4,0},{5,1},{6,2},{7,3},{8,12},{9,13},{10,... | collective-permute-start | bytes 3932168 | tf_op jit(solution)/shard_map/ppermute | solution.py:56
  64.4 3.9 %shard_map.91 = (f32[2,640,768]{2,1,0:T(8,128)S(1)}, f32[8,128]{1,0:T(8,128)S(1)}) custom-call(f32[8,128]{1,0:T(8,128)S(1)} %get-tuple-element.113.refs_0_, bf16[2,320,1024]{2,1,0:T(8,128)(2,1)S(1)} %get-tuple-element.114.refs_1_, bf16[2,320,1024]{2,1,0:T(8,128)(2,1)S(1)} %get-tuple-element.115.refs_2_.refs_1_, bf16[2,768,4096]{2,1,0:T(8,128)(2,1)S(1)} %bitcast.14), custom_call_target="tpu_custom_call" | custom-call | flops 20000000000 | tf_op jit(solution)/shard_map/pallas_call | solution.py:77
  68.3 1.9 %collective-permute-done.10.refs_2_ = bf16[512,1024]{1,0:T(8,128)(2,1)S(1)} collective-permute-done((bf16[512,1024]{1,0:T(8,128)(2,1)S(1)}, bf16[512,1024]{1,0:T(8,128)(2,1)S(1)}, u32[]{:S(2)}, u32[]{:S(2)}) %collective-permute-start.10) | collective-permute-done | bytes 1048608 | tf_op jit(solution)/shard_map/ppermute | solution.py:56
  70.3 2.0 %shard_map.92 = (bf16[2,320,1024]{2,1,0:T(8,128)(2,1)S(1)}, bf16[2,320,1024]{2,1,0:T(8,128)(2,1)S(1)}, f32[8,128]{1,0:T(8,128)S(1)}) custom-call(f32[8,128]{1,0:T(8,128)S(1)} %get-tuple-element.116.refs_0_, bf16[512,1024]{1,0:T(8,128)(2,1)S(1)} %get-tuple-element.117.refs_1_, bf16[512,1024]{1,0:T(8,128)(2,1)S(1)} %collective-permute-done.10.refs_2_, ...), custom_call_target="tpu_custom_call" | custom-call | flops 20000000000 | tf_op jit(solution)/shard_map/pallas_call | solution.py:77
  72.3 2.8 %shard_map.93 = (bf16[2,320,1024]{2,1,0:T(8,128)(2,1)S(1)}, bf16[2,320,1024]{2,1,0:T(8,128)(2,1)}, f32[8,128]{1,0:T(8,128)S(1)}) custom-call(f32[8,128]{1,0:T(8,128)S(1)} %get-tuple-element.118.refs_0_, bf16[512,1024]{1,0:T(8,128)(2,1)S(1)} %get-tuple-element.119.refs_1_, bf16[512,1024]{1,0:T(8,128)(2,1)S(1)} %collective-permute-done.11.refs_2_, ...), custom_call_target="tpu_custom_call" | custom-call | flops 20000000000 | tf_op jit(solution)/shard_map/pallas_call | solution.py:77
  75.4 1.2 collective-permute-start.16
  76.6 3.9 %shard_map.94 = (f32[2,640,768]{2,1,0:T(8,128)S(1)}, f32[8,128]{1,0:T(8,128)S(1)}) custom-call(f32[8,128]{1,0:T(8,128)S(1)} %get-tuple-element.120.refs_0_, bf16[2,320,1024]{2,1,0:T(8,128)(2,1)S(1)} %get-tuple-element.121.refs_1_, bf16[2,320,1024]{2,1,0:T(8,128)(2,1)S(1)} %get-tuple-element.122.refs_2_.refs_1_, bf16[2,768,4096]{2,1,0:T(8,128)(2,1)S(1)} %bitcast.14), custom_call_target="tpu_custom_call" | custom-call | flops 20000000000 | tf_op jit(solution)/shard_map/pallas_call | solution.py:77
  80.5 2.2 %collective-permute-done.12.refs_2_.refs_7_ = bf16[2,320,1024]{2,1,0:T(8,128)(2,1)S(1)} collective-permute-done((bf16[2,320,1024]{2,1,0:T(8,128)(2,1)S(1)}, bf16[2,320,1024]{2,1,0:T(8,128)(2,1)S(1)}, u32[]{:S(2)}, u32[]{:S(2)}) %collective-permute-start.12) | collective-permute-done | bytes 1310752 | tf_op jit(solution)/shard_map/ppermute | solution.py:56
  82.7 2.1 %shard_map.95 = (bf16[2,640,1024]{2,1,0:T(8,128)(2,1)S(1)}, bf16[4,2,96,1024]{3,2,1,0:T(8,128)(2,1)S(1)}, f32[8,128]{1,0:T(8,128)S(1)}) custom-call(f32[8,128]{1,0:T(8,128)S(1)} %get-tuple-element.123.refs_0_, bf16[2,320,1024]{2,1,0:T(8,128)(2,1)S(1)} %get-tuple-element.114.refs_1_, bf16[2,320,1024]{2,1,0:T(8,128)(2,1)S(1)} %collective-permute-done.12.refs_2_.refs_7_, ...), custom_call_target="tpu_custom_call" | custom-call | flops 20000000000 | tf_op jit(solution)/shard_map/pallas_call | solution.py:77
  84.9 1.9 %shard_map.96 = (bf16[4,2,96,1024]{3,2,1,0:T(8,128)(2,1)S(1)}, f32[8,128]{1,0:T(8,128)S(1)}) custom-call(f32[8,128]{1,0:T(8,128)S(1)} %get-tuple-element.126.refs_0_, bf16[2,640,1024]{2,1,0:T(8,128)(2,1)S(1)} %get-tuple-element.127.refs_1_, bf16[8,2,96,640]{3,2,1,0:T(8,128)(2,1)S(1)} %get-tuple-element.125.refs_3_.refs_2_), custom_call_target="tpu_custom_call" | custom-call | flops 20000000000 | tf_op jit(solution)/shard_map/pallas_call | solution.py:77
  86.8 2.1 %shard_map.97 = (bf16[2,640,1024]{2,1,0:T(8,128)(2,1)S(1)}, bf16[4,2,96,1024]{3,2,1,0:T(8,128)(2,1)S(1)}, f32[8,128]{1,0:T(8,128)S(1)}) custom-call(f32[8,128]{1,0:T(8,128)S(1)} %get-tuple-element.128.refs_0_, bf16[2,320,1024]{2,1,0:T(8,128)(2,1)S(1)} %get-tuple-element.115.refs_2_.refs_1_, ...), custom_call_target="tpu_custom_call" | custom-call | flops 20000000000 | tf_op jit(solution)/shard_map/pallas_call | solution.py:77
  89.5 1.9 %shard_map.98 = (bf16[4,2,96,1024]{3,2,1,0:T(8,128)(2,1)S(1)}, f32[8,128]{1,0:T(8,128)S(1)}) custom-call(f32[8,128]{1,0:T(8,128)S(1)} %get-tuple-element.130.refs_0_, bf16[2,640,1024]{2,1,0:T(8,128)(2,1)S(1)} %get-tuple-element.131.refs_1_, bf16[8,2,96,640]{3,2,1,0:T(8,128)(2,1)S(1)} %get-tuple-element.125.refs_3_.refs_2_), custom_call_target="tpu_custom_call" | custom-call | flops 20000000000 | tf_op jit(solution)/shard_map/pallas_call | solution.py:77
  91.4 1.4 shard_map.99
  92.8 1.9 %collective-permute-start.20 = (bf16[2,2,96,1024]{3,2,1,0:T(8,128)(2,1)}, bf16[2,2,96,1024]{3,2,1,0:T(8,128)(2,1)}, u32[]{:S(2)}, u32[]{:S(2)}) collective-permute-start(bf16[2,2,96,1024]{3,2,1,0:T(8,128)(2,1)} %get-tuple-element.157), channel_id=1, source_target_pairs={{0,32},{1,33},{2,34},{3,35},{4,36},{5,37},{6,38},{7,39},{8,40},{9,... | collective-permute-start | bytes 2359304 | tf_op jit(solution)/shard_map/ppermute | solution.py:56
  95.1 2.6 %collective-permute-start.21 = (bf16[2,2,96,1024]{3,2,1,0:T(8,128)(2,1)S(1)}, bf16[2,2,96,1024]{3,2,1,0:T(8,128)(2,1)S(1)}, u32[]{:S(2)}, u32[]{:S(2)}) collective-permute-start(bf16[2,2,96,1024]{3,2,1,0:T(8,128)(2,1)S(1)} %get-tuple-element.159), channel_id=1, source_target_pairs={{0,96},{1,97},{2,98},{3,99},{4,100},{5,101},{6,102},{7,103},{8,104... | collective-permute-start | bytes 2359304 | tf_op jit(solution)/shard_map/ppermute | solution.py:56
  97.7 2.1 %shard_map.101 = (bf16[2,640,1024]{2,1,0:T(8,128)(2,1)S(1)}, bf16[4,2,96,1024]{3,2,1,0:T(8,128)(2,1)S(1)}, f32[8,128]{1,0:T(8,128)S(1)}) custom-call(f32[8,128]{1,0:T(8,128)S(1)} %get-tuple-element.138.refs_0_, bf16[2,320,1024]{2,1,0:T(8,128)(2,1)S(1)} %get-tuple-element.121.refs_1_, bf16[2,320,1024]{2,1,0:T(8,128)(2,1)S(1)} %collective-permute-done.16.refs_2_.refs_9_, ...), custom_call_target="tpu_custom_call" | custom-call | flops 20000000000 | tf_op jit(solution)/shard_map/pallas_call | solution.py:77
  99.9 3.0 %shard_map.102 = (bf16[2,640,1024]{2,1,0:T(8,128)(2,1)S(1)}, bf16[4,2,96,1024]{3,2,1,0:T(8,128)(2,1)S(1)}, f32[8,128]{1,0:T(8,128)S(1)}) custom-call(f32[8,128]{1,0:T(8,128)S(1)} %get-tuple-element.140.refs_0_, bf16[2,320,1024]{2,1,0:T(8,128)(2,1)S(1)} %get-tuple-element.122.refs_2_.refs_1_, bf16[2,320,1024]{2,1,0:T(8,128)(2,1)} %collective-permute-done.17.refs_2_.refs_10_, ...), custom_call_target="tpu_custom_call" | custom-call | flops 20000000000 | tf_op jit(solution)/shard_map/pallas_call | solution.py:77
  103.5 1.5 copy-done.13
  105.1 1.9 %shard_map.103 = (bf16[4,2,96,1024]{3,2,1,0:T(8,128)(2,1)S(1)}, f32[8,128]{1,0:T(8,128)S(1)}) custom-call(f32[8,128]{1,0:T(8,128)S(1)} %get-tuple-element.142.refs_0_, bf16[2,640,1024]{2,1,0:T(8,128)(2,1)S(1)} %get-tuple-element.143.refs_1_, bf16[8,2,96,640]{3,2,1,0:T(8,128)(2,1)S(1)} %copy-done.13), custom_call_target="tpu_custom_call" | custom-call | flops 20000000000 | tf_op jit(solution)/shard_map/pallas_call | solution.py:77
  106.9 1.9 %shard_map.104 = (bf16[4,2,96,1024]{3,2,1,0:T(8,128)(2,1)S(1)}, f32[8,128]{1,0:T(8,128)S(1)}) custom-call(f32[8,128]{1,0:T(8,128)S(1)} %get-tuple-element.144.refs_0_, bf16[2,640,1024]{2,1,0:T(8,128)(2,1)S(1)} %get-tuple-element.145.refs_1_, bf16[8,2,96,640]{3,2,1,0:T(8,128)(2,1)S(1)} %copy-done.13), custom_call_target="tpu_custom_call" | custom-call | flops 20000000000 | tf_op jit(solution)/shard_map/pallas_call | solution.py:77
  109.2 1.1 collective-permute-start.22
  110.8 2.8 %collective-permute-start.23 = (bf16[2,2,96,1024]{3,2,1,0:T(8,128)(2,1)S(1)}, bf16[2,2,96,1024]{3,2,1,0:T(8,128)(2,1)S(1)}, u32[]{:S(2)}, u32[]{:S(2)}) collective-permute-start(bf16[2,2,96,1024]{3,2,1,0:T(8,128)(2,1)S(1)} %get-tuple-element.163), channel_id=1, source_target_pairs={{0,96},{1,97},{2,98},{3,99},{4,100},{5,101},{6,102},{7,103},{8,104... | collective-permute-start | bytes 2359304 | tf_op jit(solution)/shard_map/ppermute | solution.py:56
  113.6 4.6 %copy-done.11 = bf16[2,768,4096]{2,1,0:T(8,128)(2,1)S(1)} copy-done((bf16[2,768,4096]{2,1,0:T(8,128)(2,1)S(1)}, bf16[2,768,4096]{2,1,0:T(8,128)(2,1)}, u32[]{:S(2)}) %copy-start.11) | copy-done | bytes 12582936
  118.2 10.5 %shard_map.107 = (bf16[2,16,40,768]{3,2,1,0:T(8,128)(2,1)}, f32[16,2,128]{2,1,0:T(2,128)S(1)}, f32[8,128]{1,0:T(8,128)S(1)}) custom-call(f32[8,128]{1,0:T(8,128)S(1)} %get-tuple-element.152.refs_0_, s32[32]{0:T(128)S(1)} %pad_add_fusion.1.refs_1_, f32[32,128]{1,0:T(8,128)S(1)} %copy-done.8, f32[32,128]{1,0:T(8,128)S(1)} %copy-done.10, ...), custom_call_target="tpu_custom_call" | custom-call | flops 20000000000 | tf_op jit(solution)/shard_map/pallas_call | solution.py:77
  128.6 1.2 shard_map.108
  131.2 2.0 %collective-permute-start.24 = (bf16[1,2,96,1024]{3,2,1,0:T(8,128)(2,1)S(1)}, bf16[1,2,96,1024]{3,2,1,0:T(8,128)(2,1)S(1)}, u32[]{:S(2)}, u32[]{:S(2)}) collective-permute-start(bf16[1,2,96,1024]{3,2,1,0:T(8,128)(2,1)S(1)} %get-tuple-element.165), channel_id=1, source_target_pairs={{0,96},{1,97},{2,98},{3,99},{4,100},{5,101},{6,102},{7,103},{8,104... | collective-permute-start | bytes 1179656 | tf_op jit(solution)/shard_map/ppermute | solution.py:56
  133.5 1.3 collective-permute-start.26
  135.3 13.9 %all_to_all.10 = f32[16,2,128]{2,1,0:T(2,128)S(1)} all-to-all(f32[16,2,128]{2,1,0:T(2,128)S(1)} %get-tuple-element.170), channel_id=1, replica_groups=mesh['section'=8,'expert'=16] {'expert'}, dimensions={0} | all-to-all | bytes 32768 | tf_op jit(solution)/shard_map/all_to_all | solution.py:571
  149.8 1.8 %collective-permute-done.26.refs_12_ = bf16[1,2,96,1024]{3,2,1,0:T(8,128)(2,1)S(1)} collective-permute-done((bf16[1,2,96,1024]{3,2,1,0:T(8,128)(2,1)S(1)}, bf16[1,2,96,1024]{3,2,1,0:T(8,128)(2,1)S(1)}, u32[]{:S(2)}, u32[]{:S(2)}) %collective-permute-start.26) | collective-permute-done | bytes 393248 | tf_op jit(solution)/shard_map/ppermute | solution.py:56
  151.6 3.1 %shard_map.112 = (bf16[2,96,4096]{2,1,0:T(8,128)(2,1)}, f32[8,128]{1,0:T(8,128)}) custom-call(f32[8,128]{1,0:T(8,128)S(1)} %get-tuple-element.164.refs_0_, bf16[4,2,96,1024]{3,2,1,0:T(8,128)(2,1)S(1)} %copy-done.6, bf16[4,2,96,1024]{3,2,1,0:T(8,128)(2,1)S(1)} %copy-done.4, bf16[2,2,96,1024]{3,2,1,0:T(8,128)(2,1)} %collective-permute-done.20.refs_3_, ...), custom_call_target="tpu_custom_call" | custom-call | flops 20000000000 | tf_op jit(solution)/shard_map/pallas_call | solution.py:77
  (124 shorter events, 17.3 us)
Async XLA Ops:
  1.7 10.7 %collective-permute-start.1 = (bf16[128,1024]{1,0:T(8,128)(2,1)S(1)}, bf16[128,1024]{1,0:T(8,128)(2,1)S(1)}, u32[]{:S(2)}, u32[]{:S(2)}) collective-permute-start(bf16[128,1024]{1,0:T(8,128)(2,1)S(1)} %get-tuple-element.176), channel_id=1, source_target_pairs={{0,3},{1,2},{2,1},{3,0},{4,7},{5,6},{6,5},{7,4},{8,11},{9,10},{10,... | collective-permute-start | bytes 786440 | tf_op jit(solution)/shard_map/ppermute | solution.py:56
  4.6 6.4 %collective-permute-start = (bf16[128,1024]{1,0:T(8,128)(2,1)S(1)}, bf16[128,1024]{1,0:T(8,128)(2,1)S(1)}, u32[]{:S(2)}, u32[]{:S(2)}) collective-permute-start(bf16[128,1024]{1,0:T(8,128)(2,1)S(1)} %get-tuple-element.177), channel_id=1, source_target_pairs={{0,1},{1,0},{2,3},{3,2},{4,5},{5,4},{6,7},{7,6},{8,9},{9,8},{10,11... | collective-permute-start | bytes 786440 | tf_op jit(solution)/shard_map/ppermute | solution.py:56
  12.6 12.0 %collective-permute-start.3 = (bf16[256,1024]{1,0:T(8,128)(2,1)S(1)}, bf16[256,1024]{1,0:T(8,128)(2,1)S(1)}, u32[]{:S(2)}, u32[]{:S(2)}) collective-permute-start(bf16[256,1024]{1,0:T(8,128)(2,1)S(1)} %get-tuple-element.93), channel_id=1, source_target_pairs={{0,1},{1,0},{2,3},{3,2},{4,5},{5,4},{6,7},{7,6},{8,9},{9,8},{10,11... | collective-permute-start | bytes 1572872 | tf_op jit(solution)/shard_map/ppermute | solution.py:56
  12.9 10.4 %collective-permute-start.2 = (bf16[256,1024]{1,0:T(8,128)(2,1)S(1)}, bf16[256,1024]{1,0:T(8,128)(2,1)S(1)}, u32[]{:S(2)}, u32[]{:S(2)}) collective-permute-start(bf16[256,1024]{1,0:T(8,128)(2,1)S(1)} %get-tuple-element.91), channel_id=1, source_target_pairs={{0,3},{1,2},{2,1},{3,0},{4,7},{5,6},{6,5},{7,4},{8,11},{9,10},{10,... | collective-permute-start | bytes 1572872 | tf_op jit(solution)/shard_map/ppermute | solution.py:56
  14.3 13.6 %collective-permute-start.5 = (bf16[128,1024]{1,0:T(8,128)(2,1)S(1)}, bf16[128,1024]{1,0:T(8,128)(2,1)S(1)}, u32[]{:S(2)}, u32[]{:S(2)}) collective-permute-start(bf16[128,1024]{1,0:T(8,128)(2,1)S(1)} %get-tuple-element.97), channel_id=1, source_target_pairs={{0,3},{1,2},{2,1},{3,0},{4,7},{5,6},{6,5},{7,4},{8,11},{9,10},{10,... | collective-permute-start | bytes 786440 | tf_op jit(solution)/shard_map/ppermute | solution.py:56
  16.5 9.3 %collective-permute-start.4 = (bf16[128,1024]{1,0:T(8,128)(2,1)S(1)}, bf16[128,1024]{1,0:T(8,128)(2,1)S(1)}, u32[]{:S(2)}, u32[]{:S(2)}) collective-permute-start(bf16[128,1024]{1,0:T(8,128)(2,1)S(1)} %get-tuple-element.95), channel_id=1, source_target_pairs={{0,1},{1,0},{2,3},{3,2},{4,5},{5,4},{6,7},{7,6},{8,9},{9,8},{10,11... | collective-permute-start | bytes 786440 | tf_op jit(solution)/shard_map/ppermute | solution.py:56
  26.7 19.5 %collective-permute-start.6 = (bf16[256,1024]{1,0:T(8,128)(2,1)}, bf16[256,1024]{1,0:T(8,128)(2,1)}, u32[]{:S(2)}, u32[]{:S(2)}) collective-permute-start(bf16[256,1024]{1,0:T(8,128)(2,1)} %get-tuple-element.105), channel_id=1, source_target_pairs={{0,3},{1,2},{2,1},{3,0},{4,7},{5,6},{6,5},{7,4},{8,11},{9,10},{10,... | collective-permute-start | bytes 1572872 | tf_op jit(solution)/shard_map/ppermute | solution.py:56
  27.9 16.8 %copy-start.2 = (bf16[1,2,16,40,768]{4,3,2,1,0:T(8,128)(2,1)S(1)}, bf16[1,2,16,40,768]{4,3,2,1,0:T(8,128)(2,1)}, u32[]{:S(2)}) copy-start(bf16[1,2,16,40,768]{4,3,2,1,0:T(8,128)(2,1)} %param.8) | copy-start | bytes 5898244
  28.9 17.4 %copy-start.1 = (bf16[128,4096]{1,0:T(8,128)(2,1)S(1)}, bf16[128,4096]{1,0:T(8,128)(2,1)}, u32[]{:S(2)}) copy-start(bf16[128,4096]{1,0:T(8,128)(2,1)} %refs_1_.17) | copy-start | bytes 3145732
  29.5 14.2 %all-to-all-start = ((bf16[16,16,128]{2,1,0:T(8,128)(2,1)}), bf16[16,16,128]{2,1,0:T(8,128)(2,1)S(1)}, u32[]{:S(2)}, u32[]{:S(2)}) async-start(bf16[16,16,128]{2,1,0:T(8,128)(2,1)} %get-tuple-element.100), calls=%async_computation | async-start | bytes 131072 | tf_op jit(solution)/shard_map/all_to_all | solution.py:537
  35.7 15.6 %collective-permute-start.7 = (bf16[256,1024]{1,0:T(8,128)(2,1)}, bf16[256,1024]{1,0:T(8,128)(2,1)}, u32[]{:S(2)}, u32[]{:S(2)}) collective-permute-start(bf16[256,1024]{1,0:T(8,128)(2,1)} %copy-done.24), channel_id=1, source_target_pairs={{0,1},{1,0},{2,3},{3,2},{4,5},{5,4},{6,7},{7,6},{8,9},{9,8},{10,11... | collective-permute-start | bytes 1572872 | tf_op jit(solution)/shard_map/ppermute | solution.py:56
  37.6 21.2 %collective-permute-start.9 = (bf16[512,1024]{1,0:T(8,128)(2,1)}, bf16[512,1024]{1,0:T(8,128)(2,1)}, u32[]{:S(2)}, u32[]{:S(2)}) collective-permute-start(bf16[512,1024]{1,0:T(8,128)(2,1)} %copy-done.22), channel_id=1, source_target_pairs={{0,12},{1,13},{2,14},{3,15},{4,8},{5,9},{6,10},{7,11},{8,4},{9,5},... | collective-permute-start | bytes 3145736 | tf_op jit(solution)/shard_map/ppermute | solution.py:56
  40.3 15.4 %collective-permute-start.8 = (bf16[512,1024]{1,0:T(8,128)(2,1)}, bf16[512,1024]{1,0:T(8,128)(2,1)}, u32[]{:S(2)}, u32[]{:S(2)}) collective-permute-start(bf16[512,1024]{1,0:T(8,128)(2,1)} %copy-done.20), channel_id=1, source_target_pairs={{0,4},{1,5},{2,6},{3,7},{4,0},{5,1},{6,2},{7,3},{8,12},{9,13},{10,... | collective-permute-start | bytes 3145736 | tf_op jit(solution)/shard_map/ppermute | solution.py:56
  44.7 3.4 %copy-start.7 = (f32[32,128]{1,0:T(8,128)}, f32[32,128]{1,0:T(8,128)S(1)}, u32[]{:S(2)}) copy-start(f32[32,128]{1,0:T(8,128)S(1)} %get-tuple-element.102.refs_2_) | copy-start | bytes 49156
  44.7 3.4 %copy-start.9 = (f32[32,128]{1,0:T(8,128)}, f32[32,128]{1,0:T(8,128)S(1)}, u32[]{:S(2)}) copy-start(f32[32,128]{1,0:T(8,128)S(1)} %get-tuple-element.103.refs_3_) | copy-start | bytes 49156
  46.2 53.7 %copy-start.12 = (bf16[8,2,96,640]{3,2,1,0:T(8,128)(2,1)}, bf16[8,2,96,640]{3,2,1,0:T(8,128)(2,1)S(1)}, u32[]{:S(2)}) copy-start(bf16[8,2,96,640]{3,2,1,0:T(8,128)(2,1)S(1)} %get-tuple-element.125.refs_3_.refs_2_) | copy-start | bytes 5898244
  51.3 4.4 %copy-start.21 = (bf16[512,1024]{1,0:T(8,128)(2,1)S(1)}, bf16[512,1024]{1,0:T(8,128)(2,1)}, u32[]{:S(2)}) copy-start(bf16[512,1024]{1,0:T(8,128)(2,1)} %copy-done.20) | copy-start | bytes 3145732
  52.6 19.7 %collective-permute-start.11 = (bf16[512,1024]{1,0:T(8,128)(2,1)S(1)}, bf16[512,1024]{1,0:T(8,128)(2,1)S(1)}, u32[]{:S(2)}, u32[]{:S(2)}) collective-permute-start(bf16[512,1024]{1,0:T(8,128)(2,1)S(1)} %get-tuple-element.119.refs_1_), channel_id=1, source_target_pairs={{0,12},{1,13},{2,14},{3,15},{4,8},{5,9},{6,10},{7,11},{8,4},{9,5},... | collective-permute-start | bytes 3145736 | tf_op jit(solution)/shard_map/ppermute | solution.py:56
  55.5 14.8 %collective-permute-start.10 = (bf16[512,1024]{1,0:T(8,128)(2,1)S(1)}, bf16[512,1024]{1,0:T(8,128)(2,1)S(1)}, u32[]{:S(2)}, u32[]{:S(2)}) collective-permute-start(bf16[512,1024]{1,0:T(8,128)(2,1)S(1)} %get-tuple-element.117.refs_1_), channel_id=1, source_target_pairs={{0,4},{1,5},{2,6},{3,7},{4,0},{5,1},{6,2},{7,3},{8,12},{9,13},{10,... | collective-permute-start | bytes 3145736 | tf_op jit(solution)/shard_map/ppermute | solution.py:56
  55.7 8.7 %slice-start = ((s8[12582912]{0:T(1024)(128)(4,1)}), s8[4194304]{0:T(1024)(128)(4,1)S(1)}, s32[]{:S(2)}) async-start(s8[12582912]{0:T(1024)(128)(4,1)} %bitcast.13), calls=%async_computation.2 | async-start | bytes 8388608
  55.7 8.7 %slice-start.1 = ((s8[12582912]{0:T(1024)(128)(4,1)}), s8[4194304]{0:T(1024)(128)(4,1)S(1)}, s32[]{:S(2)}) async-start(s8[12582912]{0:T(1024)(128)(4,1)} %bitcast.13), calls=%async_computation.3 | async-start | bytes 8388608
  58.9 5.5 %slice-start.2 = ((s8[12582912]{0:T(1024)(128)(4,1)}), s8[4194304]{0:T(1024)(128)(4,1)S(1)}, s32[]{:S(2)}) async-start(s8[12582912]{0:T(1024)(128)(4,1)} %bitcast.13), calls=%async_computation.4 | async-start | bytes 8388608
  62.0 24.8 %collective-permute-start.13 = (bf16[2,320,1024]{2,1,0:T(8,128)(2,1)S(1)}, bf16[2,320,1024]{2,1,0:T(8,128)(2,1)S(1)}, u32[]{:S(2)}, u32[]{:S(2)}) collective-permute-start(bf16[2,320,1024]{2,1,0:T(8,128)(2,1)S(1)} %get-tuple-element.129), channel_id=1, source_target_pairs={{0,4},{1,5},{2,6},{3,7},{4,0},{5,1},{6,2},{7,3},{8,12},{9,13},{10,... | collective-permute-start | bytes 3932168 | tf_op jit(solution)/shard_map/ppermute | solution.py:56
  63.9 18.8 %collective-permute-start.12 = (bf16[2,320,1024]{2,1,0:T(8,128)(2,1)S(1)}, bf16[2,320,1024]{2,1,0:T(8,128)(2,1)S(1)}, u32[]{:S(2)}, u32[]{:S(2)}) collective-permute-start(bf16[2,320,1024]{2,1,0:T(8,128)(2,1)S(1)} %get-tuple-element.124), channel_id=1, source_target_pairs={{0,12},{1,13},{2,14},{3,15},{4,8},{5,9},{6,10},{7,11},{8,4},{9,5},... | collective-permute-start | bytes 3932168 | tf_op jit(solution)/shard_map/ppermute | solution.py:56
  75.2 24.8 %collective-permute-start.17 = (bf16[2,320,1024]{2,1,0:T(8,128)(2,1)}, bf16[2,320,1024]{2,1,0:T(8,128)(2,1)}, u32[]{:S(2)}, u32[]{:S(2)}) collective-permute-start(bf16[2,320,1024]{2,1,0:T(8,128)(2,1)} %get-tuple-element.141), channel_id=1, source_target_pairs={{0,4},{1,5},{2,6},{3,7},{4,0},{5,1},{6,2},{7,3},{8,12},{9,13},{10,... | collective-permute-start | bytes 3932168 | tf_op jit(solution)/shard_map/ppermute | solution.py:56
  75.4 22.3 %collective-permute-start.16 = (bf16[2,320,1024]{2,1,0:T(8,128)(2,1)S(1)}, bf16[2,320,1024]{2,1,0:T(8,128)(2,1)S(1)}, u32[]{:S(2)}, u32[]{:S(2)}) collective-permute-start(bf16[2,320,1024]{2,1,0:T(8,128)(2,1)S(1)} %get-tuple-element.139), channel_id=1, source_target_pairs={{0,12},{1,13},{2,14},{3,15},{4,8},{5,9},{6,10},{7,11},{8,4},{9,5},... | collective-permute-start | bytes 3932168 | tf_op jit(solution)/shard_map/ppermute | solution.py:56
  84.8 6.5 %collective-permute-start.14 = (bf16[4,2,96,1024]{3,2,1,0:T(8,128)(2,1)S(1)}, bf16[4,2,96,1024]{3,2,1,0:T(8,128)(2,1)S(1)}, u32[]{:S(2)}, u32[]{:S(2)}) collective-permute-start(bf16[4,2,96,1024]{3,2,1,0:T(8,128)(2,1)S(1)} %get-tuple-element.134), channel_id=1, source_target_pairs={{0,16},{1,17},{2,18},{3,19},{4,20},{5,21},{6,22},{7,23},{8,24},{9,... | collective-permute-start | bytes 4718600 | tf_op jit(solution)/shard_map/ppermute | solution.py:56
  86.8 4.6 %copy-start.5 = (bf16[4,2,96,1024]{3,2,1,0:T(8,128)(2,1)}, bf16[4,2,96,1024]{3,2,1,0:T(8,128)(2,1)S(1)}, u32[]{:S(2)}) copy-start(bf16[4,2,96,1024]{3,2,1,0:T(8,128)(2,1)S(1)} %get-tuple-element.133.refs_1_.refs_3_) | copy-start | bytes 4718596
  88.9 5.8 %collective-permute-start.15 = (bf16[4,2,96,1024]{3,2,1,0:T(8,128)(2,1)S(1)}, bf16[4,2,96,1024]{3,2,1,0:T(8,128)(2,1)S(1)}, u32[]{:S(2)}, u32[]{:S(2)}) collective-permute-start(bf16[4,2,96,1024]{3,2,1,0:T(8,128)(2,1)S(1)} %get-tuple-element.137), channel_id=1, source_target_pairs={{0,16},{1,17},{2,18},{3,19},{4,20},{5,21},{6,22},{7,23},{8,24},{9,... | collective-permute-start | bytes 4718600 | tf_op jit(solution)/shard_map/ppermute | solution.py:56
  92.8 35.8 %collective-permute-start.20 = (bf16[2,2,96,1024]{3,2,1,0:T(8,128)(2,1)}, bf16[2,2,96,1024]{3,2,1,0:T(8,128)(2,1)}, u32[]{:S(2)}, u32[]{:S(2)}) collective-permute-start(bf16[2,2,96,1024]{3,2,1,0:T(8,128)(2,1)} %get-tuple-element.157), channel_id=1, source_target_pairs={{0,32},{1,33},{2,34},{3,35},{4,36},{5,37},{6,38},{7,39},{8,40},{9,... | collective-permute-start | bytes 2359304 | tf_op jit(solution)/shard_map/ppermute | solution.py:56
  95.1 34.7 %collective-permute-start.21 = (bf16[2,2,96,1024]{3,2,1,0:T(8,128)(2,1)S(1)}, bf16[2,2,96,1024]{3,2,1,0:T(8,128)(2,1)S(1)}, u32[]{:S(2)}, u32[]{:S(2)}) collective-permute-start(bf16[2,2,96,1024]{3,2,1,0:T(8,128)(2,1)S(1)} %get-tuple-element.159), channel_id=1, source_target_pairs={{0,96},{1,97},{2,98},{3,99},{4,100},{5,101},{6,102},{7,103},{8,104... | collective-permute-start | bytes 2359304 | tf_op jit(solution)/shard_map/ppermute | solution.py:56
  99.8 9.0 %collective-permute-start.18 = (bf16[4,2,96,1024]{3,2,1,0:T(8,128)(2,1)S(1)}, bf16[4,2,96,1024]{3,2,1,0:T(8,128)(2,1)S(1)}, u32[]{:S(2)}, u32[]{:S(2)}) collective-permute-start(bf16[4,2,96,1024]{3,2,1,0:T(8,128)(2,1)S(1)} %get-tuple-element.148), channel_id=1, source_target_pairs={{0,16},{1,17},{2,18},{3,19},{4,20},{5,21},{6,22},{7,23},{8,24},{9,... | collective-permute-start | bytes 4718600 | tf_op jit(solution)/shard_map/ppermute | solution.py:56
  103.0 7.4 %collective-permute-start.19 = (bf16[4,2,96,1024]{3,2,1,0:T(8,128)(2,1)S(1)}, bf16[4,2,96,1024]{3,2,1,0:T(8,128)(2,1)S(1)}, u32[]{:S(2)}, u32[]{:S(2)}) collective-permute-start(bf16[4,2,96,1024]{3,2,1,0:T(8,128)(2,1)S(1)} %get-tuple-element.151), channel_id=1, source_target_pairs={{0,16},{1,17},{2,18},{3,19},{4,20},{5,21},{6,22},{7,23},{8,24},{9,... | collective-permute-start | bytes 4718600 | tf_op jit(solution)/shard_map/ppermute | solution.py:56
  109.2 24.0 %collective-permute-start.22 = (bf16[2,2,96,1024]{3,2,1,0:T(8,128)(2,1)S(1)}, bf16[2,2,96,1024]{3,2,1,0:T(8,128)(2,1)S(1)}, u32[]{:S(2)}, u32[]{:S(2)}) collective-permute-start(bf16[2,2,96,1024]{3,2,1,0:T(8,128)(2,1)S(1)} %get-tuple-element.161), channel_id=1, source_target_pairs={{0,32},{1,33},{2,34},{3,35},{4,36},{5,37},{6,38},{7,39},{8,40},{9,... | collective-permute-start | bytes 2359304 | tf_op jit(solution)/shard_map/ppermute | solution.py:56
  110.3 3.2 %copy-start.8 = (f32[32,128]{1,0:T(8,128)S(1)}, f32[32,128]{1,0:T(8,128)}, u32[]{:S(2)}) copy-start(f32[32,128]{1,0:T(8,128)} %copy-done.7) | copy-start | bytes 49156
  110.3 3.2 %copy-start.10 = (f32[32,128]{1,0:T(8,128)S(1)}, f32[32,128]{1,0:T(8,128)}, u32[]{:S(2)}) copy-start(f32[32,128]{1,0:T(8,128)} %copy-done.9) | copy-start | bytes 49156
  110.3 3.2 %copy-start.15 = (bf16[2,320,1024]{2,1,0:T(8,128)(2,1)S(1)}, bf16[2,320,1024]{2,1,0:T(8,128)(2,1)}, u32[]{:S(2)}) copy-start(bf16[2,320,1024]{2,1,0:T(8,128)(2,1)} %copy-done.14) | copy-start | bytes 3932164
  110.3 3.2 %copy-start.17 = (bf16[2,320,1024]{2,1,0:T(8,128)(2,1)S(1)}, bf16[2,320,1024]{2,1,0:T(8,128)(2,1)}, u32[]{:S(2)}) copy-start(bf16[2,320,1024]{2,1,0:T(8,128)(2,1)} %copy-done.16) | copy-start | bytes 3932164
  110.4 3.2 %copy-start.19 = (bf16[2,320,1024]{2,1,0:T(8,128)(2,1)S(1)}, bf16[2,320,1024]{2,1,0:T(8,128)(2,1)}, u32[]{:S(2)}) copy-start(bf16[2,320,1024]{2,1,0:T(8,128)(2,1)} %copy-done.18) | copy-start | bytes 3932164
  110.8 24.1 %collective-permute-start.23 = (bf16[2,2,96,1024]{3,2,1,0:T(8,128)(2,1)S(1)}, bf16[2,2,96,1024]{3,2,1,0:T(8,128)(2,1)S(1)}, u32[]{:S(2)}, u32[]{:S(2)}) collective-permute-start(bf16[2,2,96,1024]{3,2,1,0:T(8,128)(2,1)S(1)} %get-tuple-element.163), channel_id=1, source_target_pairs={{0,96},{1,97},{2,98},{3,99},{4,100},{5,101},{6,102},{7,103},{8,104... | collective-permute-start | bytes 2359304 | tf_op jit(solution)/shard_map/ppermute | solution.py:56
  113.6 4.6 %copy-start.11 = (bf16[2,768,4096]{2,1,0:T(8,128)(2,1)S(1)}, bf16[2,768,4096]{2,1,0:T(8,128)(2,1)}, u32[]{:S(2)}) copy-start(bf16[2,768,4096]{2,1,0:T(8,128)(2,1)} %refs_11_.1) | copy-start | bytes 37748740
  118.2 10.5 %copy-start.4 = (bf16[4,2,96,1024]{3,2,1,0:T(8,128)(2,1)S(1)}, bf16[4,2,96,1024]{3,2,1,0:T(8,128)(2,1)}, u32[]{:S(2)}) copy-start(bf16[4,2,96,1024]{3,2,1,0:T(8,128)(2,1)} %copy-done.3) | copy-start | bytes 4718596
  118.2 10.5 %copy-start.6 = (bf16[4,2,96,1024]{3,2,1,0:T(8,128)(2,1)S(1)}, bf16[4,2,96,1024]{3,2,1,0:T(8,128)(2,1)}, u32[]{:S(2)}) copy-start(bf16[4,2,96,1024]{3,2,1,0:T(8,128)(2,1)} %copy-done.5) | copy-start | bytes 4718596
  130.2 19.7 %collective-permute-start.25 = (bf16[1,2,96,1024]{3,2,1,0:T(8,128)(2,1)S(1)}, bf16[1,2,96,1024]{3,2,1,0:T(8,128)(2,1)S(1)}, u32[]{:S(2)}, u32[]{:S(2)}) collective-permute-start(bf16[1,2,96,1024]{3,2,1,0:T(8,128)(2,1)S(1)} %get-tuple-element.166), channel_id=1, source_target_pairs={{0,32},{1,33},{2,34},{3,35},{4,36},{5,37},{6,38},{7,39},{8,40},{9,... | collective-permute-start | bytes 1179656 | tf_op jit(solution)/shard_map/ppermute | solution.py:56
  131.2 18.6 %collective-permute-start.24 = (bf16[1,2,96,1024]{3,2,1,0:T(8,128)(2,1)S(1)}, bf16[1,2,96,1024]{3,2,1,0:T(8,128)(2,1)S(1)}, u32[]{:S(2)}, u32[]{:S(2)}) collective-permute-start(bf16[1,2,96,1024]{3,2,1,0:T(8,128)(2,1)S(1)} %get-tuple-element.165), channel_id=1, source_target_pairs={{0,96},{1,97},{2,98},{3,99},{4,100},{5,101},{6,102},{7,103},{8,104... | collective-permute-start | bytes 1179656 | tf_op jit(solution)/shard_map/ppermute | solution.py:56
  133.5 18.1 %collective-permute-start.26 = (bf16[1,2,96,1024]{3,2,1,0:T(8,128)(2,1)S(1)}, bf16[1,2,96,1024]{3,2,1,0:T(8,128)(2,1)S(1)}, u32[]{:S(2)}, u32[]{:S(2)}) collective-permute-start(bf16[1,2,96,1024]{3,2,1,0:T(8,128)(2,1)S(1)} %get-tuple-element.167), channel_id=1, source_target_pairs={{0,96},{1,97},{2,98},{3,99},{4,100},{5,101},{6,102},{7,103},{8,104... | collective-permute-start | bytes 1179656 | tf_op jit(solution)/shard_map/ppermute | solution.py:56
  134.9 14.3 %copy-start.27 = (s32[128,8]{0,1:T(8,128)S(1)}, s32[128,8]{0,1:T(8,128)}, u32[]{:S(2)}) copy-start(s32[128,8]{0,1:T(8,128)} %param.7) | copy-start | bytes 12292
  135.2 16.4 %collective-permute-start.27 = (bf16[1,2,96,1024]{3,2,1,0:T(8,128)(2,1)S(1)}, bf16[1,2,96,1024]{3,2,1,0:T(8,128)(2,1)S(1)}, u32[]{:S(2)}, u32[]{:S(2)}) collective-permute-start(bf16[1,2,96,1024]{3,2,1,0:T(8,128)(2,1)S(1)} %get-tuple-element.168), channel_id=1, source_target_pairs={{0,32},{1,33},{2,34},{3,35},{4,36},{5,37},{6,38},{7,39},{8,40},{9,... | collective-permute-start | bytes 1179656 | tf_op jit(solution)/shard_map/ppermute | solution.py:56
  (12 other events, 19.9 us)

commit v3 on v2

--- a/solution.py
+++ b/solution.py
@@ -7,13 +7,14 @@
 
 AXES = ("section", "expert")
 CHUNKS = (1024, 1024, 1024, 1024)
-TILE = 512
+TILE = 1024
 DEEP = 1024
 VMEM_LIMIT = 20 * 1024 * 1024
+END_LIMIT = 46 * 1024 * 1024
 PLAN = (
-    "a0", "a1", "o2", "o3-", "r0-", "r1", "a2", "a3", "I-", "P-", "T-", "r2", "r3", "p0", "p1",
-    "h0", "p2", "p3", "h1", "w0", "m0", "w1", "m1", "s0", "s1", "w2", "w3", "m2", "m3", "s2",
-    "s3", "H", "t0-", "t1-", "t2-", "t3-", "e",
+    "a0", "a1", "o2-", "o3-", "I-", "r0-", "r1-", "a2", "a3", "P-", "T-", "r2", "r3", "p0",
+    "p1", "h0", "p2", "p3", "h1", "w0", "m0", "w1", "m1", "s0", "s1", "w2", "w3", "m2", "m3",
+    "s2", "s3", "H", "t0-", "t1-", "t2-", "t3-", "e",
 )
 F32, BF16 = jnp.float32, jnp.bfloat16
 
@@ -60,6 +61,7 @@
     def __init__(self):
         self.token = None
         self.cost = 0
+        self.room = VMEM_LIMIT
 
 
 ORDER = Order()
@@ -81,7 +83,7 @@
         out_specs=[spec for _, spec in outputs] + [whole((8, 128))],
         out_shape=[shape for shape, _ in outputs] + [out(8, 128, dtype=F32)],
         scratch_shapes=list(scratch),
-        compiler_params=pltpu.CompilerParams(vmem_limit_bytes=VMEM_LIMIT),
+        compiler_params=pltpu.CompilerParams(vmem_limit_bytes=ORDER.room),
         cost_estimate=pl.CostEstimate(
             flops=int(ORDER.cost * 10**9), bytes_accessed=0, transcendentals=0
         ),
@@ -530,6 +532,7 @@
     for step in PLAN:
         kind, n = step[0], int(step[1:2].strip("-") or 0)
         parity = n % 2
+        ORDER.room = END_LIMIT if kind == "H" else VMEM_LIMIT
         ORDER.cost = 0 if step.endswith("-") else 20
         if kind == "o":
             one[n] = send(own_rows(d_output, offsets[n], CHUNKS[n]), along("first", 0, parity))

time: 155 us -> 150 us (0.968)
  local copies, waits for them, and re-layouts: 11.4 us -> 5.42 us
  Pallas kernels: 62.5 us -> 67.6 us
  waiting for transfers between devices: 22.8 us -> 18.9 us
  starting transfers between devices: 40.5 us -> 42.3 us
    unnamed x62 -> x64, local copies, waits for them, and re-layouts: 10.2 us -> 4.19 us
    pallas_call x37, Pallas kernels: 62.5 us -> 67.6 us  [call(): pl.pallas_call(run, grid=grid, in_specs=[pl.BlockSpec(memory_space=pltpu....]
    all_to_all x1, waiting for transfers between devices: 3.11 us -> 0.01 us  [shards(): all_info = lax.all_to_all(share(info, sources), 'expert', 0, 0, tiled=True)]
  transfers between devices with their start and end apart: 29 -> 29, of which waited for: 7 -> 7; matrix products, arithmetic and copies ran while one was open for 2% -> 1% of each run, Pallas kernels for 38% -> 42%
where the time goes in v3:
time: 150 us
  Pallas kernels  67.6 us (45%)
  starting transfers between devices  42.3 us (28%)
  waiting for transfers between devices  18.9 us (13%)
  blocking collectives  13.5 us (9%)
  local copies, waits for them, and re-layouts  5.42 us (4%)
    pallas_call x37, Pallas kernels, call(): pl.pallas_call(run, grid=grid, in_specs=[pl.BlockSpec(memory_space=pltpu....  67.6 us
    ppermute x28, starting transfers between devices, send(): return lax.ppermute(value, AXES, pairs)  35.4 us
    ppermute x28, waiting for transfers between devices, send(): return lax.ppermute(value, AXES, pairs)  18.9 us
    all_to_all x1, blocking collectives, shards(): lax.all_to_all(token_grad, 'expert', 0, 0, tiled=True).reshape(-1, tokens)  13.5 us
    all_to_all x1, starting transfers between devices, shards(): all_info = lax.all_to_all(share(info, sources), 'expert', 0, 0, tiled=True)  6.9 us
    unnamed x64, local copies, waits for them, and re-layouts  4.19 us
  transfers between devices with their start and end apart: 29, of which 7 were waited for; matrix products, arithmetic and copies ran while one was open for 1% of the time, Pallas kernels for 42%

profile of v3, /device:TPU:0, one launch (start us, length us, event | category | flops | bytes accessed | tf_op | source)
XLA Modules:
  0.0 149.9 jit_solution(17085707351317876010)
XLA Ops:
  1.7 2.9 %collective-permute-start.1 = (bf16[128,1024]{1,0:T(8,128)(2,1)S(1)}, bf16[128,1024]{1,0:T(8,128)(2,1)S(1)}, u32[]{:S(2)}, u32[]{:S(2)}) collective-permute-start(bf16[128,1024]{1,0:T(8,128)(2,1)S(1)} %get-tuple-element.176), channel_id=1, source_target_pairs={{0,3},{1,2},{2,1},{3,0},{4,7},{5,6},{6,5},{7,4},{8,11},{9,10},{10,... | collective-permute-start | bytes 786440 | tf_op jit(solution)/shard_map/ppermute | solution.py:57
  5.1 5.9 %collective-permute-done.refs_1_.refs_2_ = bf16[128,1024]{1,0:T(8,128)(2,1)S(1)} collective-permute-done((bf16[128,1024]{1,0:T(8,128)(2,1)S(1)}, bf16[128,1024]{1,0:T(8,128)(2,1)S(1)}, u32[]{:S(2)}, u32[]{:S(2)}) %collective-permute-start) | collective-permute-done | bytes 262176 | tf_op jit(solution)/shard_map/ppermute | solution.py:57
  11.0 1.2 copy-done
  14.1 1.1 collective-permute-start.2
  17.7 6.9 %all-to-all-start = ((bf16[16,16,128]{2,1,0:T(8,128)(2,1)}), bf16[16,16,128]{2,1,0:T(8,128)(2,1)S(1)}, u32[]{:S(2)}, u32[]{:S(2)}) async-start(bf16[16,16,128]{2,1,0:T(8,128)(2,1)} %get-tuple-element.100), calls=%async_computation | async-start | bytes 131072 | tf_op jit(solution)/shard_map/all_to_all | solution.py:540
  24.6 3.1 %collective-permute-start.5 = (bf16[128,1024]{1,0:T(8,128)(2,1)}, bf16[128,1024]{1,0:T(8,128)(2,1)S(1)}, u32[]{:S(2)}, u32[]{:S(2)}) collective-permute-start(bf16[128,1024]{1,0:T(8,128)(2,1)} %copy-done.23), channel_id=1, source_target_pairs={{0,3},{1,2},{2,1},{3,0},{4,7},{5,6},{6,5},{7,4},{8,11},{9,10},{10,... | collective-permute-start | bytes 786440 | tf_op jit(solution)/shard_map/ppermute | solution.py:57
  30.9 1.8 %collective-permute-done.5.refs_2_.refs_3_ = bf16[128,1024]{1,0:T(8,128)(2,1)S(1)} collective-permute-done((bf16[128,1024]{1,0:T(8,128)(2,1)}, bf16[128,1024]{1,0:T(8,128)(2,1)S(1)}, u32[]{:S(2)}, u32[]{:S(2)}) %collective-permute-start.5) | collective-permute-done | bytes 262176 | tf_op jit(solution)/shard_map/ppermute | solution.py:57
  34.2 2.7 %collective-permute-start.9 = (bf16[512,1024]{1,0:T(8,128)(2,1)}, bf16[512,1024]{1,0:T(8,128)(2,1)}, u32[]{:S(2)}, u32[]{:S(2)}) collective-permute-start(bf16[512,1024]{1,0:T(8,128)(2,1)} %get-tuple-element.112.refs_1_), channel_id=1, source_target_pairs={{0,12},{1,13},{2,14},{3,15},{4,8},{5,9},{6,10},{7,11},{8,4},{9,5},... | collective-permute-start | bytes 3145736 | tf_op jit(solution)/shard_map/ppermute | solution.py:57
  38.2 1.5 shard_map.86
  39.6 5.0 %collective-permute-done.6.refs_3_.refs_4_ = bf16[256,1024]{1,0:T(8,128)(2,1)} collective-permute-done((bf16[256,1024]{1,0:T(8,128)(2,1)}, bf16[256,1024]{1,0:T(8,128)(2,1)}, u32[]{:S(2)}, u32[]{:S(2)}) %collective-permute-start.6) | collective-permute-done | bytes 524320 | tf_op jit(solution)/shard_map/ppermute | solution.py:57
  44.6 1.1 shard_map.87
  45.8 3.0 %collective-permute-done.7.refs_2_.refs_4_ = bf16[256,1024]{1,0:T(8,128)(2,1)} collective-permute-done((bf16[256,1024]{1,0:T(8,128)(2,1)}, bf16[256,1024]{1,0:T(8,128)(2,1)}, u32[]{:S(2)}, u32[]{:S(2)}) %collective-permute-start.7) | collective-permute-done | bytes 524320 | tf_op jit(solution)/shard_map/ppermute | solution.py:57
  48.7 1.1 shard_map.88
  49.8 3.0 %collective-permute-start.11 = (bf16[512,1024]{1,0:T(8,128)(2,1)S(1)}, bf16[512,1024]{1,0:T(8,128)(2,1)S(1)}, u32[]{:S(2)}, u32[]{:S(2)}) collective-permute-start(bf16[512,1024]{1,0:T(8,128)(2,1)S(1)} %get-tuple-element.119.refs_1_), channel_id=1, source_target_pairs={{0,12},{1,13},{2,14},{3,15},{4,8},{5,9},{6,10},{7,11},{8,4},{9,5},... | collective-permute-start | bytes 3145736 | tf_op jit(solution)/shard_map/ppermute | solution.py:57
  53.1 3.2 %shard_map.89 = (bf16[2,320,1024]{2,1,0:T(8,128)(2,1)S(1)}, bf16[2,320,1024]{2,1,0:T(8,128)(2,1)S(1)}, f32[8,128]{1,0:T(8,128)S(1)}) custom-call(f32[8,128]{1,0:T(8,128)S(1)} %get-tuple-element.108.refs_0_, bf16[512,1024]{1,0:T(8,128)(2,1)} %get-tuple-element.109.refs_1_, bf16[512,1024]{1,0:T(8,128)(2,1)} %collective-permute-done.8.refs_2_, ...), custom_call_target="tpu_custom_call" | custom-call | flops 20000000000 | tf_op jit(solution)/shard_map/pallas_call | solution.py:79
  56.4 3.2 %shard_map.90 = (bf16[2,320,1024]{2,1,0:T(8,128)(2,1)S(1)}, bf16[2,320,1024]{2,1,0:T(8,128)(2,1)S(1)}, f32[8,128]{1,0:T(8,128)S(1)}) custom-call(f32[8,128]{1,0:T(8,128)S(1)} %get-tuple-element.111.refs_0_, bf16[512,1024]{1,0:T(8,128)(2,1)} %get-tuple-element.112.refs_1_, bf16[512,1024]{1,0:T(8,128)(2,1)} %collective-permute-done.9.refs_2_, ...), custom_call_target="tpu_custom_call" | custom-call | flops 20000000000 | tf_op jit(solution)/shard_map/pallas_call | solution.py:79
  59.6 1.9 %collective-permute-start.13 = (bf16[2,320,1024]{2,1,0:T(8,128)(2,1)S(1)}, bf16[2,320,1024]{2,1,0:T(8,128)(2,1)S(1)}, u32[]{:S(2)}, u32[]{:S(2)}) collective-permute-start(bf16[2,320,1024]{2,1,0:T(8,128)(2,1)S(1)} %get-tuple-element.129), channel_id=1, source_target_pairs={{0,4},{1,5},{2,6},{3,7},{4,0},{5,1},{6,2},{7,3},{8,12},{9,13},{10,... | collective-permute-start | bytes 3932168 | tf_op jit(solution)/shard_map/ppermute | solution.py:57
  61.7 3.9 %shard_map.91 = (f32[2,640,768]{2,1,0:T(8,128)S(1)}, f32[8,128]{1,0:T(8,128)S(1)}) custom-call(f32[8,128]{1,0:T(8,128)S(1)} %get-tuple-element.113.refs_0_, bf16[2,320,1024]{2,1,0:T(8,128)(2,1)S(1)} %get-tuple-element.114.refs_1_, bf16[2,320,1024]{2,1,0:T(8,128)(2,1)S(1)} %get-tuple-element.115.refs_2_.refs_1_, bf16[2,768,4096]{2,1,0:T(8,128)(2,1)S(1)} %bitcast.14), custom_call_target="tpu_custom_call" | custom-call | flops 20000000000 | tf_op jit(solution)/shard_map/pallas_call | solution.py:79
  65.7 1.9 %copy-done.24 = f32[2,640,768]{2,1,0:T(8,128)} copy-done((f32[2,640,768]{2,1,0:T(8,128)}, f32[2,640,768]{2,1,0:T(8,128)S(1)}, u32[]{:S(2)}) %copy-start.24) | copy-done | bytes 3932184
  67.6 1.5 %shard_map.92 = (bf16[2,320,1024]{2,1,0:T(8,128)(2,1)S(1)}, bf16[2,320,1024]{2,1,0:T(8,128)(2,1)S(1)}, f32[8,128]{1,0:T(8,128)S(1)}) custom-call(f32[8,128]{1,0:T(8,128)S(1)} %get-tuple-element.116.refs_0_, bf16[512,1024]{1,0:T(8,128)(2,1)S(1)} %get-tuple-element.117.refs_1_, bf16[512,1024]{1,0:T(8,128)(2,1)S(1)} %collective-permute-done.10.refs_2_, ...), custom_call_target="tpu_custom_call" | custom-call | flops 20000000000 | tf_op jit(solution)/shard_map/pallas_call | solution.py:79
  69.2 2.1 %shard_map.93 = (bf16[2,320,1024]{2,1,0:T(8,128)(2,1)S(1)}, bf16[2,320,1024]{2,1,0:T(8,128)(2,1)}, f32[8,128]{1,0:T(8,128)S(1)}) custom-call(f32[8,128]{1,0:T(8,128)S(1)} %get-tuple-element.118.refs_0_, bf16[512,1024]{1,0:T(8,128)(2,1)S(1)} %get-tuple-element.119.refs_1_, bf16[512,1024]{1,0:T(8,128)(2,1)S(1)} %collective-permute-done.11.refs_2_, ...), custom_call_target="tpu_custom_call" | custom-call | flops 20000000000 | tf_op jit(solution)/shard_map/pallas_call | solution.py:79
  71.8 2.4 %collective-permute-start.16 = (bf16[2,320,1024]{2,1,0:T(8,128)(2,1)S(1)}, bf16[2,320,1024]{2,1,0:T(8,128)(2,1)S(1)}, u32[]{:S(2)}, u32[]{:S(2)}) collective-permute-start(bf16[2,320,1024]{2,1,0:T(8,128)(2,1)S(1)} %get-tuple-element.139), channel_id=1, source_target_pairs={{0,12},{1,13},{2,14},{3,15},{4,8},{5,9},{6,10},{7,11},{8,4},{9,5},... | collective-permute-start | bytes 3932168 | tf_op jit(solution)/shard_map/ppermute | solution.py:57
  74.2 3.9 %shard_map.94 = (f32[2,640,768]{2,1,0:T(8,128)S(1)}, f32[8,128]{1,0:T(8,128)S(1)}) custom-call(f32[8,128]{1,0:T(8,128)S(1)} %get-tuple-element.120.refs_0_, bf16[2,320,1024]{2,1,0:T(8,128)(2,1)S(1)} %get-tuple-element.121.refs_1_, bf16[2,320,1024]{2,1,0:T(8,128)(2,1)S(1)} %get-tuple-element.122.refs_2_.refs_1_, bf16[2,768,4096]{2,1,0:T(8,128)(2,1)S(1)} %bitcast.14), custom_call_target="tpu_custom_call" | custom-call | flops 20000000000 | tf_op jit(solution)/shard_map/pallas_call | solution.py:79
  78.1 2.1 %collective-permute-done.12.refs_2_.refs_7_ = bf16[2,320,1024]{2,1,0:T(8,128)(2,1)S(1)} collective-permute-done((bf16[2,320,1024]{2,1,0:T(8,128)(2,1)S(1)}, bf16[2,320,1024]{2,1,0:T(8,128)(2,1)S(1)}, u32[]{:S(2)}, u32[]{:S(2)}) %collective-permute-start.12) | collective-permute-done | bytes 1310752 | tf_op jit(solution)/shard_map/ppermute | solution.py:57
  80.2 1.4 shard_map.95
  81.8 1.4 shard_map.96
  83.2 1.4 shard_map.97
  85.2 1.4 shard_map.98
  86.6 1.2 shard_map.99
  88.0 1.9 %collective-permute-start.20 = (bf16[2,2,96,1024]{3,2,1,0:T(8,128)(2,1)}, bf16[2,2,96,1024]{3,2,1,0:T(8,128)(2,1)}, u32[]{:S(2)}, u32[]{:S(2)}) collective-permute-start(bf16[2,2,96,1024]{3,2,1,0:T(8,128)(2,1)} %get-tuple-element.157), channel_id=1, source_target_pairs={{0,32},{1,33},{2,34},{3,35},{4,36},{5,37},{6,38},{7,39},{8,40},{9,... | collective-permute-start | bytes 2359304 | tf_op jit(solution)/shard_map/ppermute | solution.py:57
  89.9 1.1 shard_map.100
  91.0 2.5 %collective-permute-start.21 = (bf16[2,2,96,1024]{3,2,1,0:T(8,128)(2,1)}, bf16[2,2,96,1024]{3,2,1,0:T(8,128)(2,1)S(1)}, u32[]{:S(2)}, u32[]{:S(2)}) collective-permute-start(bf16[2,2,96,1024]{3,2,1,0:T(8,128)(2,1)} %get-tuple-element.159), channel_id=1, source_target_pairs={{0,96},{1,97},{2,98},{3,99},{4,100},{5,101},{6,102},{7,103},{8,104... | collective-permute-start | bytes 2359304 | tf_op jit(solution)/shard_map/ppermute | solution.py:57
  94.3 1.4 shard_map.101
  96.0 2.7 %shard_map.102 = (bf16[2,640,1024]{2,1,0:T(8,128)(2,1)S(1)}, bf16[4,2,96,1024]{3,2,1,0:T(8,128)(2,1)S(1)}, f32[8,128]{1,0:T(8,128)S(1)}) custom-call(f32[8,128]{1,0:T(8,128)S(1)} %get-tuple-element.140.refs_0_, bf16[2,320,1024]{2,1,0:T(8,128)(2,1)S(1)} %get-tuple-element.122.refs_2_.refs_1_, bf16[2,320,1024]{2,1,0:T(8,128)(2,1)} %collective-permute-done.17.refs_2_.refs_10_, ...), custom_call_target="tpu_custom_call" | custom-call | flops 20000000000 | tf_op jit(solution)/shard_map/pallas_call | solution.py:79
  99.3 1.4 shard_map.103
  100.7 1.4 shard_map.104
  102.1 1.3 shard_map.105
  103.4 1.9 %collective-permute-start.22 = (bf16[2,2,96,1024]{3,2,1,0:T(8,128)(2,1)}, bf16[2,2,96,1024]{3,2,1,0:T(8,128)(2,1)}, u32[]{:S(2)}, u32[]{:S(2)}) collective-permute-start(bf16[2,2,96,1024]{3,2,1,0:T(8,128)(2,1)} %get-tuple-element.161), channel_id=1, source_target_pairs={{0,32},{1,33},{2,34},{3,35},{4,36},{5,37},{6,38},{7,39},{8,40},{9,... | collective-permute-start | bytes 2359304 | tf_op jit(solution)/shard_map/ppermute | solution.py:57
  106.4 2.5 %collective-permute-start.23 = (bf16[2,2,96,1024]{3,2,1,0:T(8,128)(2,1)}, bf16[2,2,96,1024]{3,2,1,0:T(8,128)(2,1)}, u32[]{:S(2)}, u32[]{:S(2)}) collective-permute-start(bf16[2,2,96,1024]{3,2,1,0:T(8,128)(2,1)} %get-tuple-element.163), channel_id=1, source_target_pairs={{0,96},{1,97},{2,98},{3,99},{4,100},{5,101},{6,102},{7,103},{8,104... | collective-permute-start | bytes 2359304 | tf_op jit(solution)/shard_map/ppermute | solution.py:57
  109.0 14.8 %shard_map.107 = (bf16[2,16,40,768]{3,2,1,0:T(8,128)(2,1)}, f32[16,2,128]{2,1,0:T(2,128)S(1)}, f32[8,128]{1,0:T(8,128)S(1)}) custom-call(f32[8,128]{1,0:T(8,128)S(1)} %get-tuple-element.152.refs_0_, s32[32]{0:T(128)S(1)} %pad_add_fusion.1.refs_1_, f32[32,128]{1,0:T(8,128)S(1)} %copy-done.12, f32[32,128]{1,0:T(8,128)S(1)} %copy-done.14, ...), custom_call_target="tpu_custom_call" | custom-call | flops 20000000000 | tf_op jit(solution)/shard_map/pallas_call | solution.py:79
  123.8 1.1 shard_map.108
  125.2 1.1 collective-permute-start.25
  126.2 1.9 %collective-permute-start.24 = (bf16[1,2,96,1024]{3,2,1,0:T(8,128)(2,1)S(1)}, bf16[1,2,96,1024]{3,2,1,0:T(8,128)(2,1)S(1)}, u32[]{:S(2)}, u32[]{:S(2)}) collective-permute-start(bf16[1,2,96,1024]{3,2,1,0:T(8,128)(2,1)S(1)} %get-tuple-element.165), channel_id=1, source_target_pairs={{0,96},{1,97},{2,98},{3,99},{4,100},{5,101},{6,102},{7,103},{8,104... | collective-permute-start | bytes 1179656 | tf_op jit(solution)/shard_map/ppermute | solution.py:57
  128.1 1.3 shard_map.110
  129.4 1.4 collective-permute-start.26
  130.8 1.2 shard_map.111
  132.1 13.5 %all_to_all.10 = f32[16,2,128]{2,1,0:T(2,128)S(1)} all-to-all(f32[16,2,128]{2,1,0:T(2,128)S(1)} %get-tuple-element.170), channel_id=1, replica_groups=mesh['section'=8,'expert'=16] {'expert'}, dimensions={0} | all-to-all | bytes 32768 | tf_op jit(solution)/shard_map/all_to_all | solution.py:574
  146.5 3.4 %shard_map.112 = (bf16[2,96,4096]{2,1,0:T(8,128)(2,1)}, f32[8,128]{1,0:T(8,128)}) custom-call(f32[8,128]{1,0:T(8,128)S(1)} %get-tuple-element.164.refs_0_, bf16[4,2,96,1024]{3,2,1,0:T(8,128)(2,1)S(1)} %copy-done.6, bf16[4,2,96,1024]{3,2,1,0:T(8,128)(2,1)S(1)} %copy-done.4, bf16[2,2,96,1024]{3,2,1,0:T(8,128)(2,1)} %collective-permute-done.20.refs_3_, ...), custom_call_target="tpu_custom_call" | custom-call | flops 20000000000 | tf_op jit(solution)/shard_map/pallas_call | solution.py:79
  (126 shorter events, 17.5 us)
Async XLA Ops:
  1.7 11.4 %collective-permute-start.1 = (bf16[128,1024]{1,0:T(8,128)(2,1)S(1)}, bf16[128,1024]{1,0:T(8,128)(2,1)S(1)}, u32[]{:S(2)}, u32[]{:S(2)}) collective-permute-start(bf16[128,1024]{1,0:T(8,128)(2,1)S(1)} %get-tuple-element.176), channel_id=1, source_target_pairs={{0,3},{1,2},{2,1},{3,0},{4,7},{5,6},{6,5},{7,4},{8,11},{9,10},{10,... | collective-permute-start | bytes 786440 | tf_op jit(solution)/shard_map/ppermute | solution.py:57
  4.6 6.4 %collective-permute-start = (bf16[128,1024]{1,0:T(8,128)(2,1)S(1)}, bf16[128,1024]{1,0:T(8,128)(2,1)S(1)}, u32[]{:S(2)}, u32[]{:S(2)}) collective-permute-start(bf16[128,1024]{1,0:T(8,128)(2,1)S(1)} %get-tuple-element.177), channel_id=1, source_target_pairs={{0,1},{1,0},{2,3},{3,2},{4,5},{5,4},{6,7},{7,6},{8,9},{9,8},{10,11... | collective-permute-start | bytes 786440 | tf_op jit(solution)/shard_map/ppermute | solution.py:57
  13.1 3.2 %copy-start.26 = (s32[128,8]{0,1:T(8,128)S(1)}, s32[128,8]{0,1:T(8,128)}, u32[]{:S(2)}) copy-start(s32[128,8]{0,1:T(8,128)} %param.7) | copy-start | bytes 12292
  13.9 14.9 %collective-permute-start.3 = (bf16[256,1024]{1,0:T(8,128)(2,1)}, bf16[256,1024]{1,0:T(8,128)(2,1)S(1)}, u32[]{:S(2)}, u32[]{:S(2)}) collective-permute-start(bf16[256,1024]{1,0:T(8,128)(2,1)} %get-tuple-element.94), channel_id=1, source_target_pairs={{0,1},{1,0},{2,3},{3,2},{4,5},{5,4},{6,7},{7,6},{8,9},{9,8},{10,11... | collective-permute-start | bytes 1572872 | tf_op jit(solution)/shard_map/ppermute | solution.py:57
  14.1 13.7 %collective-permute-start.2 = (bf16[256,1024]{1,0:T(8,128)(2,1)}, bf16[256,1024]{1,0:T(8,128)(2,1)S(1)}, u32[]{:S(2)}, u32[]{:S(2)}) collective-permute-start(bf16[256,1024]{1,0:T(8,128)(2,1)} %get-tuple-element.92), channel_id=1, source_target_pairs={{0,3},{1,2},{2,1},{3,0},{4,7},{5,6},{6,5},{7,4},{8,11},{9,10},{10,... | collective-permute-start | bytes 1572872 | tf_op jit(solution)/shard_map/ppermute | solution.py:57
  15.3 14.5 %collective-permute-start.4 = (bf16[128,1024]{1,0:T(8,128)(2,1)S(1)}, bf16[128,1024]{1,0:T(8,128)(2,1)S(1)}, u32[]{:S(2)}, u32[]{:S(2)}) collective-permute-start(bf16[128,1024]{1,0:T(8,128)(2,1)S(1)} %get-tuple-element.96), channel_id=1, source_target_pairs={{0,1},{1,0},{2,3},{3,2},{4,5},{5,4},{6,7},{7,6},{8,9},{9,8},{10,11... | collective-permute-start | bytes 786440 | tf_op jit(solution)/shard_map/ppermute | solution.py:57
  17.7 19.4 %all-to-all-start = ((bf16[16,16,128]{2,1,0:T(8,128)(2,1)}), bf16[16,16,128]{2,1,0:T(8,128)(2,1)S(1)}, u32[]{:S(2)}, u32[]{:S(2)}) async-start(bf16[16,16,128]{2,1,0:T(8,128)(2,1)} %get-tuple-element.100), calls=%async_computation | async-start | bytes 131072 | tf_op jit(solution)/shard_map/all_to_all | solution.py:540
  24.6 8.0 %collective-permute-start.5 = (bf16[128,1024]{1,0:T(8,128)(2,1)}, bf16[128,1024]{1,0:T(8,128)(2,1)S(1)}, u32[]{:S(2)}, u32[]{:S(2)}) collective-permute-start(bf16[128,1024]{1,0:T(8,128)(2,1)} %copy-done.23), channel_id=1, source_target_pairs={{0,3},{1,2},{2,1},{3,0},{4,7},{5,6},{6,5},{7,4},{8,11},{9,10},{10,... | collective-permute-start | bytes 786440 | tf_op jit(solution)/shard_map/ppermute | solution.py:57
  30.7 13.9 %collective-permute-start.6 = (bf16[256,1024]{1,0:T(8,128)(2,1)}, bf16[256,1024]{1,0:T(8,128)(2,1)}, u32[]{:S(2)}, u32[]{:S(2)}) collective-permute-start(bf16[256,1024]{1,0:T(8,128)(2,1)} %get-tuple-element.105), channel_id=1, source_target_pairs={{0,3},{1,2},{2,1},{3,0},{4,7},{5,6},{6,5},{7,4},{8,11},{9,10},{10,... | collective-permute-start | bytes 1572872 | tf_op jit(solution)/shard_map/ppermute | solution.py:57
  32.7 5.5 %copy-start.2 = (bf16[1,2,16,40,768]{4,3,2,1,0:T(8,128)(2,1)S(1)}, bf16[1,2,16,40,768]{4,3,2,1,0:T(8,128)(2,1)}, u32[]{:S(2)}) copy-start(bf16[1,2,16,40,768]{4,3,2,1,0:T(8,128)(2,1)} %param.8) | copy-start | bytes 5898244
  33.5 15.2 %collective-permute-start.7 = (bf16[256,1024]{1,0:T(8,128)(2,1)}, bf16[256,1024]{1,0:T(8,128)(2,1)}, u32[]{:S(2)}, u32[]{:S(2)}) collective-permute-start(bf16[256,1024]{1,0:T(8,128)(2,1)} %get-tuple-element.107), channel_id=1, source_target_pairs={{0,1},{1,0},{2,3},{3,2},{4,5},{5,4},{6,7},{7,6},{8,9},{9,8},{10,11... | collective-permute-start | bytes 1572872 | tf_op jit(solution)/shard_map/ppermute | solution.py:57
  34.2 22.2 %collective-permute-start.9 = (bf16[512,1024]{1,0:T(8,128)(2,1)}, bf16[512,1024]{1,0:T(8,128)(2,1)}, u32[]{:S(2)}, u32[]{:S(2)}) collective-permute-start(bf16[512,1024]{1,0:T(8,128)(2,1)} %get-tuple-element.112.refs_1_), channel_id=1, source_target_pairs={{0,12},{1,13},{2,14},{3,15},{4,8},{5,9},{6,10},{7,11},{8,4},{9,5},... | collective-permute-start | bytes 3145736 | tf_op jit(solution)/shard_map/ppermute | solution.py:57
  36.9 16.2 %collective-permute-start.8 = (bf16[512,1024]{1,0:T(8,128)(2,1)}, bf16[512,1024]{1,0:T(8,128)(2,1)}, u32[]{:S(2)}, u32[]{:S(2)}) collective-permute-start(bf16[512,1024]{1,0:T(8,128)(2,1)} %get-tuple-element.109.refs_1_), channel_id=1, source_target_pairs={{0,4},{1,5},{2,6},{3,7},{4,0},{5,1},{6,2},{7,3},{8,12},{9,13},{10,... | collective-permute-start | bytes 3145736 | tf_op jit(solution)/shard_map/ppermute | solution.py:57
  38.1 7.6 %copy-start.11 = (f32[32,128]{1,0:T(8,128)}, f32[32,128]{1,0:T(8,128)S(1)}, u32[]{:S(2)}) copy-start(f32[32,128]{1,0:T(8,128)S(1)} %get-tuple-element.102.refs_2_) | copy-start | bytes 49156
  38.1 7.6 %copy-start.13 = (f32[32,128]{1,0:T(8,128)}, f32[32,128]{1,0:T(8,128)S(1)}, u32[]{:S(2)}) copy-start(f32[32,128]{1,0:T(8,128)S(1)} %get-tuple-element.103.refs_3_) | copy-start | bytes 49156
  44.6 4.1 %copy-start.22 = (bf16[128,1024]{1,0:T(8,128)(2,1)S(1)}, bf16[128,1024]{1,0:T(8,128)(2,1)}, u32[]{:S(2)}) copy-start(bf16[128,1024]{1,0:T(8,128)(2,1)} %copy-done.21) | copy-start | bytes 786436
  49.8 19.3 %collective-permute-start.11 = (bf16[512,1024]{1,0:T(8,128)(2,1)S(1)}, bf16[512,1024]{1,0:T(8,128)(2,1)S(1)}, u32[]{:S(2)}, u32[]{:S(2)}) collective-permute-start(bf16[512,1024]{1,0:T(8,128)(2,1)S(1)} %get-tuple-element.119.refs_1_), channel_id=1, source_target_pairs={{0,12},{1,13},{2,14},{3,15},{4,8},{5,9},{6,10},{7,11},{8,4},{9,5},... | collective-permute-start | bytes 3145736 | tf_op jit(solution)/shard_map/ppermute | solution.py:57
  52.8 14.8 %collective-permute-start.10 = (bf16[512,1024]{1,0:T(8,128)(2,1)S(1)}, bf16[512,1024]{1,0:T(8,128)(2,1)S(1)}, u32[]{:S(2)}, u32[]{:S(2)}) collective-permute-start(bf16[512,1024]{1,0:T(8,128)(2,1)S(1)} %get-tuple-element.117.refs_1_), channel_id=1, source_target_pairs={{0,4},{1,5},{2,6},{3,7},{4,0},{5,1},{6,2},{7,3},{8,12},{9,13},{10,... | collective-permute-start | bytes 3145736 | tf_op jit(solution)/shard_map/ppermute | solution.py:57
  53.1 8.6 %slice-start = ((s8[12582912]{0:T(1024)(128)(4,1)}), s8[4194304]{0:T(1024)(128)(4,1)S(1)}, s32[]{:S(2)}) async-start(s8[12582912]{0:T(1024)(128)(4,1)} %bitcast.13), calls=%async_computation.2 | async-start | bytes 8388608
  53.1 8.6 %slice-start.1 = ((s8[12582912]{0:T(1024)(128)(4,1)}), s8[4194304]{0:T(1024)(128)(4,1)S(1)}, s32[]{:S(2)}) async-start(s8[12582912]{0:T(1024)(128)(4,1)} %bitcast.13), calls=%async_computation.3 | async-start | bytes 8388608
  56.3 5.4 %slice-start.2 = ((s8[12582912]{0:T(1024)(128)(4,1)}), s8[4194304]{0:T(1024)(128)(4,1)S(1)}, s32[]{:S(2)}) async-start(s8[12582912]{0:T(1024)(128)(4,1)} %bitcast.13), calls=%async_computation.4 | async-start | bytes 8388608
  59.6 23.6 %collective-permute-start.13 = (bf16[2,320,1024]{2,1,0:T(8,128)(2,1)S(1)}, bf16[2,320,1024]{2,1,0:T(8,128)(2,1)S(1)}, u32[]{:S(2)}, u32[]{:S(2)}) collective-permute-start(bf16[2,320,1024]{2,1,0:T(8,128)(2,1)S(1)} %get-tuple-element.129), channel_id=1, source_target_pairs={{0,4},{1,5},{2,6},{3,7},{4,0},{5,1},{6,2},{7,3},{8,12},{9,13},{10,... | collective-permute-start | bytes 3932168 | tf_op jit(solution)/shard_map/ppermute | solution.py:57
  61.4 18.8 %collective-permute-start.12 = (bf16[2,320,1024]{2,1,0:T(8,128)(2,1)S(1)}, bf16[2,320,1024]{2,1,0:T(8,128)(2,1)S(1)}, u32[]{:S(2)}, u32[]{:S(2)}) collective-permute-start(bf16[2,320,1024]{2,1,0:T(8,128)(2,1)S(1)} %get-tuple-element.124), channel_id=1, source_target_pairs={{0,12},{1,13},{2,14},{3,15},{4,8},{5,9},{6,10},{7,11},{8,4},{9,5},... | collective-permute-start | bytes 3932168 | tf_op jit(solution)/shard_map/ppermute | solution.py:57
  71.3 24.7 %collective-permute-start.17 = (bf16[2,320,1024]{2,1,0:T(8,128)(2,1)}, bf16[2,320,1024]{2,1,0:T(8,128)(2,1)}, u32[]{:S(2)}, u32[]{:S(2)}) collective-permute-start(bf16[2,320,1024]{2,1,0:T(8,128)(2,1)} %get-tuple-element.141), channel_id=1, source_target_pairs={{0,4},{1,5},{2,6},{3,7},{4,0},{5,1},{6,2},{7,3},{8,12},{9,13},{10,... | collective-permute-start | bytes 3932168 | tf_op jit(solution)/shard_map/ppermute | solution.py:57
  71.8 22.5 %collective-permute-start.16 = (bf16[2,320,1024]{2,1,0:T(8,128)(2,1)S(1)}, bf16[2,320,1024]{2,1,0:T(8,128)(2,1)S(1)}, u32[]{:S(2)}, u32[]{:S(2)}) collective-permute-start(bf16[2,320,1024]{2,1,0:T(8,128)(2,1)S(1)} %get-tuple-element.139), channel_id=1, source_target_pairs={{0,12},{1,13},{2,14},{3,15},{4,8},{5,9},{6,10},{7,11},{8,4},{9,5},... | collective-permute-start | bytes 3932168 | tf_op jit(solution)/shard_map/ppermute | solution.py:57
  78.1 3.5 %copy-start.25 = (f32[2,640,768]{2,1,0:T(8,128)}, f32[2,640,768]{2,1,0:T(8,128)S(1)}, u32[]{:S(2)}) copy-start(f32[2,640,768]{2,1,0:T(8,128)S(1)} %get-tuple-element.154.refs_6_) | copy-start | bytes 11796484
  81.7 4.9 %collective-permute-start.14 = (bf16[4,2,96,1024]{3,2,1,0:T(8,128)(2,1)S(1)}, bf16[4,2,96,1024]{3,2,1,0:T(8,128)(2,1)S(1)}, u32[]{:S(2)}, u32[]{:S(2)}) collective-permute-start(bf16[4,2,96,1024]{3,2,1,0:T(8,128)(2,1)S(1)} %get-tuple-element.134), channel_id=1, source_target_pairs={{0,16},{1,17},{2,18},{3,19},{4,20},{5,21},{6,22},{7,23},{8,24},{9,... | collective-permute-start | bytes 4718600 | tf_op jit(solution)/shard_map/ppermute | solution.py:57
  83.1 3.4 %copy-start.5 = (bf16[4,2,96,1024]{3,2,1,0:T(8,128)(2,1)}, bf16[4,2,96,1024]{3,2,1,0:T(8,128)(2,1)S(1)}, u32[]{:S(2)}) copy-start(bf16[4,2,96,1024]{3,2,1,0:T(8,128)(2,1)S(1)} %get-tuple-element.133.refs_1_.refs_3_) | copy-start | bytes 4718596
  84.6 5.4 %collective-permute-start.15 = (bf16[4,2,96,1024]{3,2,1,0:T(8,128)(2,1)S(1)}, bf16[4,2,96,1024]{3,2,1,0:T(8,128)(2,1)S(1)}, u32[]{:S(2)}, u32[]{:S(2)}) collective-permute-start(bf16[4,2,96,1024]{3,2,1,0:T(8,128)(2,1)S(1)} %get-tuple-element.137), channel_id=1, source_target_pairs={{0,16},{1,17},{2,18},{3,19},{4,20},{5,21},{6,22},{7,23},{8,24},{9,... | collective-permute-start | bytes 4718600 | tf_op jit(solution)/shard_map/ppermute | solution.py:57
  88.0 35.8 %collective-permute-start.20 = (bf16[2,2,96,1024]{3,2,1,0:T(8,128)(2,1)}, bf16[2,2,96,1024]{3,2,1,0:T(8,128)(2,1)}, u32[]{:S(2)}, u32[]{:S(2)}) collective-permute-start(bf16[2,2,96,1024]{3,2,1,0:T(8,128)(2,1)} %get-tuple-element.157), channel_id=1, source_target_pairs={{0,32},{1,33},{2,34},{3,35},{4,36},{5,37},{6,38},{7,39},{8,40},{9,... | collective-permute-start | bytes 2359304 | tf_op jit(solution)/shard_map/ppermute | solution.py:57
  91.0 34.0 %collective-permute-start.21 = (bf16[2,2,96,1024]{3,2,1,0:T(8,128)(2,1)}, bf16[2,2,96,1024]{3,2,1,0:T(8,128)(2,1)S(1)}, u32[]{:S(2)}, u32[]{:S(2)}) collective-permute-start(bf16[2,2,96,1024]{3,2,1,0:T(8,128)(2,1)} %get-tuple-element.159), channel_id=1, source_target_pairs={{0,96},{1,97},{2,98},{3,99},{4,100},{5,101},{6,102},{7,103},{8,104... | collective-permute-start | bytes 2359304 | tf_op jit(solution)/shard_map/ppermute | solution.py:57
  95.7 6.4 %collective-permute-start.18 = (bf16[4,2,96,1024]{3,2,1,0:T(8,128)(2,1)S(1)}, bf16[4,2,96,1024]{3,2,1,0:T(8,128)(2,1)S(1)}, u32[]{:S(2)}, u32[]{:S(2)}) collective-permute-start(bf16[4,2,96,1024]{3,2,1,0:T(8,128)(2,1)S(1)} %get-tuple-element.148), channel_id=1, source_target_pairs={{0,16},{1,17},{2,18},{3,19},{4,20},{5,21},{6,22},{7,23},{8,24},{9,... | collective-permute-start | bytes 4718600 | tf_op jit(solution)/shard_map/ppermute | solution.py:57
  98.7 6.6 %collective-permute-start.19 = (bf16[4,2,96,1024]{3,2,1,0:T(8,128)(2,1)S(1)}, bf16[4,2,96,1024]{3,2,1,0:T(8,128)(2,1)S(1)}, u32[]{:S(2)}, u32[]{:S(2)}) collective-permute-start(bf16[4,2,96,1024]{3,2,1,0:T(8,128)(2,1)S(1)} %get-tuple-element.151), channel_id=1, source_target_pairs={{0,16},{1,17},{2,18},{3,19},{4,20},{5,21},{6,22},{7,23},{8,24},{9,... | collective-permute-start | bytes 4718600 | tf_op jit(solution)/shard_map/ppermute | solution.py:57
  102.1 3.2 %copy-start.9 = (bf16[4,2,96,1024]{3,2,1,0:T(8,128)(2,1)}, bf16[4,2,96,1024]{3,2,1,0:T(8,128)(2,1)S(1)}, u32[]{:S(2)}) copy-start(bf16[4,2,96,1024]{3,2,1,0:T(8,128)(2,1)S(1)} %get-tuple-element.150.refs_1_.refs_3_.refs_13_) | copy-start | bytes 4718596
  103.4 24.7 %collective-permute-start.22 = (bf16[2,2,96,1024]{3,2,1,0:T(8,128)(2,1)}, bf16[2,2,96,1024]{3,2,1,0:T(8,128)(2,1)}, u32[]{:S(2)}, u32[]{:S(2)}) collective-permute-start(bf16[2,2,96,1024]{3,2,1,0:T(8,128)(2,1)} %get-tuple-element.161), channel_id=1, source_target_pairs={{0,32},{1,33},{2,34},{3,35},{4,36},{5,37},{6,38},{7,39},{8,40},{9,... | collective-permute-start | bytes 2359304 | tf_op jit(solution)/shard_map/ppermute | solution.py:57
  105.3 3.6 %copy-start.12 = (f32[32,128]{1,0:T(8,128)S(1)}, f32[32,128]{1,0:T(8,128)}, u32[]{:S(2)}) copy-start(f32[32,128]{1,0:T(8,128)} %copy-done.11) | copy-start | bytes 49156
  105.3 3.6 %copy-start.14 = (f32[32,128]{1,0:T(8,128)S(1)}, f32[32,128]{1,0:T(8,128)}, u32[]{:S(2)}) copy-start(f32[32,128]{1,0:T(8,128)} %copy-done.13) | copy-start | bytes 49156
  105.3 3.6 %copy-start.16 = (bf16[2,320,1024]{2,1,0:T(8,128)(2,1)S(1)}, bf16[2,320,1024]{2,1,0:T(8,128)(2,1)}, u32[]{:S(2)}) copy-start(bf16[2,320,1024]{2,1,0:T(8,128)(2,1)} %copy-done.15) | copy-start | bytes 3932164
  105.3 3.6 %copy-start.18 = (bf16[2,320,1024]{2,1,0:T(8,128)(2,1)S(1)}, bf16[2,320,1024]{2,1,0:T(8,128)(2,1)}, u32[]{:S(2)}) copy-start(bf16[2,320,1024]{2,1,0:T(8,128)(2,1)} %copy-done.17) | copy-start | bytes 3932164
  105.4 3.6 %copy-start.20 = (bf16[2,320,1024]{2,1,0:T(8,128)(2,1)S(1)}, bf16[2,320,1024]{2,1,0:T(8,128)(2,1)}, u32[]{:S(2)}) copy-start(bf16[2,320,1024]{2,1,0:T(8,128)(2,1)} %copy-done.19) | copy-start | bytes 3932164
  106.4 24.4 %collective-permute-start.23 = (bf16[2,2,96,1024]{3,2,1,0:T(8,128)(2,1)}, bf16[2,2,96,1024]{3,2,1,0:T(8,128)(2,1)}, u32[]{:S(2)}, u32[]{:S(2)}) collective-permute-start(bf16[2,2,96,1024]{3,2,1,0:T(8,128)(2,1)} %get-tuple-element.163), channel_id=1, source_target_pairs={{0,96},{1,97},{2,98},{3,99},{4,100},{5,101},{6,102},{7,103},{8,104... | collective-permute-start | bytes 2359304 | tf_op jit(solution)/shard_map/ppermute | solution.py:57
  109.0 14.8 %copy-start.4 = (bf16[4,2,96,1024]{3,2,1,0:T(8,128)(2,1)S(1)}, bf16[4,2,96,1024]{3,2,1,0:T(8,128)(2,1)}, u32[]{:S(2)}) copy-start(bf16[4,2,96,1024]{3,2,1,0:T(8,128)(2,1)} %copy-done.3) | copy-start | bytes 4718596
  109.0 14.8 %copy-start.6 = (bf16[4,2,96,1024]{3,2,1,0:T(8,128)(2,1)S(1)}, bf16[4,2,96,1024]{3,2,1,0:T(8,128)(2,1)}, u32[]{:S(2)}) copy-start(bf16[4,2,96,1024]{3,2,1,0:T(8,128)(2,1)} %copy-done.5) | copy-start | bytes 4718596
  125.2 21.1 %collective-permute-start.25 = (bf16[1,2,96,1024]{3,2,1,0:T(8,128)(2,1)S(1)}, bf16[1,2,96,1024]{3,2,1,0:T(8,128)(2,1)S(1)}, u32[]{:S(2)}, u32[]{:S(2)}) collective-permute-start(bf16[1,2,96,1024]{3,2,1,0:T(8,128)(2,1)S(1)} %get-tuple-element.166), channel_id=1, source_target_pairs={{0,32},{1,33},{2,34},{3,35},{4,36},{5,37},{6,38},{7,39},{8,40},{9,... | collective-permute-start | bytes 1179656 | tf_op jit(solution)/shard_map/ppermute | solution.py:57
  126.2 20.0 %collective-permute-start.24 = (bf16[1,2,96,1024]{3,2,1,0:T(8,128)(2,1)S(1)}, bf16[1,2,96,1024]{3,2,1,0:T(8,128)(2,1)S(1)}, u32[]{:S(2)}, u32[]{:S(2)}) collective-permute-start(bf16[1,2,96,1024]{3,2,1,0:T(8,128)(2,1)S(1)} %get-tuple-element.165), channel_id=1, source_target_pairs={{0,96},{1,97},{2,98},{3,99},{4,100},{5,101},{6,102},{7,103},{8,104... | collective-permute-start | bytes 1179656 | tf_op jit(solution)/shard_map/ppermute | solution.py:57
  129.4 17.1 %collective-permute-start.26 = (bf16[1,2,96,1024]{3,2,1,0:T(8,128)(2,1)S(1)}, bf16[1,2,96,1024]{3,2,1,0:T(8,128)(2,1)S(1)}, u32[]{:S(2)}, u32[]{:S(2)}) collective-permute-start(bf16[1,2,96,1024]{3,2,1,0:T(8,128)(2,1)S(1)} %get-tuple-element.167), channel_id=1, source_target_pairs={{0,96},{1,97},{2,98},{3,99},{4,100},{5,101},{6,102},{7,103},{8,104... | collective-permute-start | bytes 1179656 | tf_op jit(solution)/shard_map/ppermute | solution.py:57
  130.8 14.7 %copy-start.27 = (s32[128,8]{0,1:T(8,128)S(1)}, s32[128,8]{0,1:T(8,128)}, u32[]{:S(2)}) copy-start(s32[128,8]{0,1:T(8,128)} %param.7) | copy-start | bytes 12292
  132.0 14.5 %collective-permute-start.27 = (bf16[1,2,96,1024]{3,2,1,0:T(8,128)(2,1)S(1)}, bf16[1,2,96,1024]{3,2,1,0:T(8,128)(2,1)S(1)}, u32[]{:S(2)}, u32[]{:S(2)}) collective-permute-start(bf16[1,2,96,1024]{3,2,1,0:T(8,128)(2,1)S(1)} %get-tuple-element.168), channel_id=1, source_target_pairs={{0,32},{1,33},{2,34},{3,35},{4,36},{5,37},{6,38},{7,39},{8,40},{9,... | collective-permute-start | bytes 1179656 | tf_op jit(solution)/shard_map/ppermute | solution.py:57
  (13 other events, 23.4 us)

commit v4 on v3

--- a/solution.py
+++ b/solution.py
@@ -13,8 +13,8 @@
 END_LIMIT = 46 * 1024 * 1024
 PLAN = (
     "a0", "a1", "o2-", "o3-", "I-", "r0-", "r1-", "a2", "a3", "P-", "T-", "r2", "r3", "p0",
-    "p1", "h0", "p2", "p3", "h1", "w0", "m0", "w1", "m1", "s0", "s1", "w2", "w3", "m2", "m3",
-    "s2", "s3", "H", "t0-", "t1-", "t2-", "t3-", "e",
+    "p1", "h0", "p2", "p3", "h1", "w0", "m0", "w1", "m1", "s0", "s1", "w2", "w3", "m2", "s2",
+    "m3", "s3", "H", "t0-", "t1-", "t2-", "t3-", "e",
 )
 F32, BF16 = jnp.float32, jnp.bfloat16
 

time: 150 us -> 151 us (level)
  no operation moved by 1% of the time
where the time goes in v4:
time: 151 us
  Pallas kernels  67.6 us (45%)
  starting transfers between devices  42.3 us (28%)
  waiting for transfers between devices  19.1 us (13%)
  blocking collectives  13.5 us (9%)
  local copies, waits for them, and re-layouts  5.85 us (4%)
    pallas_call x37, Pallas kernels, call(): pl.pallas_call(run, grid=grid, in_specs=[pl.BlockSpec(memory_space=pltpu....  67.6 us
    ppermute x28, starting transfers between devices, send(): return lax.ppermute(value, AXES, pairs)  35.4 us
    ppermute x28, waiting for transfers between devices, send(): return lax.ppermute(value, AXES, pairs)  19.1 us
    all_to_all x1, blocking collectives, shards(): lax.all_to_all(token_grad, 'expert', 0, 0, tiled=True).reshape(-1, tokens)  13.5 us
    all_to_all x1, starting transfers between devices, shards(): all_info = lax.all_to_all(share(info, sources), 'expert', 0, 0, tiled=True)  6.9 us
    unnamed x64, local copies, waits for them, and re-layouts  4.61 us
  transfers between devices with their start and end apart: 29, of which 7 were waited for; matrix products, arithmetic and copies ran while one was open for 1% of the time, Pallas kernels for 42%

profile of v4, /device:TPU:0, one launch (start us, length us, event | category | flops | bytes accessed | tf_op | source)
XLA Modules:
  0.0 150.6 jit_solution(12652336423333746428)
XLA Ops:
  1.7 2.9 %collective-permute-start.1 = (bf16[128,1024]{1,0:T(8,128)(2,1)S(1)}, bf16[128,1024]{1,0:T(8,128)(2,1)S(1)}, u32[]{:S(2)}, u32[]{:S(2)}) collective-permute-start(bf16[128,1024]{1,0:T(8,128)(2,1)S(1)} %get-tuple-element.176), channel_id=1, source_target_pairs={{0,3},{1,2},{2,1},{3,0},{4,7},{5,6},{6,5},{7,4},{8,11},{9,10},{10,... | collective-permute-start | bytes 786440 | tf_op jit(solution)/shard_map/ppermute | solution.py:57
  5.1 5.9 %collective-permute-done.refs_1_.refs_2_ = bf16[128,1024]{1,0:T(8,128)(2,1)S(1)} collective-permute-done((bf16[128,1024]{1,0:T(8,128)(2,1)S(1)}, bf16[128,1024]{1,0:T(8,128)(2,1)S(1)}, u32[]{:S(2)}, u32[]{:S(2)}) %collective-permute-start) | collective-permute-done | bytes 262176 | tf_op jit(solution)/shard_map/ppermute | solution.py:57
  11.0 1.2 copy-done
  14.1 1.1 collective-permute-start.2
  17.7 6.9 %all-to-all-start = ((bf16[16,16,128]{2,1,0:T(8,128)(2,1)}), bf16[16,16,128]{2,1,0:T(8,128)(2,1)S(1)}, u32[]{:S(2)}, u32[]{:S(2)}) async-start(bf16[16,16,128]{2,1,0:T(8,128)(2,1)} %get-tuple-element.100), calls=%async_computation | async-start | bytes 131072 | tf_op jit(solution)/shard_map/all_to_all | solution.py:540
  24.6 3.1 %collective-permute-start.5 = (bf16[128,1024]{1,0:T(8,128)(2,1)}, bf16[128,1024]{1,0:T(8,128)(2,1)S(1)}, u32[]{:S(2)}, u32[]{:S(2)}) collective-permute-start(bf16[128,1024]{1,0:T(8,128)(2,1)} %copy-done.23), channel_id=1, source_target_pairs={{0,3},{1,2},{2,1},{3,0},{4,7},{5,6},{6,5},{7,4},{8,11},{9,10},{10,... | collective-permute-start | bytes 786440 | tf_op jit(solution)/shard_map/ppermute | solution.py:57
  30.9 1.8 %collective-permute-done.5.refs_2_.refs_3_ = bf16[128,1024]{1,0:T(8,128)(2,1)S(1)} collective-permute-done((bf16[128,1024]{1,0:T(8,128)(2,1)}, bf16[128,1024]{1,0:T(8,128)(2,1)S(1)}, u32[]{:S(2)}, u32[]{:S(2)}) %collective-permute-start.5) | collective-permute-done | bytes 262176 | tf_op jit(solution)/shard_map/ppermute | solution.py:57
  34.2 2.7 %collective-permute-start.9 = (bf16[512,1024]{1,0:T(8,128)(2,1)}, bf16[512,1024]{1,0:T(8,128)(2,1)}, u32[]{:S(2)}, u32[]{:S(2)}) collective-permute-start(bf16[512,1024]{1,0:T(8,128)(2,1)} %get-tuple-element.112.refs_1_), channel_id=1, source_target_pairs={{0,12},{1,13},{2,14},{3,15},{4,8},{5,9},{6,10},{7,11},{8,4},{9,5},... | collective-permute-start | bytes 3145736 | tf_op jit(solution)/shard_map/ppermute | solution.py:57
  38.2 1.5 shard_map.86
  39.6 5.0 %collective-permute-done.6.refs_3_.refs_4_ = bf16[256,1024]{1,0:T(8,128)(2,1)} collective-permute-done((bf16[256,1024]{1,0:T(8,128)(2,1)}, bf16[256,1024]{1,0:T(8,128)(2,1)}, u32[]{:S(2)}, u32[]{:S(2)}) %collective-permute-start.6) | collective-permute-done | bytes 524320 | tf_op jit(solution)/shard_map/ppermute | solution.py:57
  44.6 1.1 shard_map.87
  45.8 3.0 %collective-permute-done.7.refs_2_.refs_4_ = bf16[256,1024]{1,0:T(8,128)(2,1)} collective-permute-done((bf16[256,1024]{1,0:T(8,128)(2,1)}, bf16[256,1024]{1,0:T(8,128)(2,1)}, u32[]{:S(2)}, u32[]{:S(2)}) %collective-permute-start.7) | collective-permute-done | bytes 524320 | tf_op jit(solution)/shard_map/ppermute | solution.py:57
  48.7 1.1 shard_map.88
  49.8 3.0 %collective-permute-start.11 = (bf16[512,1024]{1,0:T(8,128)(2,1)S(1)}, bf16[512,1024]{1,0:T(8,128)(2,1)S(1)}, u32[]{:S(2)}, u32[]{:S(2)}) collective-permute-start(bf16[512,1024]{1,0:T(8,128)(2,1)S(1)} %get-tuple-element.119.refs_1_), channel_id=1, source_target_pairs={{0,12},{1,13},{2,14},{3,15},{4,8},{5,9},{6,10},{7,11},{8,4},{9,5},... | collective-permute-start | bytes 3145736 | tf_op jit(solution)/shard_map/ppermute | solution.py:57
  53.1 3.2 %shard_map.89 = (bf16[2,320,1024]{2,1,0:T(8,128)(2,1)S(1)}, bf16[2,320,1024]{2,1,0:T(8,128)(2,1)S(1)}, f32[8,128]{1,0:T(8,128)S(1)}) custom-call(f32[8,128]{1,0:T(8,128)S(1)} %get-tuple-element.108.refs_0_, bf16[512,1024]{1,0:T(8,128)(2,1)} %get-tuple-element.109.refs_1_, bf16[512,1024]{1,0:T(8,128)(2,1)} %collective-permute-done.8.refs_2_, ...), custom_call_target="tpu_custom_call" | custom-call | flops 20000000000 | tf_op jit(solution)/shard_map/pallas_call | solution.py:79
  56.4 3.2 %shard_map.90 = (bf16[2,320,1024]{2,1,0:T(8,128)(2,1)S(1)}, bf16[2,320,1024]{2,1,0:T(8,128)(2,1)S(1)}, f32[8,128]{1,0:T(8,128)S(1)}) custom-call(f32[8,128]{1,0:T(8,128)S(1)} %get-tuple-element.111.refs_0_, bf16[512,1024]{1,0:T(8,128)(2,1)} %get-tuple-element.112.refs_1_, bf16[512,1024]{1,0:T(8,128)(2,1)} %collective-permute-done.9.refs_2_, ...), custom_call_target="tpu_custom_call" | custom-call | flops 20000000000 | tf_op jit(solution)/shard_map/pallas_call | solution.py:79
  59.6 1.9 %collective-permute-start.13 = (bf16[2,320,1024]{2,1,0:T(8,128)(2,1)S(1)}, bf16[2,320,1024]{2,1,0:T(8,128)(2,1)S(1)}, u32[]{:S(2)}, u32[]{:S(2)}) collective-permute-start(bf16[2,320,1024]{2,1,0:T(8,128)(2,1)S(1)} %get-tuple-element.129), channel_id=1, source_target_pairs={{0,4},{1,5},{2,6},{3,7},{4,0},{5,1},{6,2},{7,3},{8,12},{9,13},{10,... | collective-permute-start | bytes 3932168 | tf_op jit(solution)/shard_map/ppermute | solution.py:57
  61.7 3.9 %shard_map.91 = (f32[2,640,768]{2,1,0:T(8,128)S(1)}, f32[8,128]{1,0:T(8,128)S(1)}) custom-call(f32[8,128]{1,0:T(8,128)S(1)} %get-tuple-element.113.refs_0_, bf16[2,320,1024]{2,1,0:T(8,128)(2,1)S(1)} %get-tuple-element.114.refs_1_, bf16[2,320,1024]{2,1,0:T(8,128)(2,1)S(1)} %get-tuple-element.115.refs_2_.refs_1_, bf16[2,768,4096]{2,1,0:T(8,128)(2,1)S(1)} %bitcast.14), custom_call_target="tpu_custom_call" | custom-call | flops 20000000000 | tf_op jit(solution)/shard_map/pallas_call | solution.py:79
  65.7 1.9 %copy-done.24 = f32[2,640,768]{2,1,0:T(8,128)} copy-done((f32[2,640,768]{2,1,0:T(8,128)}, f32[2,640,768]{2,1,0:T(8,128)S(1)}, u32[]{:S(2)}) %copy-start.24) | copy-done | bytes 3932184
  67.6 1.5 %shard_map.92 = (bf16[2,320,1024]{2,1,0:T(8,128)(2,1)S(1)}, bf16[2,320,1024]{2,1,0:T(8,128)(2,1)S(1)}, f32[8,128]{1,0:T(8,128)S(1)}) custom-call(f32[8,128]{1,0:T(8,128)S(1)} %get-tuple-element.116.refs_0_, bf16[512,1024]{1,0:T(8,128)(2,1)S(1)} %get-tuple-element.117.refs_1_, bf16[512,1024]{1,0:T(8,128)(2,1)S(1)} %collective-permute-done.10.refs_2_, ...), custom_call_target="tpu_custom_call" | custom-call | flops 20000000000 | tf_op jit(solution)/shard_map/pallas_call | solution.py:79
  69.2 2.1 %shard_map.93 = (bf16[2,320,1024]{2,1,0:T(8,128)(2,1)S(1)}, bf16[2,320,1024]{2,1,0:T(8,128)(2,1)}, f32[8,128]{1,0:T(8,128)S(1)}) custom-call(f32[8,128]{1,0:T(8,128)S(1)} %get-tuple-element.118.refs_0_, bf16[512,1024]{1,0:T(8,128)(2,1)S(1)} %get-tuple-element.119.refs_1_, bf16[512,1024]{1,0:T(8,128)(2,1)S(1)} %collective-permute-done.11.refs_2_, ...), custom_call_target="tpu_custom_call" | custom-call | flops 20000000000 | tf_op jit(solution)/shard_map/pallas_call | solution.py:79
  71.8 2.4 %collective-permute-start.16 = (bf16[2,320,1024]{2,1,0:T(8,128)(2,1)S(1)}, bf16[2,320,1024]{2,1,0:T(8,128)(2,1)S(1)}, u32[]{:S(2)}, u32[]{:S(2)}) collective-permute-start(bf16[2,320,1024]{2,1,0:T(8,128)(2,1)S(1)} %get-tuple-element.139), channel_id=1, source_target_pairs={{0,12},{1,13},{2,14},{3,15},{4,8},{5,9},{6,10},{7,11},{8,4},{9,5},... | collective-permute-start | bytes 3932168 | tf_op jit(solution)/shard_map/ppermute | solution.py:57
  74.2 3.9 %shard_map.94 = (f32[2,640,768]{2,1,0:T(8,128)S(1)}, f32[8,128]{1,0:T(8,128)S(1)}) custom-call(f32[8,128]{1,0:T(8,128)S(1)} %get-tuple-element.120.refs_0_, bf16[2,320,1024]{2,1,0:T(8,128)(2,1)S(1)} %get-tuple-element.121.refs_1_, bf16[2,320,1024]{2,1,0:T(8,128)(2,1)S(1)} %get-tuple-element.122.refs_2_.refs_1_, bf16[2,768,4096]{2,1,0:T(8,128)(2,1)S(1)} %bitcast.14), custom_call_target="tpu_custom_call" | custom-call | flops 20000000000 | tf_op jit(solution)/shard_map/pallas_call | solution.py:79
  78.1 2.1 %collective-permute-done.12.refs_2_.refs_7_ = bf16[2,320,1024]{2,1,0:T(8,128)(2,1)S(1)} collective-permute-done((bf16[2,320,1024]{2,1,0:T(8,128)(2,1)S(1)}, bf16[2,320,1024]{2,1,0:T(8,128)(2,1)S(1)}, u32[]{:S(2)}, u32[]{:S(2)}) %collective-permute-start.12) | collective-permute-done | bytes 1310752 | tf_op jit(solution)/shard_map/ppermute | solution.py:57
  80.2 1.4 shard_map.95
  81.8 1.4 shard_map.96
  83.2 1.4 shard_map.97
  85.2 1.4 shard_map.98
  86.6 1.2 shard_map.99
  88.0 1.9 %collective-permute-start.20 = (bf16[2,2,96,1024]{3,2,1,0:T(8,128)(2,1)}, bf16[2,2,96,1024]{3,2,1,0:T(8,128)(2,1)}, u32[]{:S(2)}, u32[]{:S(2)}) collective-permute-start(bf16[2,2,96,1024]{3,2,1,0:T(8,128)(2,1)} %get-tuple-element.157), channel_id=1, source_target_pairs={{0,32},{1,33},{2,34},{3,35},{4,36},{5,37},{6,38},{7,39},{8,40},{9,... | collective-permute-start | bytes 2359304 | tf_op jit(solution)/shard_map/ppermute | solution.py:57
  89.9 1.1 shard_map.100
  91.0 2.5 %collective-permute-start.21 = (bf16[2,2,96,1024]{3,2,1,0:T(8,128)(2,1)}, bf16[2,2,96,1024]{3,2,1,0:T(8,128)(2,1)S(1)}, u32[]{:S(2)}, u32[]{:S(2)}) collective-permute-start(bf16[2,2,96,1024]{3,2,1,0:T(8,128)(2,1)} %get-tuple-element.159), channel_id=1, source_target_pairs={{0,96},{1,97},{2,98},{3,99},{4,100},{5,101},{6,102},{7,103},{8,104... | collective-permute-start | bytes 2359304 | tf_op jit(solution)/shard_map/ppermute | solution.py:57
  94.3 1.4 shard_map.101
  96.0 2.7 %shard_map.102 = (bf16[2,640,1024]{2,1,0:T(8,128)(2,1)S(1)}, bf16[4,2,96,1024]{3,2,1,0:T(8,128)(2,1)S(1)}, f32[8,128]{1,0:T(8,128)S(1)}) custom-call(f32[8,128]{1,0:T(8,128)S(1)} %get-tuple-element.140.refs_0_, bf16[2,320,1024]{2,1,0:T(8,128)(2,1)S(1)} %get-tuple-element.122.refs_2_.refs_1_, bf16[2,320,1024]{2,1,0:T(8,128)(2,1)} %collective-permute-done.17.refs_2_.refs_10_, ...), custom_call_target="tpu_custom_call" | custom-call | flops 20000000000 | tf_op jit(solution)/shard_map/pallas_call | solution.py:79
  99.3 1.4 shard_map.103
  100.7 1.3 shard_map.104
  102.1 1.9 %collective-permute-start.22 = (bf16[2,2,96,1024]{3,2,1,0:T(8,128)(2,1)}, bf16[2,2,96,1024]{3,2,1,0:T(8,128)(2,1)}, u32[]{:S(2)}, u32[]{:S(2)}) collective-permute-start(bf16[2,2,96,1024]{3,2,1,0:T(8,128)(2,1)} %get-tuple-element.161), channel_id=1, source_target_pairs={{0,32},{1,33},{2,34},{3,35},{4,36},{5,37},{6,38},{7,39},{8,40},{9,... | collective-permute-start | bytes 2359304 | tf_op jit(solution)/shard_map/ppermute | solution.py:57
  104.0 1.4 shard_map.105
  106.9 2.5 %collective-permute-start.23 = (bf16[2,2,96,1024]{3,2,1,0:T(8,128)(2,1)}, bf16[2,2,96,1024]{3,2,1,0:T(8,128)(2,1)}, u32[]{:S(2)}, u32[]{:S(2)}) collective-permute-start(bf16[2,2,96,1024]{3,2,1,0:T(8,128)(2,1)} %get-tuple-element.163), channel_id=1, source_target_pairs={{0,96},{1,97},{2,98},{3,99},{4,100},{5,101},{6,102},{7,103},{8,104... | collective-permute-start | bytes 2359304 | tf_op jit(solution)/shard_map/ppermute | solution.py:57
  109.4 14.8 %shard_map.107 = (bf16[2,16,40,768]{3,2,1,0:T(8,128)(2,1)}, f32[16,2,128]{2,1,0:T(2,128)S(1)}, f32[8,128]{1,0:T(8,128)S(1)}) custom-call(f32[8,128]{1,0:T(8,128)S(1)} %get-tuple-element.152.refs_0_, s32[32]{0:T(128)S(1)} %pad_add_fusion.1.refs_1_, f32[32,128]{1,0:T(8,128)S(1)} %copy-done.12, f32[32,128]{1,0:T(8,128)S(1)} %copy-done.14, ...), custom_call_target="tpu_custom_call" | custom-call | flops 20000000000 | tf_op jit(solution)/shard_map/pallas_call | solution.py:79
  124.3 1.1 shard_map.108
  125.6 1.1 collective-permute-start.25
  126.7 2.1 %collective-permute-start.24 = (bf16[1,2,96,1024]{3,2,1,0:T(8,128)(2,1)S(1)}, bf16[1,2,96,1024]{3,2,1,0:T(8,128)(2,1)S(1)}, u32[]{:S(2)}, u32[]{:S(2)}) collective-permute-start(bf16[1,2,96,1024]{3,2,1,0:T(8,128)(2,1)S(1)} %get-tuple-element.165), channel_id=1, source_target_pairs={{0,96},{1,97},{2,98},{3,99},{4,100},{5,101},{6,102},{7,103},{8,104... | collective-permute-start | bytes 1179656 | tf_op jit(solution)/shard_map/ppermute | solution.py:57
  128.8 1.3 shard_map.110
  130.1 1.2 collective-permute-start.26
  131.3 1.2 shard_map.111
  132.5 13.5 %all_to_all.10 = f32[16,2,128]{2,1,0:T(2,128)S(1)} all-to-all(f32[16,2,128]{2,1,0:T(2,128)S(1)} %get-tuple-element.170), channel_id=1, replica_groups=mesh['section'=8,'expert'=16] {'expert'}, dimensions={0} | all-to-all | bytes 32768 | tf_op jit(solution)/shard_map/all_to_all | solution.py:574
  147.2 3.4 %shard_map.112 = (bf16[2,96,4096]{2,1,0:T(8,128)(2,1)}, f32[8,128]{1,0:T(8,128)}) custom-call(f32[8,128]{1,0:T(8,128)S(1)} %get-tuple-element.164.refs_0_, bf16[4,2,96,1024]{3,2,1,0:T(8,128)(2,1)S(1)} %copy-done.6, bf16[4,2,96,1024]{3,2,1,0:T(8,128)(2,1)S(1)} %copy-done.4, bf16[2,2,96,1024]{3,2,1,0:T(8,128)(2,1)} %collective-permute-done.20.refs_3_, ...), custom_call_target="tpu_custom_call" | custom-call | flops 20000000000 | tf_op jit(solution)/shard_map/pallas_call | solution.py:79
  (126 shorter events, 18.2 us)
Async XLA Ops:
  1.7 11.4 %collective-permute-start.1 = (bf16[128,1024]{1,0:T(8,128)(2,1)S(1)}, bf16[128,1024]{1,0:T(8,128)(2,1)S(1)}, u32[]{:S(2)}, u32[]{:S(2)}) collective-permute-start(bf16[128,1024]{1,0:T(8,128)(2,1)S(1)} %get-tuple-element.176), channel_id=1, source_target_pairs={{0,3},{1,2},{2,1},{3,0},{4,7},{5,6},{6,5},{7,4},{8,11},{9,10},{10,... | collective-permute-start | bytes 786440 | tf_op jit(solution)/shard_map/ppermute | solution.py:57
  4.6 6.4 %collective-permute-start = (bf16[128,1024]{1,0:T(8,128)(2,1)S(1)}, bf16[128,1024]{1,0:T(8,128)(2,1)S(1)}, u32[]{:S(2)}, u32[]{:S(2)}) collective-permute-start(bf16[128,1024]{1,0:T(8,128)(2,1)S(1)} %get-tuple-element.177), channel_id=1, source_target_pairs={{0,1},{1,0},{2,3},{3,2},{4,5},{5,4},{6,7},{7,6},{8,9},{9,8},{10,11... | collective-permute-start | bytes 786440 | tf_op jit(solution)/shard_map/ppermute | solution.py:57
  13.1 3.2 %copy-start.26 = (s32[128,8]{0,1:T(8,128)S(1)}, s32[128,8]{0,1:T(8,128)}, u32[]{:S(2)}) copy-start(s32[128,8]{0,1:T(8,128)} %param.7) | copy-start | bytes 12292
  13.9 14.9 %collective-permute-start.3 = (bf16[256,1024]{1,0:T(8,128)(2,1)}, bf16[256,1024]{1,0:T(8,128)(2,1)S(1)}, u32[]{:S(2)}, u32[]{:S(2)}) collective-permute-start(bf16[256,1024]{1,0:T(8,128)(2,1)} %get-tuple-element.94), channel_id=1, source_target_pairs={{0,1},{1,0},{2,3},{3,2},{4,5},{5,4},{6,7},{7,6},{8,9},{9,8},{10,11... | collective-permute-start | bytes 1572872 | tf_op jit(solution)/shard_map/ppermute | solution.py:57
  14.1 13.7 %collective-permute-start.2 = (bf16[256,1024]{1,0:T(8,128)(2,1)}, bf16[256,1024]{1,0:T(8,128)(2,1)S(1)}, u32[]{:S(2)}, u32[]{:S(2)}) collective-permute-start(bf16[256,1024]{1,0:T(8,128)(2,1)} %get-tuple-element.92), channel_id=1, source_target_pairs={{0,3},{1,2},{2,1},{3,0},{4,7},{5,6},{6,5},{7,4},{8,11},{9,10},{10,... | collective-permute-start | bytes 1572872 | tf_op jit(solution)/shard_map/ppermute | solution.py:57
  15.3 14.5 %collective-permute-start.4 = (bf16[128,1024]{1,0:T(8,128)(2,1)S(1)}, bf16[128,1024]{1,0:T(8,128)(2,1)S(1)}, u32[]{:S(2)}, u32[]{:S(2)}) collective-permute-start(bf16[128,1024]{1,0:T(8,128)(2,1)S(1)} %get-tuple-element.96), channel_id=1, source_target_pairs={{0,1},{1,0},{2,3},{3,2},{4,5},{5,4},{6,7},{7,6},{8,9},{9,8},{10,11... | collective-permute-start | bytes 786440 | tf_op jit(solution)/shard_map/ppermute | solution.py:57
  17.7 19.4 %all-to-all-start = ((bf16[16,16,128]{2,1,0:T(8,128)(2,1)}), bf16[16,16,128]{2,1,0:T(8,128)(2,1)S(1)}, u32[]{:S(2)}, u32[]{:S(2)}) async-start(bf16[16,16,128]{2,1,0:T(8,128)(2,1)} %get-tuple-element.100), calls=%async_computation | async-start | bytes 131072 | tf_op jit(solution)/shard_map/all_to_all | solution.py:540
  24.6 8.0 %collective-permute-start.5 = (bf16[128,1024]{1,0:T(8,128)(2,1)}, bf16[128,1024]{1,0:T(8,128)(2,1)S(1)}, u32[]{:S(2)}, u32[]{:S(2)}) collective-permute-start(bf16[128,1024]{1,0:T(8,128)(2,1)} %copy-done.23), channel_id=1, source_target_pairs={{0,3},{1,2},{2,1},{3,0},{4,7},{5,6},{6,5},{7,4},{8,11},{9,10},{10,... | collective-permute-start | bytes 786440 | tf_op jit(solution)/shard_map/ppermute | solution.py:57
  30.7 13.9 %collective-permute-start.6 = (bf16[256,1024]{1,0:T(8,128)(2,1)}, bf16[256,1024]{1,0:T(8,128)(2,1)}, u32[]{:S(2)}, u32[]{:S(2)}) collective-permute-start(bf16[256,1024]{1,0:T(8,128)(2,1)} %get-tuple-element.105), channel_id=1, source_target_pairs={{0,3},{1,2},{2,1},{3,0},{4,7},{5,6},{6,5},{7,4},{8,11},{9,10},{10,... | collective-permute-start | bytes 1572872 | tf_op jit(solution)/shard_map/ppermute | solution.py:57
  32.7 5.5 %copy-start.2 = (bf16[1,2,16,40,768]{4,3,2,1,0:T(8,128)(2,1)S(1)}, bf16[1,2,16,40,768]{4,3,2,1,0:T(8,128)(2,1)}, u32[]{:S(2)}) copy-start(bf16[1,2,16,40,768]{4,3,2,1,0:T(8,128)(2,1)} %param.8) | copy-start | bytes 5898244
  33.5 15.2 %collective-permute-start.7 = (bf16[256,1024]{1,0:T(8,128)(2,1)}, bf16[256,1024]{1,0:T(8,128)(2,1)}, u32[]{:S(2)}, u32[]{:S(2)}) collective-permute-start(bf16[256,1024]{1,0:T(8,128)(2,1)} %get-tuple-element.107), channel_id=1, source_target_pairs={{0,1},{1,0},{2,3},{3,2},{4,5},{5,4},{6,7},{7,6},{8,9},{9,8},{10,11... | collective-permute-start | bytes 1572872 | tf_op jit(solution)/shard_map/ppermute | solution.py:57
  34.2 22.2 %collective-permute-start.9 = (bf16[512,1024]{1,0:T(8,128)(2,1)}, bf16[512,1024]{1,0:T(8,128)(2,1)}, u32[]{:S(2)}, u32[]{:S(2)}) collective-permute-start(bf16[512,1024]{1,0:T(8,128)(2,1)} %get-tuple-element.112.refs_1_), channel_id=1, source_target_pairs={{0,12},{1,13},{2,14},{3,15},{4,8},{5,9},{6,10},{7,11},{8,4},{9,5},... | collective-permute-start | bytes 3145736 | tf_op jit(solution)/shard_map/ppermute | solution.py:57
  36.9 16.2 %collective-permute-start.8 = (bf16[512,1024]{1,0:T(8,128)(2,1)}, bf16[512,1024]{1,0:T(8,128)(2,1)}, u32[]{:S(2)}, u32[]{:S(2)}) collective-permute-start(bf16[512,1024]{1,0:T(8,128)(2,1)} %get-tuple-element.109.refs_1_), channel_id=1, source_target_pairs={{0,4},{1,5},{2,6},{3,7},{4,0},{5,1},{6,2},{7,3},{8,12},{9,13},{10,... | collective-permute-start | bytes 3145736 | tf_op jit(solution)/shard_map/ppermute | solution.py:57
  38.1 7.6 %copy-start.11 = (f32[32,128]{1,0:T(8,128)}, f32[32,128]{1,0:T(8,128)S(1)}, u32[]{:S(2)}) copy-start(f32[32,128]{1,0:T(8,128)S(1)} %get-tuple-element.102.refs_2_) | copy-start | bytes 49156
  38.1 7.6 %copy-start.13 = (f32[32,128]{1,0:T(8,128)}, f32[32,128]{1,0:T(8,128)S(1)}, u32[]{:S(2)}) copy-start(f32[32,128]{1,0:T(8,128)S(1)} %get-tuple-element.103.refs_3_) | copy-start | bytes 49156
  44.6 4.1 %copy-start.22 = (bf16[128,1024]{1,0:T(8,128)(2,1)S(1)}, bf16[128,1024]{1,0:T(8,128)(2,1)}, u32[]{:S(2)}) copy-start(bf16[128,1024]{1,0:T(8,128)(2,1)} %copy-done.21) | copy-start | bytes 786436
  49.8 19.3 %collective-permute-start.11 = (bf16[512,1024]{1,0:T(8,128)(2,1)S(1)}, bf16[512,1024]{1,0:T(8,128)(2,1)S(1)}, u32[]{:S(2)}, u32[]{:S(2)}) collective-permute-start(bf16[512,1024]{1,0:T(8,128)(2,1)S(1)} %get-tuple-element.119.refs_1_), channel_id=1, source_target_pairs={{0,12},{1,13},{2,14},{3,15},{4,8},{5,9},{6,10},{7,11},{8,4},{9,5},... | collective-permute-start | bytes 3145736 | tf_op jit(solution)/shard_map/ppermute | solution.py:57
  52.8 14.8 %collective-permute-start.10 = (bf16[512,1024]{1,0:T(8,128)(2,1)S(1)}, bf16[512,1024]{1,0:T(8,128)(2,1)S(1)}, u32[]{:S(2)}, u32[]{:S(2)}) collective-permute-start(bf16[512,1024]{1,0:T(8,128)(2,1)S(1)} %get-tuple-element.117.refs_1_), channel_id=1, source_target_pairs={{0,4},{1,5},{2,6},{3,7},{4,0},{5,1},{6,2},{7,3},{8,12},{9,13},{10,... | collective-permute-start | bytes 3145736 | tf_op jit(solution)/shard_map/ppermute | solution.py:57
  53.1 8.6 %slice-start = ((s8[12582912]{0:T(1024)(128)(4,1)}), s8[4194304]{0:T(1024)(128)(4,1)S(1)}, s32[]{:S(2)}) async-start(s8[12582912]{0:T(1024)(128)(4,1)} %bitcast.13), calls=%async_computation.2 | async-start | bytes 8388608
  53.1 8.6 %slice-start.1 = ((s8[12582912]{0:T(1024)(128)(4,1)}), s8[4194304]{0:T(1024)(128)(4,1)S(1)}, s32[]{:S(2)}) async-start(s8[12582912]{0:T(1024)(128)(4,1)} %bitcast.13), calls=%async_computation.3 | async-start | bytes 8388608
  56.3 5.4 %slice-start.2 = ((s8[12582912]{0:T(1024)(128)(4,1)}), s8[4194304]{0:T(1024)(128)(4,1)S(1)}, s32[]{:S(2)}) async-start(s8[12582912]{0:T(1024)(128)(4,1)} %bitcast.13), calls=%async_computation.4 | async-start | bytes 8388608
  59.6 23.6 %collective-permute-start.13 = (bf16[2,320,1024]{2,1,0:T(8,128)(2,1)S(1)}, bf16[2,320,1024]{2,1,0:T(8,128)(2,1)S(1)}, u32[]{:S(2)}, u32[]{:S(2)}) collective-permute-start(bf16[2,320,1024]{2,1,0:T(8,128)(2,1)S(1)} %get-tuple-element.129), channel_id=1, source_target_pairs={{0,4},{1,5},{2,6},{3,7},{4,0},{5,1},{6,2},{7,3},{8,12},{9,13},{10,... | collective-permute-start | bytes 3932168 | tf_op jit(solution)/shard_map/ppermute | solution.py:57
  61.4 18.8 %collective-permute-start.12 = (bf16[2,320,1024]{2,1,0:T(8,128)(2,1)S(1)}, bf16[2,320,1024]{2,1,0:T(8,128)(2,1)S(1)}, u32[]{:S(2)}, u32[]{:S(2)}) collective-permute-start(bf16[2,320,1024]{2,1,0:T(8,128)(2,1)S(1)} %get-tuple-element.124), channel_id=1, source_target_pairs={{0,12},{1,13},{2,14},{3,15},{4,8},{5,9},{6,10},{7,11},{8,4},{9,5},... | collective-permute-start | bytes 3932168 | tf_op jit(solution)/shard_map/ppermute | solution.py:57
  71.3 24.7 %collective-permute-start.17 = (bf16[2,320,1024]{2,1,0:T(8,128)(2,1)}, bf16[2,320,1024]{2,1,0:T(8,128)(2,1)}, u32[]{:S(2)}, u32[]{:S(2)}) collective-permute-start(bf16[2,320,1024]{2,1,0:T(8,128)(2,1)} %get-tuple-element.141), channel_id=1, source_target_pairs={{0,4},{1,5},{2,6},{3,7},{4,0},{5,1},{6,2},{7,3},{8,12},{9,13},{10,... | collective-permute-start | bytes 3932168 | tf_op jit(solution)/shard_map/ppermute | solution.py:57
  71.8 22.5 %collective-permute-start.16 = (bf16[2,320,1024]{2,1,0:T(8,128)(2,1)S(1)}, bf16[2,320,1024]{2,1,0:T(8,128)(2,1)S(1)}, u32[]{:S(2)}, u32[]{:S(2)}) collective-permute-start(bf16[2,320,1024]{2,1,0:T(8,128)(2,1)S(1)} %get-tuple-element.139), channel_id=1, source_target_pairs={{0,12},{1,13},{2,14},{3,15},{4,8},{5,9},{6,10},{7,11},{8,4},{9,5},... | collective-permute-start | bytes 3932168 | tf_op jit(solution)/shard_map/ppermute | solution.py:57
  78.1 3.5 %copy-start.25 = (f32[2,640,768]{2,1,0:T(8,128)}, f32[2,640,768]{2,1,0:T(8,128)S(1)}, u32[]{:S(2)}) copy-start(f32[2,640,768]{2,1,0:T(8,128)S(1)} %get-tuple-element.154.refs_6_) | copy-start | bytes 11796484
  81.7 4.9 %collective-permute-start.14 = (bf16[4,2,96,1024]{3,2,1,0:T(8,128)(2,1)S(1)}, bf16[4,2,96,1024]{3,2,1,0:T(8,128)(2,1)S(1)}, u32[]{:S(2)}, u32[]{:S(2)}) collective-permute-start(bf16[4,2,96,1024]{3,2,1,0:T(8,128)(2,1)S(1)} %get-tuple-element.134), channel_id=1, source_target_pairs={{0,16},{1,17},{2,18},{3,19},{4,20},{5,21},{6,22},{7,23},{8,24},{9,... | collective-permute-start | bytes 4718600 | tf_op jit(solution)/shard_map/ppermute | solution.py:57
  83.1 3.4 %copy-start.5 = (bf16[4,2,96,1024]{3,2,1,0:T(8,128)(2,1)}, bf16[4,2,96,1024]{3,2,1,0:T(8,128)(2,1)S(1)}, u32[]{:S(2)}) copy-start(bf16[4,2,96,1024]{3,2,1,0:T(8,128)(2,1)S(1)} %get-tuple-element.133.refs_1_.refs_3_) | copy-start | bytes 4718596
  84.6 5.4 %collective-permute-start.15 = (bf16[4,2,96,1024]{3,2,1,0:T(8,128)(2,1)S(1)}, bf16[4,2,96,1024]{3,2,1,0:T(8,128)(2,1)S(1)}, u32[]{:S(2)}, u32[]{:S(2)}) collective-permute-start(bf16[4,2,96,1024]{3,2,1,0:T(8,128)(2,1)S(1)} %get-tuple-element.137), channel_id=1, source_target_pairs={{0,16},{1,17},{2,18},{3,19},{4,20},{5,21},{6,22},{7,23},{8,24},{9,... | collective-permute-start | bytes 4718600 | tf_op jit(solution)/shard_map/ppermute | solution.py:57
  88.0 36.2 %collective-permute-start.20 = (bf16[2,2,96,1024]{3,2,1,0:T(8,128)(2,1)}, bf16[2,2,96,1024]{3,2,1,0:T(8,128)(2,1)}, u32[]{:S(2)}, u32[]{:S(2)}) collective-permute-start(bf16[2,2,96,1024]{3,2,1,0:T(8,128)(2,1)} %get-tuple-element.157), channel_id=1, source_target_pairs={{0,32},{1,33},{2,34},{3,35},{4,36},{5,37},{6,38},{7,39},{8,40},{9,... | collective-permute-start | bytes 2359304 | tf_op jit(solution)/shard_map/ppermute | solution.py:57
  91.0 34.4 %collective-permute-start.21 = (bf16[2,2,96,1024]{3,2,1,0:T(8,128)(2,1)}, bf16[2,2,96,1024]{3,2,1,0:T(8,128)(2,1)S(1)}, u32[]{:S(2)}, u32[]{:S(2)}) collective-permute-start(bf16[2,2,96,1024]{3,2,1,0:T(8,128)(2,1)} %get-tuple-element.159), channel_id=1, source_target_pairs={{0,96},{1,97},{2,98},{3,99},{4,100},{5,101},{6,102},{7,103},{8,104... | collective-permute-start | bytes 2359304 | tf_op jit(solution)/shard_map/ppermute | solution.py:57
  95.7 5.0 %collective-permute-start.18 = (bf16[4,2,96,1024]{3,2,1,0:T(8,128)(2,1)S(1)}, bf16[4,2,96,1024]{3,2,1,0:T(8,128)(2,1)S(1)}, u32[]{:S(2)}, u32[]{:S(2)}) collective-permute-start(bf16[4,2,96,1024]{3,2,1,0:T(8,128)(2,1)S(1)} %get-tuple-element.146), channel_id=1, source_target_pairs={{0,16},{1,17},{2,18},{3,19},{4,20},{5,21},{6,22},{7,23},{8,24},{9,... | collective-permute-start | bytes 4718600 | tf_op jit(solution)/shard_map/ppermute | solution.py:57
  98.7 6.7 %collective-permute-start.19 = (bf16[4,2,96,1024]{3,2,1,0:T(8,128)(2,1)S(1)}, bf16[4,2,96,1024]{3,2,1,0:T(8,128)(2,1)S(1)}, u32[]{:S(2)}, u32[]{:S(2)}) collective-permute-start(bf16[4,2,96,1024]{3,2,1,0:T(8,128)(2,1)S(1)} %get-tuple-element.151), channel_id=1, source_target_pairs={{0,16},{1,17},{2,18},{3,19},{4,20},{5,21},{6,22},{7,23},{8,24},{9,... | collective-permute-start | bytes 4718600 | tf_op jit(solution)/shard_map/ppermute | solution.py:57
  102.1 26.7 %collective-permute-start.22 = (bf16[2,2,96,1024]{3,2,1,0:T(8,128)(2,1)}, bf16[2,2,96,1024]{3,2,1,0:T(8,128)(2,1)}, u32[]{:S(2)}, u32[]{:S(2)}) collective-permute-start(bf16[2,2,96,1024]{3,2,1,0:T(8,128)(2,1)} %get-tuple-element.161), channel_id=1, source_target_pairs={{0,32},{1,33},{2,34},{3,35},{4,36},{5,37},{6,38},{7,39},{8,40},{9,... | collective-permute-start | bytes 2359304 | tf_op jit(solution)/shard_map/ppermute | solution.py:57
  105.4 4.0 %copy-start.12 = (f32[32,128]{1,0:T(8,128)S(1)}, f32[32,128]{1,0:T(8,128)}, u32[]{:S(2)}) copy-start(f32[32,128]{1,0:T(8,128)} %copy-done.11) | copy-start | bytes 49156
  105.4 3.9 %copy-start.14 = (f32[32,128]{1,0:T(8,128)S(1)}, f32[32,128]{1,0:T(8,128)}, u32[]{:S(2)}) copy-start(f32[32,128]{1,0:T(8,128)} %copy-done.13) | copy-start | bytes 49156
  105.5 3.9 %copy-start.16 = (bf16[2,320,1024]{2,1,0:T(8,128)(2,1)S(1)}, bf16[2,320,1024]{2,1,0:T(8,128)(2,1)}, u32[]{:S(2)}) copy-start(bf16[2,320,1024]{2,1,0:T(8,128)(2,1)} %copy-done.15) | copy-start | bytes 3932164
  105.5 3.9 %copy-start.18 = (bf16[2,320,1024]{2,1,0:T(8,128)(2,1)S(1)}, bf16[2,320,1024]{2,1,0:T(8,128)(2,1)}, u32[]{:S(2)}) copy-start(bf16[2,320,1024]{2,1,0:T(8,128)(2,1)} %copy-done.17) | copy-start | bytes 3932164
  105.5 3.9 %copy-start.20 = (bf16[2,320,1024]{2,1,0:T(8,128)(2,1)S(1)}, bf16[2,320,1024]{2,1,0:T(8,128)(2,1)}, u32[]{:S(2)}) copy-start(bf16[2,320,1024]{2,1,0:T(8,128)(2,1)} %copy-done.19) | copy-start | bytes 3932164
  106.9 24.4 %collective-permute-start.23 = (bf16[2,2,96,1024]{3,2,1,0:T(8,128)(2,1)}, bf16[2,2,96,1024]{3,2,1,0:T(8,128)(2,1)}, u32[]{:S(2)}, u32[]{:S(2)}) collective-permute-start(bf16[2,2,96,1024]{3,2,1,0:T(8,128)(2,1)} %get-tuple-element.163), channel_id=1, source_target_pairs={{0,96},{1,97},{2,98},{3,99},{4,100},{5,101},{6,102},{7,103},{8,104... | collective-permute-start | bytes 2359304 | tf_op jit(solution)/shard_map/ppermute | solution.py:57
  109.4 14.8 %copy-start.4 = (bf16[4,2,96,1024]{3,2,1,0:T(8,128)(2,1)S(1)}, bf16[4,2,96,1024]{3,2,1,0:T(8,128)(2,1)}, u32[]{:S(2)}) copy-start(bf16[4,2,96,1024]{3,2,1,0:T(8,128)(2,1)} %copy-done.3) | copy-start | bytes 4718596
  109.4 14.8 %copy-start.6 = (bf16[4,2,96,1024]{3,2,1,0:T(8,128)(2,1)S(1)}, bf16[4,2,96,1024]{3,2,1,0:T(8,128)(2,1)}, u32[]{:S(2)}) copy-start(bf16[4,2,96,1024]{3,2,1,0:T(8,128)(2,1)} %copy-done.5) | copy-start | bytes 4718596
  125.4 3.4 %copy-start.8 = (bf16[4,2,96,1024]{3,2,1,0:T(8,128)(2,1)S(1)}, bf16[4,2,96,1024]{3,2,1,0:T(8,128)(2,1)}, u32[]{:S(2)}) copy-start(bf16[4,2,96,1024]{3,2,1,0:T(8,128)(2,1)} %copy-done.7) | copy-start | bytes 4718596
  125.6 21.1 %collective-permute-start.25 = (bf16[1,2,96,1024]{3,2,1,0:T(8,128)(2,1)S(1)}, bf16[1,2,96,1024]{3,2,1,0:T(8,128)(2,1)S(1)}, u32[]{:S(2)}, u32[]{:S(2)}) collective-permute-start(bf16[1,2,96,1024]{3,2,1,0:T(8,128)(2,1)S(1)} %get-tuple-element.166), channel_id=1, source_target_pairs={{0,32},{1,33},{2,34},{3,35},{4,36},{5,37},{6,38},{7,39},{8,40},{9,... | collective-permute-start | bytes 1179656 | tf_op jit(solution)/shard_map/ppermute | solution.py:57
  126.7 20.0 %collective-permute-start.24 = (bf16[1,2,96,1024]{3,2,1,0:T(8,128)(2,1)S(1)}, bf16[1,2,96,1024]{3,2,1,0:T(8,128)(2,1)S(1)}, u32[]{:S(2)}, u32[]{:S(2)}) collective-permute-start(bf16[1,2,96,1024]{3,2,1,0:T(8,128)(2,1)S(1)} %get-tuple-element.165), channel_id=1, source_target_pairs={{0,96},{1,97},{2,98},{3,99},{4,100},{5,101},{6,102},{7,103},{8,104... | collective-permute-start | bytes 1179656 | tf_op jit(solution)/shard_map/ppermute | solution.py:57
  130.1 17.1 %collective-permute-start.26 = (bf16[1,2,96,1024]{3,2,1,0:T(8,128)(2,1)S(1)}, bf16[1,2,96,1024]{3,2,1,0:T(8,128)(2,1)S(1)}, u32[]{:S(2)}, u32[]{:S(2)}) collective-permute-start(bf16[1,2,96,1024]{3,2,1,0:T(8,128)(2,1)S(1)} %get-tuple-element.167), channel_id=1, source_target_pairs={{0,96},{1,97},{2,98},{3,99},{4,100},{5,101},{6,102},{7,103},{8,104... | collective-permute-start | bytes 1179656 | tf_op jit(solution)/shard_map/ppermute | solution.py:57
  131.3 14.7 %copy-start.27 = (s32[128,8]{0,1:T(8,128)S(1)}, s32[128,8]{0,1:T(8,128)}, u32[]{:S(2)}) copy-start(s32[128,8]{0,1:T(8,128)} %param.7) | copy-start | bytes 12292
  132.4 14.7 %collective-permute-start.27 = (bf16[1,2,96,1024]{3,2,1,0:T(8,128)(2,1)S(1)}, bf16[1,2,96,1024]{3,2,1,0:T(8,128)(2,1)S(1)}, u32[]{:S(2)}, u32[]{:S(2)}) collective-permute-start(bf16[1,2,96,1024]{3,2,1,0:T(8,128)(2,1)S(1)} %get-tuple-element.168), channel_id=1, source_target_pairs={{0,32},{1,33},{2,34},{3,35},{4,36},{5,37},{6,38},{7,39},{8,40},{9,... | collective-permute-start | bytes 1179656 | tf_op jit(solution)/shard_map/ppermute | solution.py:57
  (13 other events, 21.4 us)
